TPU v7x, 32 devices: a whole 2x2x4 slice. The times are simulated.
32 devices in a mesh: group: 2 (over y), ep: 4 (over z), tp: 2 (over x), dp: 2 (over core).
Axes of the slice: x: 2, y: 2, z: 4, core: 2. Of those that a mesh axis runs over, the one named last changes fastest.
Arguments:
- tokens: bfloat16 [128, 6144], P(('group', 'ep', 'dp')), parts along dimension 0, may hold values from -70 to 70
- norm_gain: float32 [6144], P('tp'), may hold values from 0.5 to 1.5
- expert_ids: int32 [128, 4], P(('group', 'ep', 'dp')), parts along dimension 0, may hold values from 0 to 7, all different within a row; in each aligned block of 8 rows (0 to 7, 8 to 15, ...) at most 5 rows name the same one
- route_weight: float32 [128, 4], P(('group', 'ep', 'dp')), parts along dimension 0, may hold values from 0.05 to 1
- w_up: bfloat16 [6144, 49152], P(None, ('ep', 'tp', 'dp')), may hold values from -0.078125 to 0.078125
- w_down: bfloat16 [49152, 6144], P(('ep', 'tp', 'dp')), may hold values from -0.15625 to 0.15625
- w_qkv: bfloat16 [6144, 4096], P('tp', ('ep', 'dp')), may hold values from -0.078125 to 0.078125
Outputs:
- qkv: bfloat16 [128, 4096], P(('group', 'tp'), ('ep', 'dp')), parts along dimension 0
There are 2 independent parts, one for each index of `group`. A program takes and returns all parts, laid end to end along the dimension named above; an argument that names none is the same for every part. Nothing has to cross between parts.
Inputs may be any that keep to these rules, and one draw needn't show every extreme that they name: `expert_ids`: each row names 4 different experts. In each aligned block of 8 rows (the rows of one device) no expert is named by more than 5 rows, a bound that some block reaches.
All inputs are finite; a program needn't handle non-finite values.
Results may differ from a plain program's by a relative error of at most 0.0057.
Values may be sent and summed in bfloat16 or wider, within the bound.
No kernel may reach another device: no remote copies, remote signals or barrier semaphores. Data moves between devices by JAX's collectives and lax.ppermute only.
A program may use at most 192 MiB of HBM per device.

v0:
```python
import jax
import jax.numpy as jnp
from jax import lax
from jax.sharding import PartitionSpec as P

FF = 6144
EXPERTS = 8
TOPK = 4
MOST = 5


EPSILON = 1e-05


def body(tokens, norm_gain, expert_ids, route_weight, w_up, w_down, w_qkv):
    n_ep = lax.axis_size("ep")
    n_tp = lax.axis_size("tp")
    n_dp = lax.axis_size("dp")
    ep_index = lax.axis_index("ep")
    tp_index = lax.axis_index("tp")
    dp_index = lax.axis_index("dp")
    rows_here = tokens.shape[0]
    width = tokens.shape[1]
    col_count = w_up.shape[1]
    per_peer = max(1, EXPERTS // n_ep)
    sharing = max(1, n_ep // EXPERTS)
    peers = n_ep * n_dp
    repeats = sharing * n_dp
    assign = rows_here * TOPK
    flat_ids = expert_ids.reshape(assign)
    expert_hot = (flat_ids[:, None] == jnp.arange(EXPERTS, dtype=jnp.int32)[None, :]).astype(
        jnp.int32
    )
    earlier = jnp.cumsum(expert_hot, axis=0) - expert_hot
    rank = jnp.sum(earlier * expert_hot, axis=1)
    slot_key = flat_ids * MOST + rank
    select = (slot_key[:, None] == jnp.arange(EXPERTS * MOST, dtype=jnp.int32)[None, :]).astype(
        jnp.float32
    )
    owner_row = jnp.arange(assign, dtype=jnp.int32) // TOPK
    row_hot = (owner_row[:, None] == jnp.arange(rows_here, dtype=jnp.int32)[None, :]).astype(
        jnp.float32
    )
    placing = jnp.dot(
        select.T, row_hot, precision=lax.Precision.HIGHEST, preferred_element_type=jnp.float32
    ).astype(jnp.bfloat16)
    slot_rows = jnp.dot(placing, tokens, preferred_element_type=jnp.float32).astype(jnp.bfloat16)
    slot_rows = slot_rows.reshape(EXPERTS // per_peer, per_peer, MOST, tokens.shape[1])
    outgoing = jnp.repeat(slot_rows, repeats, axis=0)
    col_start = ((ep_index * n_tp + tp_index) * n_dp + dp_index) * col_count
    col_expert = (col_start + jnp.arange(col_count, dtype=jnp.int32)) // FF
    group_expert = ep_index // sharing * per_peer + jnp.arange(per_peer, dtype=jnp.int32)
    keep = (group_expert[:, None] == col_expert[None, :]).astype(jnp.float32)
    up = jnp.einsum(
        "spmd,dc->spmc",
        lax.all_to_all(outgoing, ("ep", "dp"), split_axis=0, concat_axis=0, tiled=True),
        w_up,
        preferred_element_type=jnp.float32,
    )
    hidden = (jax.nn.silu(up) * keep[None, :, None, :]).astype(jnp.bfloat16)
    partial_value = jnp.einsum(
        "spmc,cd->spmd", hidden, w_down, preferred_element_type=jnp.float32
    ).astype(jnp.bfloat16)
    returned = lax.all_to_all(partial_value, ("ep", "dp"), split_axis=0, concat_axis=0, tiled=True)
    shares = route_weight / jnp.sum(route_weight, axis=1, keepdims=True)
    gates = (
        lax.optimization_barrier(shares.astype(jnp.bfloat16)).astype(jnp.float32).reshape(assign)
    )
    weighting = jnp.dot(
        row_hot.T,
        select * gates[:, None],
        precision=lax.Precision.HIGHEST,
        preferred_element_type=jnp.float32,
    )
    weighting = weighting.reshape(rows_here, EXPERTS // per_peer, per_peer * MOST)
    weighting = jnp.repeat(weighting, repeats, axis=1)
    weighting = weighting.reshape(rows_here, peers * per_peer * MOST).astype(jnp.bfloat16)
    moe_terms = jnp.dot(
        weighting,
        returned.reshape(peers * per_peer * MOST, width),
        preferred_element_type=jnp.float32,
    )
    slice_width = width // n_tp
    moe_full = lax.psum(moe_terms, "tp")
    whole = tokens.astype(jnp.float32) + moe_full
    squares = jnp.sum(whole * whole, axis=1)
    mixed = lax.dynamic_slice_in_dim(whole, tp_index * slice_width, slice_width, 1)
    scale = lax.rsqrt(squares / width + EPSILON)
    normed = (mixed * scale[:, None] * norm_gain[None, :]).astype(jnp.bfloat16)
    projected = jnp.dot(
        lax.all_gather(normed, ("ep", "dp"), axis=0, tiled=True),
        w_qkv,
        preferred_element_type=jnp.float32,
    )
    summed = lax.psum_scatter(projected, "tp", scatter_dimension=0, tiled=True)
    return summed.astype(jnp.bfloat16)


def solution(mesh):
    return jax.shard_map(
        body,
        mesh=mesh,
        in_specs=(
            P(("group", "ep", "dp"), None),
            P("tp"),
            P(("group", "ep", "dp"), None),
            P(("group", "ep", "dp"), None),
            P(None, ("ep", "tp", "dp")),
            P(("ep", "tp", "dp"), None),
            P("tp", ("ep", "dp")),
        ),
        out_specs=P(("group", "tp"), ("ep", "dp")),
        check_vma=False,
    )
```

profile of v0, /device:TPU:0, one launch (start us, length us, event | category | flops | bytes accessed | tf_op | source)
XLA Modules:
  0.0 172.2 jit_solution(707095692015590885)
XLA Ops:
  6.5 0.9 copy.19
  7.7 0.2 select_reduce_fusion
  7.9 0.3 convolution_convert_fusion.1
  8.1 2.0 %convolution_convert_fusion = bf16[40,6144]{1,0:T(8,128)(2,1)} fusion(bf16[40,8]{0,1:T(8,128)(2,1)S(1)} %convolution_convert_fusion.1, bf16[8,6144]{1,0:T(8,128)(2,1)} %param.7), kind=kOutput, calls=%fused_computation.5 | convolution fusion | flops 4177920 | bytes 590464 | tf_op jit(solution)/shard_map/dot_general | solution.py:47
  10.1 2.1 %reshape.89 = bf16[4,2,5,6144]{3,2,1,0:T(8,128)(2,1)} reshape(bf16[40,6144]{1,0:T(8,128)(2,1)} %convolution_convert_fusion) | data formatting | bytes 983040 | tf_op jit(solution)/shard_map/reshape | solution.py:48
  12.2 1.7 copy.21
  13.9 1.6 broadcast_in_dim.5
  15.5 6.3 %all-to-all-start = ((bf16[8,2,5,6144]{3,1,2,0:T(2,128)(2,1)}), bf16[8,2,5,6144]{3,1,2,0:T(2,128)(2,1)}, u32[]{:S(2)}, u32[]{:S(2)}) async-start(bf16[8,2,5,6144]{3,1,2,0:T(2,128)(2,1)} %bitcast.23), calls=%async_computation | async-start | bytes 1966080 | tf_op jit(solution)/shard_map/all_to_all | solution.py:56
  22.0 25.2 %all-to-all-done = bf16[8,2,5,6144]{3,1,2,0:T(2,128)(2,1)} async-done(((bf16[8,2,5,6144]{3,1,2,0:T(2,128)(2,1)}), bf16[8,2,5,6144]{3,1,2,0:T(2,128)(2,1)}, u32[]{:S(2)}, u32[]{:S(2)}) %all-to-all-start) | async-done | bytes 983072 | tf_op jit(solution)/shard_map/all_to_all | solution.py:56
  47.1 28.1 %fusion.4 = bf16[8,2,5,6144]{3,0,2,1:T(8,128)(2,1)} fusion(bf16[3072,6144]{1,0:T(8,128)(2,1)} %param.12, bf16[6144,3072]{1,0:T(8,128)(2,1)} %param.11, bf16[8,2,5,6144]{3,1,2,0:T(2,128)(2,1)} %all-to-all-done, f32[2,3072]{1,0:T(2,128)S(1)} %compare_convert_fusion), kind=kOutput, calls=%fused_computation.4 | convolution fusion | flops 6041763840 | bytes 77488128 | tf_op jit(solution)/shard_map/spmc,cd->spmd/dot_general | solution.py:61
  75.2 3.2 %copy.23 = bf16[8,2,5,6144]{3,1,2,0:T(2,128)(2,1)} copy(bf16[8,2,5,6144]{3,0,2,1:T(8,128)(2,1)} %fusion.4) | data formatting | bytes 1966080 | tf_op jit(solution)/shard_map/convert_element_type | solution.py:63
  78.4 4.2 %all-to-all-start.1 = ((bf16[8,2,5,6144]{3,1,2,0:T(2,128)(2,1)}), bf16[8,2,5,6144]{3,1,2,0:T(2,128)(2,1)}, u32[]{:S(2)}, u32[]{:S(2)}) async-start(bf16[8,2,5,6144]{3,1,2,0:T(2,128)(2,1)} %copy.23), calls=%async_computation.1 | async-start | bytes 1966080 | tf_op jit(solution)/shard_map/all_to_all | solution.py:64
  82.7 0.1 copy.20
  82.9 0.3 convolution_convert_fusion.2
  83.4 24.5 %all-to-all-done.1 = bf16[8,2,5,6144]{3,1,2,0:T(2,128)(2,1)} async-done(((bf16[8,2,5,6144]{3,1,2,0:T(2,128)(2,1)}), bf16[8,2,5,6144]{3,1,2,0:T(2,128)(2,1)}, u32[]{:S(2)}, u32[]{:S(2)}) %all-to-all-start.1) | async-done | bytes 983072 | tf_op jit(solution)/shard_map/all_to_all | solution.py:64
  107.8 2.7 %copy.24 = bf16[8,2,5,6144]{3,2,1,0:T(8,128)(2,1)} copy(bf16[8,2,5,6144]{3,1,2,0:T(2,128)(2,1)} %all-to-all-done.1) | data formatting | bytes 1966080 | tf_op jit(solution)/shard_map/all_to_all | solution.py:64
  110.5 2.4 %reshape.91 = bf16[80,6144]{1,0:T(8,128)(2,1)} reshape(bf16[8,2,5,6144]{3,2,1,0:T(8,128)(2,1)} %copy.24) | data formatting | bytes 1966080 | tf_op jit(solution)/shard_map/reshape | solution.py:80
  112.9 2.1 %fusion.29 = f32[8,6144]{1,0:T(8,128)} fusion(bf16[8,80]{1,0:T(8,128)(2,1)S(1)} %convert_element_type.52, bf16[80,6144]{1,0:T(8,128)(2,1)} %reshape.91), kind=kOutput, calls=%fused_computation.43 | convolution fusion | flops 7864320 | bytes 1180928 | tf_op jit(solution)/shard_map/dot_general | solution.py:78
  115.1 21.3 %all-reduce.2.cloned.1.call-done = f32[8,6144]{1,0:T(8,128)} async-done(((f32[8,6144]{1,0:T(8,128)}), f32[8,6144]{1,0:T(8,128)}) %all-reduce.2.cloned.1.call-update) | async-done | bytes 196624 | tf_op jit(solution)/shard_map/psum | solution.py:84
  136.4 1.1 multiply_reduce_fusion
  137.6 14.5 %all_gather.3 = bf16[64,3072]{1,0:T(8,128)(2,1)S(1)} all-gather(bf16[8,3072]{1,0:T(8,128)(2,1)S(1)} %multiply_convert_fusion.1), channel_id=1, replica_groups=mesh['group'=2,'ep'=4,'tp'=2,'dp'=2] {'ep','dp'}, dimensions={0}, use_global_device_ids=true | all-gather | bytes 442368 | tf_op jit(solution)/shard_map/all_gather | solution.py:91
  152.1 1.3 fusion.30
  153.4 10.5 %reduce-scatter.2.cloned.1.call-done = f32[32,512]{1,0:T(8,128)} async-done(((f32[64,512]{1,0:T(8,128)}), f32[32,512]{1,0:T(8,128)}) %reduce-scatter.2.cloned.1.call-update) | async-done | bytes 65552 | tf_op jit(solution)/shard_map/reduce_scatter | solution.py:95
  163.9 1.5 convert_element_type.59
  (27 shorter events, 0.8 us)
Async XLA Ops:
  6.5 145.6 %copy-start = (bf16[3072,512]{1,0:T(8,128)(2,1)S(1)}, bf16[3072,512]{1,0:T(8,128)(2,1)}, u32[]{:S(2)}) copy-start(bf16[3072,512]{1,0:T(8,128)(2,1)} %param.13) | copy-start | bytes 9437188
  15.5 31.6 %all-to-all-start = ((bf16[8,2,5,6144]{3,1,2,0:T(2,128)(2,1)}), bf16[8,2,5,6144]{3,1,2,0:T(2,128)(2,1)}, u32[]{:S(2)}, u32[]{:S(2)}) async-start(bf16[8,2,5,6144]{3,1,2,0:T(2,128)(2,1)} %bitcast.23), calls=%async_computation | async-start | bytes 1966080 | tf_op jit(solution)/shard_map/all_to_all | solution.py:56
  21.9 60.8 %copy-start.3 = (f32[8,4]{0,1:T(4,128)S(1)}, f32[8,4]{0,1:T(4,128)}, u32[]{:S(2)}) copy-start(f32[8,4]{0,1:T(4,128)} %param.10) | copy-start | bytes 388
  21.9 114.5 %copy-start.1 = (bf16[8,6144]{1,0:T(8,128)(2,1)S(1)}, bf16[8,6144]{1,0:T(8,128)(2,1)}, u32[]{:S(2)}) copy-start(bf16[8,6144]{1,0:T(8,128)(2,1)} %param.7) | copy-start | bytes 294916
  22.0 115.6 %copy-start.2 = (f32[3072]{0:T(1024)S(1)}, f32[3072]{0:T(1024)}, u32[]{:S(2)}) copy-start(f32[3072]{0:T(1024)} %param.8) | copy-start | bytes 36868
  78.4 29.4 %all-to-all-start.1 = ((bf16[8,2,5,6144]{3,1,2,0:T(2,128)(2,1)}), bf16[8,2,5,6144]{3,1,2,0:T(2,128)(2,1)}, u32[]{:S(2)}, u32[]{:S(2)}) async-start(bf16[8,2,5,6144]{3,1,2,0:T(2,128)(2,1)} %copy.23), calls=%async_computation.1 | async-start | bytes 1966080 | tf_op jit(solution)/shard_map/all_to_all | solution.py:64
  82.6 53.8 %all-reduce.2.cloned.1.call-start = ((), (), s32[]{:S(2)}) async-start(), calls=%async_computation.3 | async-start | bytes 393216 | tf_op jit(solution)/shard_map/psum | solution.py:84
  115.1 48.8 %reduce-scatter.2.cloned.1.call-start = ((), (), s32[]{:S(2)}) async-start(), calls=%async_computation.4 | async-start | bytes 196608 | tf_op jit(solution)/shard_map/reduce_scatter | solution.py:95
Sparse Core Ops, SparseCore 0:
  115.2 21.1 all-reduce.1
  153.5 10.2 reduce-scatter.1
where the time goes:
time: 173 us; the launch traced here: 172 us
  waiting for transfers between devices  81.4 us (47%)
  matrix products  34 us (20%)
  local copies, waits for them, and re-layouts  15 us (9%)
  blocking collectives  14.5 us (8%)
  between operations  13.5 us (8%)
  starting transfers between devices  10.6 us (6%)
  other arithmetic  3.09 us (2%)
    dot_general x1, matrix products, body(): jnp.einsum('spmc,cd->spmd', hidden, w_down, preferred_element_type=jnp.fl...  28.1 us
    all_to_all x1, waiting for transfers between devices, body(): lax.all_to_all(outgoing, ('ep', 'dp'), split_axis=0, concat_axis=0, tiled...  25.2 us
    all_to_all x1, waiting for transfers between devices, body(): lax.all_to_all(partial_value, ('ep', 'dp'), split_axis=0, concat_axis=0,...  24.5 us
    psum x1, waiting for transfers between devices, body(): moe_full = lax.psum(moe_terms, 'tp')  21.3 us
    all_gather x1, blocking collectives, body(): lax.all_gather(normed, ('ep', 'dp'), axis=0, tiled=True)  14.5 us
    reduce_scatter x1, waiting for transfers between devices, body(): summed = lax.psum_scatter(projected, 'tp', scatter_dimension=0, tiled=True)  10.5 us
    all_to_all x1, starting transfers between devices, body(): lax.all_to_all(outgoing, ('ep', 'dp'), split_axis=0, concat_axis=0, tiled...  6.33 us
    all_to_all x1, starting transfers between devices, body(): lax.all_to_all(partial_value, ('ep', 'dp'), split_axis=0, concat_axis=0,...  4.23 us
  transfers between devices with their start and end apart: 4, of which 4 were waited for; matrix products, arithmetic and copies ran while one was open for 0% of the time, Pallas kernels for 0%

commit v1 on v0

v1 whole, which is shorter than its diff:
```python
import functools

import jax
import jax.numpy as jnp
from jax import lax
from jax.experimental import pallas as pl
from jax.experimental.pallas import tpu as pltpu
from jax.sharding import PartitionSpec as P

FF = 6144
EXPERTS = 8
EPSILON = 1e-05
LANES = 128
MIB = 1 << 20


def expert_index(col_count):
    place = lax.axis_index("ep") * lax.axis_size("tp") + lax.axis_index("tp")
    place = place * lax.axis_size("dp") + lax.axis_index("dp")
    return place * col_count // FF


def pack_kernel(tokens_ref, ids_ref, weight_ref, out_ref):
    rows, width = tokens_ref.shape
    out_ref[:, :width] = tokens_ref[...]
    weight = weight_ref[...]
    gates = (weight / jnp.sum(weight, axis=1, keepdims=True)).astype(jnp.bfloat16)
    gates = gates.astype(jnp.float32)
    ids = ids_ref[...]
    column = lax.broadcasted_iota(jnp.int32, (rows, LANES), 1)
    spread = jnp.zeros((rows, LANES), jnp.float32)
    for k in range(ids.shape[1]):
        spread += jnp.where(column == ids[:, k : k + 1], gates[:, k : k + 1], 0.0)
    out_ref[:, width:] = spread.astype(jnp.bfloat16)


def chunk_plan(width, pieces):
    n_tp, n_dp = pieces
    piece = width // (n_tp * n_dp)
    parts = max(1, -(-piece // 512))
    plan = [(jt, jd, part) for jd in reversed(range(n_dp)) for jt in reversed(range(n_tp)) for part in range(parts)]
    ring = min(4, len(plan))
    held = min(2, len(plan) - ring)
    return piece, piece // parts, plan, ring, held


def chunk_start(entry, piece, part_width, pieces):
    jt, jd, part = entry
    n_tp, n_dp = pieces
    at_tp = lax.rem(lax.axis_index("tp") + jt, n_tp)
    at_dp = lax.rem(lax.axis_index("dp") + jd, n_dp)
    return pl.multiple_of((at_tp * n_dp + at_dp) * piece + part * part_width, LANES)


def load_kernel(pieces, w_up_ref, w_down_ref, up_ref, held_ref, up_sem, held_sem):
    width = w_down_ref.shape[1]
    piece, part_width, plan, ring, held = chunk_plan(width, pieces)
    blocks = up_sem.shape[0]
    depth = w_up_ref.shape[0] // blocks
    copies = [
        pltpu.make_async_copy(
            w_up_ref.at[pl.ds(b * depth, depth), :], up_ref.at[pl.ds(b * depth, depth), :], up_sem.at[b]
        )
        for b in range(blocks)
    ]
    for h in range(held):
        start = chunk_start(plan[ring + h], piece, part_width, pieces)
        copies.append(
            pltpu.make_async_copy(w_down_ref.at[:, pl.ds(start, part_width)], held_ref.at[h], held_sem.at[h])
        )
    for copy in copies:
        copy.start()
    for copy in copies:
        copy.wait()


def expert_kernel(pieces, x_ref, up_ref, held_ref, w_down_ref, *refs):
    n_tp, n_dp = pieces
    outs, (hidden, slots, sem) = refs[:n_dp], refs[n_dp:]
    width = w_down_ref.shape[1]
    piece, part_width, plan, ring, held = chunk_plan(width, pieces)
    cols = up_ref.shape[1]
    rows = x_ref.shape[0]

    def fetch(at, slot):
        start = chunk_start(plan[at], piece, part_width, pieces)
        return pltpu.make_async_copy(w_down_ref.at[:, pl.ds(start, part_width)], slots.at[slot], sem.at[slot])

    for at in range(ring):
        fetch(at, at).start()

    step = 512 if cols % 512 == 0 else cols

    @pl.loop(0, cols // step)
    def _(i):
        at = pl.ds(pl.multiple_of(i * step, step), step)
        up = jnp.dot(x_ref[:, :width], up_ref[:, at], preferred_element_type=jnp.float32)
        hidden[:, at] = (up / (1.0 + jnp.exp(-up))).astype(jnp.bfloat16)

    mine = expert_index(cols)
    column = lax.broadcasted_iota(jnp.int32, (rows, LANES), 1)
    gate = jnp.sum(
        jnp.where(column == mine, x_ref[:, width:].astype(jnp.float32), 0.0), axis=1, keepdims=True
    )
    slot_of = {}
    free = []
    later = list(range(ring + held, len(plan)))
    for at in range(ring):
        slot_of[at] = at
    for at, (jt, jd, part) in enumerate(plan):
        if at in slot_of:
            slot = slot_of[at]
            fetch(at, slot).wait()
            block = slots[slot]
        else:
            block = held_ref[at - ring]
        value = jnp.dot(hidden[...], block, preferred_element_type=jnp.float32) * gate
        outs[jd][jt, :, part * part_width : (part + 1) * part_width] = value.astype(jnp.bfloat16)
        if at in slot_of and later:
            after = later.pop(0)
            slot_of[after] = slot_of[at]
            fetch(after, slot_of[at]).start()


def project_kernel(n_dp, *refs):
    xs, (inverse_ref, w_ref, out_ref, square_ref) = refs[:n_dp], refs[n_dp:]
    piece = xs[0].shape[1]
    total = None
    square = None
    for j, x_ref in enumerate(xs):
        at = lax.rem(lax.axis_index("dp") + n_dp - j, n_dp)
        rows = pl.ds(pl.multiple_of(at * piece, piece), piece)
        x = x_ref[...]
        term = jnp.dot(x, w_ref[rows, :], preferred_element_type=jnp.float32)
        plain = x.astype(jnp.float32) * inverse_ref[:, rows]
        part = jnp.sum(plain * plain, axis=1, keepdims=True)
        total = term if total is None else total + term
        square = part if square is None else square + part
    out_ref[...] = total
    square_ref[...] = jnp.broadcast_to(square, square_ref.shape)


def shift(x, axis, by):
    size = lax.axis_size(axis)
    return lax.ppermute(x, axis, [(i, (i + by) % size) for i in range(size)])


def flip(x, axis, bit):
    size = lax.axis_size(axis)
    return lax.ppermute(x, axis, [(i, i ^ bit) for i in range(size)])


VMEM = pl.BlockSpec(memory_space=pltpu.VMEM)
ANY = pl.BlockSpec(memory_space=pl.ANY)


def params(mib, **more):
    return pltpu.CompilerParams(vmem_limit_bytes=mib * MIB, **more)


def body(tokens, norm_gain, expert_ids, route_weight, w_up, w_down, w_qkv):
    n_ep, n_tp, n_dp = (lax.axis_size(a) for a in ("ep", "tp", "dp"))
    ep_index, tp_index, dp_index = (lax.axis_index(a) for a in ("ep", "tp", "dp"))
    rows_here, width = tokens.shape
    cols = w_up.shape[1]
    pieces = (n_tp, n_dp)
    piece, part_width, plan, ring, held = chunk_plan(width, pieces)
    rows = rows_here * n_ep * n_dp

    packed = pl.pallas_call(
        pack_kernel,
        out_shape=jax.ShapeDtypeStruct((rows_here, width + LANES), jnp.bfloat16),
        in_specs=[VMEM] * 3,
        out_specs=VMEM,
        compiler_params=params(1),
    )(tokens, expert_ids, route_weight)
    gathered = lax.all_gather(packed, ("ep", "dp"), axis=0, tiled=True)

    up_here, held_here = pl.pallas_call(
        functools.partial(load_kernel, pieces),
        out_shape=(
            pltpu.VMEM((width, cols), jnp.bfloat16),
            pltpu.VMEM((held, w_down.shape[0], part_width), jnp.bfloat16),
        ),
        in_specs=[ANY, ANY],
        out_specs=(VMEM, VMEM),
        scratch_shapes=[pltpu.SemaphoreType.DMA((8,)), pltpu.SemaphoreType.DMA((held,))],
        compiler_params=params(1),
        cost_estimate=pl.CostEstimate(flops=0, transcendentals=0, bytes_accessed=50 * MIB),
    )(w_up, w_down)
    up_here = pltpu.with_memory_space_constraint(up_here, pltpu.VMEM)
    held_here = pltpu.with_memory_space_constraint(held_here, pltpu.VMEM)

    outs = pl.pallas_call(
        functools.partial(expert_kernel, pieces),
        out_shape=tuple(pltpu.VMEM((n_tp, rows, piece), jnp.bfloat16) for _ in range(n_dp)),
        in_specs=[VMEM, VMEM, VMEM, ANY],
        out_specs=tuple(VMEM for _ in range(n_dp)),
        scratch_shapes=[
            pltpu.VMEM((rows, cols), jnp.bfloat16),
            pltpu.VMEM((ring, w_down.shape[0], part_width), jnp.bfloat16),
            pltpu.SemaphoreType.DMA((ring,)),
        ],
        compiler_params=params(20),
        cost_estimate=pl.CostEstimate(flops=4 * rows * cols * width, transcendentals=rows * cols, bytes_accessed=24 * MIB),
    )(gathered, up_here, held_here, w_down)

    total = outs[0].astype(jnp.float32)
    for j in range(1, n_dp):
        total = total + shift(outs[j], "dp", j).astype(jnp.float32)
    here = total[0]
    for j in range(1, n_tp):
        here = here + shift(total[j].astype(jnp.bfloat16), "tp", j).astype(jnp.float32)
    bit = 1
    while bit < n_ep:
        here = here + flip(here.astype(jnp.bfloat16), "ep", bit).astype(jnp.float32)
        bit *= 2
    start = (tp_index * n_dp + dp_index) * piece
    mixed = here + lax.dynamic_slice_in_dim(gathered, start, piece, 1).astype(jnp.float32)
    gain = lax.dynamic_slice_in_dim(norm_gain, dp_index * piece, piece, 0)
    scaled = (mixed * gain[None, :]).astype(jnp.bfloat16)
    features = [scaled] + [shift(scaled, "dp", j) for j in range(1, n_dp)]
    out_cols = w_qkv.shape[1]
    projected, squares = pl.pallas_call(
        functools.partial(project_kernel, n_dp),
        out_shape=(
            jax.ShapeDtypeStruct((rows, out_cols), jnp.float32),
            jax.ShapeDtypeStruct((rows, LANES), jnp.float32),
        ),
        in_specs=[VMEM] * (n_dp + 2),
        out_specs=(VMEM, VMEM),
        compiler_params=params(16),
    )(*features, (1.0 / norm_gain)[None, :], w_qkv)
    both = jnp.concatenate([projected, squares], axis=1)
    share = rows // n_tp
    total = lax.dynamic_slice_in_dim(both, tp_index * share, share, 0)
    for j in range(1, n_tp):
        at = lax.rem(tp_index + j, n_tp) * share
        total = total + shift(lax.dynamic_slice_in_dim(both, at, share, 0), "tp", j)
    scale = lax.rsqrt(total[:, out_cols : out_cols + 1] / width + EPSILON)
    return (total[:, :out_cols] * scale).astype(jnp.bfloat16)


def solution(mesh):
    return jax.shard_map(
        body,
        mesh=mesh,
        in_specs=(
            P(("group", "ep", "dp"), None),
            P("tp"),
            P(("group", "ep", "dp"), None),
            P(("group", "ep", "dp"), None),
            P(None, ("ep", "tp", "dp")),
            P(("ep", "tp", "dp"), None),
            P("tp", ("ep", "dp")),
        ),
        out_specs=P(("group", "tp"), ("ep", "dp")),
        check_vma=False,
    )
```

time: 173 us -> 113 us (0.65)
  waiting for transfers between devices: 81.4 us -> 24.9 us
  matrix products: 34 us -> 0 us
  Pallas kernels: 0 us -> 31.5 us
  local copies, waits for them, and re-layouts: 15 us -> 28.6 us
  between operations: 13.5 us -> 0.11 us
  blocking collectives: 14.5 us -> 18.4 us
  starting transfers between devices: 10.6 us -> 7.06 us
    all_to_all x2 -> x0, waiting for transfers between devices: 49.6 us -> none  [the longest x1 25.2 us: body(): lax.all_to_all(outgoing, ('ep', 'dp'), split_axis=0, concat_axis=0, tiled...]
    dot_general x6 -> x0, matrix products: 34 us -> none  [the longest x1 28.1 us: body(): jnp.einsum('spmc,cd->spmd', hidden, w_down, preferred_element_type=jnp.fl...]
    pallas_call x0 -> x4, Pallas kernels: none -> 31.5 us  [the longest x1 17 us: body(): pl.pallas_call(functools.partial(expert_kernel, pieces), out_shape=tuple(...]
    unnamed x9 -> x13, local copies, waits for them, and re-layouts: 0.93 us -> 28.5 us
    ppermute x0 -> x6, waiting for transfers between devices: none -> 24.9 us  [the longest x2 13.5 us: flip(): return lax.ppermute(x, axis, [(i, i ^ bit) for i in range(size)])]
    psum x1 -> x0, waiting for transfers between devices: 21.3 us -> none  [body(): moe_full = lax.psum(moe_terms, 'tp')]
    all_to_all x2 -> x0, starting transfers between devices: 10.6 us -> none  [the longest x1 6.33 us: body(): lax.all_to_all(outgoing, ('ep', 'dp'), split_axis=0, concat_axis=0, tiled...]
    reduce_scatter x1 -> x0, waiting for transfers between devices: 10.5 us -> none  [body(): summed = lax.psum_scatter(projected, 'tp', scatter_dimension=0, tiled=True)]
  transfers between devices with their start and end apart: 4 -> 6, of which waited for: 4 -> 6; matrix products, arithmetic and copies ran while one was open for 0% -> 0% of each run, Pallas kernels for 0% -> 0%
where the time goes in v1:
time: 113 us
  Pallas kernels  31.5 us (28%)
  local copies, waits for them, and re-layouts  28.6 us (25%)
  waiting for transfers between devices  24.9 us (22%)
  blocking collectives  18.4 us (16%)
  starting transfers between devices  7.06 us (6%)
  other arithmetic  2.07 us (2%)
    unnamed x13, local copies, waits for them, and re-layouts  28.5 us
    all_gather x1, blocking collectives, body(): gathered = lax.all_gather(packed, ('ep', 'dp'), axis=0, tiled=True)  18.4 us
    pallas_call x1, Pallas kernels, body(): pl.pallas_call(functools.partial(expert_kernel, pieces), out_shape=tuple(...  17 us
    pallas_call x1, Pallas kernels, body(): pl.pallas_call(functools.partial(load_kernel, pieces), out_shape=(pltpu.V...  13.7 us
    ppermute x2, waiting for transfers between devices, flip(): return lax.ppermute(x, axis, [(i, i ^ bit) for i in range(size)])  13.5 us
    ppermute x4, waiting for transfers between devices, shift(): return lax.ppermute(x, axis, [(i, (i + by) % size) for i in range(size)])  11.5 us
    ppermute x4, starting transfers between devices, shift(): return lax.ppermute(x, axis, [(i, (i + by) % size) for i in range(size)])  3.6 us
    ppermute x2, starting transfers between devices, flip(): return lax.ppermute(x, axis, [(i, i ^ bit) for i in range(size)])  3.46 us
  transfers between devices with their start and end apart: 6, of which 6 were waited for; matrix products, arithmetic and copies ran while one was open for 0% of the time, Pallas kernels for 0%

profile of v1, /device:TPU:0, one launch (start us, length us, event | category | flops | bytes accessed | tf_op | source)
XLA Modules:
  0.0 112.7 jit_solution(1271609309349851976)
XLA Ops:
  0.0 0.8 copy.10.ids_ref
  0.8 0.8 copy.11.weight_ref
  1.5 0.9 copy-done.3
  2.4 0.2 shard_map.73
  2.6 18.4 %all_gather.3.x_ref = bf16[64,6272]{1,0:T(8,128)(2,1)} all-gather(bf16[8,6272]{1,0:T(8,128)(2,1)S(1)} %shard_map.73), channel_id=1, replica_groups=mesh['group'=2,'ep'=4,'tp'=2,'dp'=2] {'ep','dp'}, dimensions={0}, use_global_device_ids=true | all-gather | bytes 903168 | tf_op jit(solution)/shard_map/all_gather | solution.py:177
  20.9 13.7 %shard_map.74 = (bf16[6144,3072]{1,0:T(8,128)(2,1)S(1)}, bf16[2,3072,512]{2,1,0:T(8,128)(2,1)S(1)}) custom-call(bf16[6144,3072]{1,0:T(8,128)(2,1)} %w_up_ref.1, bf16[3072,6144]{1,0:T(8,128)(2,1)} %w_down_ref.3), custom_call_target="tpu_custom_call" | custom-call | bytes 52428800 | tf_op jit(solution)/shard_map/pallas_call | solution.py:179
  34.7 12.4 %copy-done = bf16[6144,3072]{1,0:T(8,128)(2,1)} copy-done((bf16[6144,3072]{1,0:T(8,128)(2,1)}, bf16[6144,3072]{1,0:T(8,128)(2,1)S(1)}, u32[]{:S(2)}) %copy-start) | copy-done | bytes 37748760
  47.1 11.7 %copy-done.1 = bf16[6144,3072]{1,0:T(8,128)(2,1)S(1)} copy-done((bf16[6144,3072]{1,0:T(8,128)(2,1)S(1)}, bf16[6144,3072]{1,0:T(8,128)(2,1)}, u32[]{:S(2)}) %copy-start.1) | copy-done | bytes 37748760
  58.8 17.0 %shard_map.75 = (bf16[2,64,1536]{2,1,0:T(8,128)(2,1)S(1)}, bf16[2,64,1536]{2,1,0:T(8,128)(2,1)S(1)}) custom-call(bf16[64,6272]{1,0:T(8,128)(2,1)} %all_gather.3.x_ref, bf16[6144,3072]{1,0:T(8,128)(2,1)S(1)} %copy-done.1, bf16[2,3072,512]{2,1,0:T(8,128)(2,1)S(1)} %get-tuple-element.12.held_ref, bf16[3072,6144]{1,0:T(8,128)(2,1)} %w_down_ref.3), custom_call_target="tpu_custom_call" | custom-call | flops 4831838208 | bytes 25165824 | tf_op jit(solution)/shard_map/pallas_call | solution.py:194
  75.8 0.4 collective-permute-start
  76.2 1.4 %collective-permute-done = bf16[2,64,1536]{2,1,0:T(8,128)(2,1)S(1)} collective-permute-done((bf16[2,64,1536]{2,1,0:T(8,128)(2,1)S(1)}, bf16[2,64,1536]{2,1,0:T(8,128)(2,1)S(1)}, u32[]{:S(2)}, u32[]{:S(2)}) %collective-permute-start) | collective-permute-done | bytes 393248 | tf_op jit(solution)/shard_map/ppermute | solution.py:145
  77.7 1.6 %collective-permute-start.1 = (bf16[64,1536]{1,0:T(8,128)(2,1)S(1)}, bf16[64,1536]{1,0:T(8,128)(2,1)S(1)}, u32[]{:S(2)}, u32[]{:S(2)}) collective-permute-start(bf16[64,1536]{1,0:T(8,128)(2,1)S(1)} %fusion.2), channel_id=1, source_target_pairs={{0,2},{2,0},{1,3},{3,1},{4,6},{6,4},{5,7},{7,5},{8,10},{10,8},{9,1... | collective-permute-start | bytes 589832 | tf_op jit(solution)/shard_map/ppermute | solution.py:145
  79.3 5.7 %collective-permute-done.1 = bf16[64,1536]{1,0:T(8,128)(2,1)S(1)} collective-permute-done((bf16[64,1536]{1,0:T(8,128)(2,1)S(1)}, bf16[64,1536]{1,0:T(8,128)(2,1)S(1)}, u32[]{:S(2)}, u32[]{:S(2)}) %collective-permute-start.1) | collective-permute-done | bytes 196640 | tf_op jit(solution)/shard_map/ppermute | solution.py:145
  85.0 1.3 %collective-permute-start.2 = (bf16[64,1536]{1,0:T(8,128)(2,1)S(1)}, bf16[64,1536]{1,0:T(8,128)(2,1)S(1)}, u32[]{:S(2)}, u32[]{:S(2)}) collective-permute-start(bf16[64,1536]{1,0:T(8,128)(2,1)S(1)} %fusion.3), channel_id=1, source_target_pairs={{0,4},{4,0},{8,12},{12,8},{1,5},{5,1},{9,13},{13,9},{2,6},{6,2},{1... | collective-permute-start | bytes 589832 | tf_op jit(solution)/shard_map/ppermute | solution.py:150
  86.3 5.1 %collective-permute-done.2 = bf16[64,1536]{1,0:T(8,128)(2,1)S(1)} collective-permute-done((bf16[64,1536]{1,0:T(8,128)(2,1)S(1)}, bf16[64,1536]{1,0:T(8,128)(2,1)S(1)}, u32[]{:S(2)}, u32[]{:S(2)}) %collective-permute-start.2) | collective-permute-done | bytes 196640 | tf_op jit(solution)/shard_map/ppermute | solution.py:150
  91.5 2.1 %collective-permute-start.3 = (bf16[64,1536]{1,0:T(8,128)(2,1)S(1)}, bf16[64,1536]{1,0:T(8,128)(2,1)S(1)}, u32[]{:S(2)}, u32[]{:S(2)}) collective-permute-start(bf16[64,1536]{1,0:T(8,128)(2,1)S(1)} %fusion.1), channel_id=1, source_target_pairs={{0,8},{4,12},{8,0},{12,4},{1,9},{5,13},{9,1},{13,5},{2,10},{6,14},... | collective-permute-start | bytes 589832 | tf_op jit(solution)/shard_map/ppermute | solution.py:150
  93.7 8.4 %collective-permute-done.3 = bf16[64,1536]{1,0:T(8,128)(2,1)S(1)} collective-permute-done((bf16[64,1536]{1,0:T(8,128)(2,1)S(1)}, bf16[64,1536]{1,0:T(8,128)(2,1)S(1)}, u32[]{:S(2)}, u32[]{:S(2)}) %collective-permute-start.3) | collective-permute-done | bytes 196640 | tf_op jit(solution)/shard_map/ppermute | solution.py:150
  102.1 1.1 multiply_convert_fusion.refs_0_
  103.2 1.4 %collective-permute-done.4.refs_1_ = bf16[64,1536]{1,0:T(8,128)(2,1)S(1)} collective-permute-done((bf16[64,1536]{1,0:T(8,128)(2,1)S(1)}, bf16[64,1536]{1,0:T(8,128)(2,1)S(1)}, u32[]{:S(2)}, u32[]{:S(2)}) %collective-permute-start.4) | collective-permute-done | bytes 196640 | tf_op jit(solution)/shard_map/ppermute | solution.py:145
  104.6 1.9 %copy-done.2 = bf16[3072,512]{1,0:T(8,128)(2,1)S(1)} copy-done((bf16[3072,512]{1,0:T(8,128)(2,1)S(1)}, bf16[3072,512]{1,0:T(8,128)(2,1)}, u32[]{:S(2)}) %copy-start.2) | copy-done | bytes 3145752
  106.5 0.7 shard_map.76
  107.3 1.5 %collective-permute-start.5 = (f32[32,640]{1,0:T(8,128)S(1)}, f32[32,640]{1,0:T(8,128)S(1)}, u32[]{:S(2)}, u32[]{:S(2)}) collective-permute-start(f32[32,640]{1,0:T(8,128)S(1)} %constant_dynamic-slice_fusion), channel_id=1, source_target_pairs={{0,2},{2,0},{1,3},{3,1},{4,6},{6,4},{5,7},{7,5},{8,10},{10,8},{9,1... | collective-permute-start | bytes 245768 | tf_op jit(solution)/shard_map/ppermute | solution.py:145
  108.8 3.0 %collective-permute-done.5 = f32[32,640]{1,0:T(8,128)S(1)} collective-permute-done((f32[32,640]{1,0:T(8,128)S(1)}, f32[32,640]{1,0:T(8,128)S(1)}, u32[]{:S(2)}, u32[]{:S(2)}) %collective-permute-start.5) | collective-permute-done | bytes 81952 | tf_op jit(solution)/shard_map/ppermute | solution.py:145
  111.9 0.7 fusion.4
  (18 shorter events, 0.5 us)
Async XLA Ops:
  1.5 0.9 copy-start.3
  34.6 12.4 %copy-start = (bf16[6144,3072]{1,0:T(8,128)(2,1)}, bf16[6144,3072]{1,0:T(8,128)(2,1)S(1)}, u32[]{:S(2)}) copy-start(bf16[6144,3072]{1,0:T(8,128)(2,1)S(1)} %get-tuple-element.11.up_ref) | copy-start | bytes 113246208
  47.1 11.7 %copy-start.1 = (bf16[6144,3072]{1,0:T(8,128)(2,1)S(1)}, bf16[6144,3072]{1,0:T(8,128)(2,1)}, u32[]{:S(2)}) copy-start(bf16[6144,3072]{1,0:T(8,128)(2,1)} %copy-done) | copy-start | bytes 113246208
  58.8 34.8 %copy-start.4 = (f32[3072]{0:T(1024)S(1)}, f32[3072]{0:T(1024)}, u32[]{:S(2)}) copy-start(f32[3072]{0:T(1024)} %param.8) | copy-start | bytes 36868
  75.8 1.8 %collective-permute-start = (bf16[2,64,1536]{2,1,0:T(8,128)(2,1)S(1)}, bf16[2,64,1536]{2,1,0:T(8,128)(2,1)S(1)}, u32[]{:S(2)}, u32[]{:S(2)}) collective-permute-start(bf16[2,64,1536]{2,1,0:T(8,128)(2,1)S(1)} %get-tuple-element.14), channel_id=1, source_target_pairs={{0,1},{1,0},{2,3},{3,2},{4,5},{5,4},{6,7},{7,6},{8,9},{9,8},{10,11... | collective-permute-start | bytes 1179656 | tf_op jit(solution)/shard_map/ppermute | solution.py:145
  77.7 7.2 %collective-permute-start.1 = (bf16[64,1536]{1,0:T(8,128)(2,1)S(1)}, bf16[64,1536]{1,0:T(8,128)(2,1)S(1)}, u32[]{:S(2)}, u32[]{:S(2)}) collective-permute-start(bf16[64,1536]{1,0:T(8,128)(2,1)S(1)} %fusion.2), channel_id=1, source_target_pairs={{0,2},{2,0},{1,3},{3,1},{4,6},{6,4},{5,7},{7,5},{8,10},{10,8},{9,1... | collective-permute-start | bytes 589832 | tf_op jit(solution)/shard_map/ppermute | solution.py:145
  85.0 6.4 %collective-permute-start.2 = (bf16[64,1536]{1,0:T(8,128)(2,1)S(1)}, bf16[64,1536]{1,0:T(8,128)(2,1)S(1)}, u32[]{:S(2)}, u32[]{:S(2)}) collective-permute-start(bf16[64,1536]{1,0:T(8,128)(2,1)S(1)} %fusion.3), channel_id=1, source_target_pairs={{0,4},{4,0},{8,12},{12,8},{1,5},{5,1},{9,13},{13,9},{2,6},{6,2},{1... | collective-permute-start | bytes 589832 | tf_op jit(solution)/shard_map/ppermute | solution.py:150
  91.5 10.6 %collective-permute-start.3 = (bf16[64,1536]{1,0:T(8,128)(2,1)S(1)}, bf16[64,1536]{1,0:T(8,128)(2,1)S(1)}, u32[]{:S(2)}, u32[]{:S(2)}) collective-permute-start(bf16[64,1536]{1,0:T(8,128)(2,1)S(1)} %fusion.1), channel_id=1, source_target_pairs={{0,8},{4,12},{8,0},{12,4},{1,9},{5,13},{9,1},{13,5},{2,10},{6,14},... | collective-permute-start | bytes 589832 | tf_op jit(solution)/shard_map/ppermute | solution.py:150
  103.1 1.5 %collective-permute-start.4 = (bf16[64,1536]{1,0:T(8,128)(2,1)S(1)}, bf16[64,1536]{1,0:T(8,128)(2,1)S(1)}, u32[]{:S(2)}, u32[]{:S(2)}) collective-permute-start(bf16[64,1536]{1,0:T(8,128)(2,1)S(1)} %multiply_convert_fusion.refs_0_), channel_id=1, source_target_pairs={{0,1},{1,0},{2,3},{3,2},{4,5},{5,4},{6,7},{7,6},{8,9},{9,8},{10,11... | collective-permute-start | bytes 589832 | tf_op jit(solution)/shard_map/ppermute | solution.py:145
  104.6 1.9 %copy-start.2 = (bf16[3072,512]{1,0:T(8,128)(2,1)S(1)}, bf16[3072,512]{1,0:T(8,128)(2,1)}, u32[]{:S(2)}) copy-start(bf16[3072,512]{1,0:T(8,128)(2,1)} %refs_3_.1) | copy-start | bytes 9437188
  107.3 4.6 %collective-permute-start.5 = (f32[32,640]{1,0:T(8,128)S(1)}, f32[32,640]{1,0:T(8,128)S(1)}, u32[]{:S(2)}, u32[]{:S(2)}) collective-permute-start(f32[32,640]{1,0:T(8,128)S(1)} %constant_dynamic-slice_fusion), channel_id=1, source_target_pairs={{0,2},{2,0},{1,3},{3,1},{4,6},{6,4},{5,7},{7,5},{8,10},{10,8},{9,1... | collective-permute-start | bytes 245768 | tf_op jit(solution)/shard_map/ppermute | solution.py:145

commit v2 on v1

v2 whole, which is shorter than its diff:
```python
import functools

import jax
import jax.numpy as jnp
from jax import lax
from jax.experimental import pallas as pl
from jax.experimental.pallas import tpu as pltpu
from jax.sharding import PartitionSpec as P

FF = 6144
EXPERTS = 8
EPSILON = 1e-05
LANES = 128
MIB = 1 << 20


def expert_index(col_count):
    place = lax.axis_index("ep") * lax.axis_size("tp") + lax.axis_index("tp")
    place = place * lax.axis_size("dp") + lax.axis_index("dp")
    return place * col_count // FF


def pack_kernel(tokens_ref, ids_ref, weight_ref, out_ref, sem):
    rows, width = tokens_ref.shape
    copy = pltpu.make_async_copy(tokens_ref, out_ref.at[:, pl.ds(0, width)], sem)
    copy.start()
    weight = weight_ref[...]
    gates = (weight / jnp.sum(weight, axis=0, keepdims=True)).astype(jnp.bfloat16)
    gates = gates.astype(jnp.float32)
    row = lax.broadcasted_iota(jnp.int32, (rows, rows), 0)
    same = row == lax.broadcasted_iota(jnp.int32, (rows, rows), 1)
    column = lax.broadcasted_iota(jnp.int32, (rows, LANES), 1)
    spread = jnp.zeros((rows, LANES), jnp.float32)
    for k in range(ids_ref.shape[0]):
        named = jnp.sum(jnp.where(same, ids_ref[k : k + 1, :], 0), axis=1, keepdims=True)
        gate = jnp.sum(jnp.where(same, gates[k : k + 1, :], 0.0), axis=1, keepdims=True)
        spread += jnp.where(column == named, gate, 0.0)
    out_ref[:, width:] = spread.astype(jnp.bfloat16)
    copy.wait()


def up_plan(cols):
    step = 512 if cols % 512 == 0 else cols
    count = cols // step
    return step, count, max(1, count - 2)


def down_plan(width, pieces):
    n_tp, n_dp = pieces
    piece = width // (n_tp * n_dp)
    parts = max(1, -(-piece // 512))
    plan = [(jt, jd, part) for jd in reversed(range(n_dp)) for jt in reversed(range(n_tp)) for part in range(parts)]
    return piece, piece // parts, plan, min(4, len(plan))


def own_place(pieces, jt=0, jd=0):
    n_tp, n_dp = pieces
    at_tp = lax.rem(lax.axis_index("tp") + jt, n_tp)
    at_dp = lax.rem(lax.axis_index("dp") + jd, n_dp)
    return at_tp * n_dp + at_dp


def load_kernel(w_up_ref, blocks_ref, done_ref, sem):
    count, _, step = blocks_ref.shape
    copies = [
        pltpu.make_async_copy(w_up_ref.at[:, pl.ds(b * step, step)], blocks_ref.at[b], sem.at[b])
        for b in range(count)
    ]
    for copy in copies:
        copy.start()
    for copy in copies:
        copy.wait()
    done_ref[...] = jnp.zeros_like(done_ref)


def expert_kernel(pieces, n_parts, *refs):
    n_tp, n_dp = pieces
    parts, refs = refs[:n_parts], refs[n_parts:]
    early_ref, w_up_ref, w_down_ref, w_qkv_ref = refs[:4]
    outs, refs = refs[4 : 4 + n_dp], refs[4 + n_dp :]
    own_ref, qkv_ref, wide, x_ref, hidden, late_ref, slots, late_sem, slot_sem, qkv_sem = refs
    width, cols = w_up_ref.shape
    rows = x_ref.shape[0]
    step, count, early = up_plan(cols)
    piece, part_width, plan, ring = down_plan(width, pieces)

    def fetch_up(b):
        return pltpu.make_async_copy(
            w_up_ref.at[:, pl.ds(b * step, step)], late_ref.at[b - early], late_sem.at[b - early]
        )

    def fetch_down(at):
        jt, jd, part = plan[at]
        start = pl.multiple_of(own_place(pieces, jt, jd) * piece + part * part_width, LANES)
        return pltpu.make_async_copy(
            w_down_ref.at[:, pl.ds(start, part_width)], slots.at[at % ring], slot_sem.at[at % ring]
        )

    fetch_qkv = pltpu.make_async_copy(w_qkv_ref, qkv_ref, qkv_sem)
    for b in range(early, count):
        fetch_up(b).start()
    for at in range(ring):
        fetch_down(at).start()

    if n_parts == 1:
        x_ref[...] = parts[0][...]
    else:
        each = parts[0].shape[0]
        per_dp = n_parts // n_dp
        for i, part in enumerate(parts):
            shift_dp, flip_ep = divmod(i, per_dp)
            from_ep = lax.axis_index("ep") ^ flip_ep
            from_dp = lax.rem(lax.axis_index("dp") + n_dp - shift_dp, n_dp)
            at = pl.multiple_of((from_ep * n_dp + from_dp) * each, each)
            wide[pl.ds(at, each), :] = part[...].astype(jnp.float32)
        x_ref[...] = wide[...].astype(jnp.bfloat16)
    own_ref[...] = x_ref[:, pl.ds(pl.multiple_of(own_place(pieces) * piece, LANES), piece)]

    for b in range(count):
        if b >= early:
            fetch_up(b).wait()
        block = early_ref[b] if b < early else late_ref[b - early]
        up = jnp.dot(x_ref[:, :width], block, preferred_element_type=jnp.float32)
        hidden[:, b * step : (b + 1) * step] = (up / (1.0 + jnp.exp(-up))).astype(jnp.bfloat16)

    mine = expert_index(cols)
    column = lax.broadcasted_iota(jnp.int32, (rows, LANES), 1)
    gate = jnp.sum(
        jnp.where(column == mine, x_ref[:, width:].astype(jnp.float32), 0.0), axis=1, keepdims=True
    )
    for at, (jt, jd, part) in enumerate(plan):
        fetch_down(at).wait()
        value = jnp.dot(hidden[...], slots[at % ring], preferred_element_type=jnp.float32) * gate
        outs[jd][jt, :, part * part_width : (part + 1) * part_width] = value.astype(jnp.bfloat16)
        if at + ring < len(plan):
            fetch_down(at + ring).start()
            if at + ring == len(plan) - 1:
                fetch_qkv.start()
    if ring == len(plan):
        fetch_qkv.start()
    fetch_qkv.wait()


def project_kernel(pieces, *refs):
    n_tp, n_dp = pieces
    xs, refs = refs[:n_dp], refs[n_dp:]
    inverse_ref, w_ref, keep_ref, square_ref = refs[:4]
    sends, total_ref = refs[4 : 4 + n_tp - 1], refs[-1]
    piece = xs[0].shape[1]
    cols = w_ref.shape[1]
    total = None
    square = None
    for j, x_ref in enumerate(xs):
        at = lax.rem(lax.axis_index("dp") + n_dp - j, n_dp)
        rows = pl.ds(pl.multiple_of(at * piece, piece), piece)
        x = x_ref[...]
        term = jnp.dot(x, w_ref[rows, :], preferred_element_type=jnp.float32)
        plain = x.astype(jnp.float32) * inverse_ref[:, rows]
        part = jnp.sum(plain * plain, axis=1, keepdims=True)
        total = term if total is None else total + term
        square = part if square is None else square + part
    high = square.astype(jnp.bfloat16).astype(jnp.float32)
    middle = (square - high).astype(jnp.bfloat16).astype(jnp.float32)
    low = square - high - middle
    lane = lax.broadcasted_iota(jnp.int32, (square.shape[0], LANES), 1)
    tail = jnp.where(lane == 0, high, jnp.where(lane == 1, middle, jnp.where(lane == 2, low, 0.0)))
    total_ref[:, :cols] = total
    total_ref[:, cols:] = tail
    share = keep_ref.shape[0]
    tp_index = lax.axis_index("tp")
    mine = pl.ds(pl.multiple_of(tp_index * share, share), share)
    keep_ref[...] = total_ref[mine, :cols]
    square_ref[...] = total_ref[mine, cols:]
    for j, send_ref in enumerate(sends):
        theirs = lax.rem(tp_index + j + 1, n_tp)
        send_ref[...] = total_ref[pl.ds(pl.multiple_of(theirs * share, share), share), :].astype(jnp.bfloat16)


def shift(x, axis, by):
    size = lax.axis_size(axis)
    return lax.ppermute(x, axis, [(i, (i + by) % size) for i in range(size)])


def flip(x, axis, bits):
    size = lax.axis_size(axis)
    return lax.ppermute(x, axis, [(i, i ^ bits) for i in range(size)])


VMEM = pl.BlockSpec(memory_space=pltpu.VMEM)
ANY = pl.BlockSpec(memory_space=pl.ANY)
SCOPED = 31


def params(mib):
    return pltpu.CompilerParams(vmem_limit_bytes=mib * MIB)


def body(tokens, norm_gain, expert_ids, route_weight, w_up, w_down, w_qkv):
    n_ep, n_tp, n_dp = (lax.axis_size(a) for a in ("ep", "tp", "dp"))
    dp_index = lax.axis_index("dp")
    rows_here, width = tokens.shape
    cols = w_up.shape[1]
    pieces = (n_tp, n_dp)
    rows = rows_here * n_ep * n_dp
    step, count, early = up_plan(cols)
    piece, part_width, plan, ring = down_plan(width, pieces)

    packed = pl.pallas_call(
        pack_kernel,
        out_shape=jax.ShapeDtypeStruct((rows_here, width + LANES), jnp.bfloat16),
        in_specs=[ANY, VMEM, VMEM],
        out_specs=VMEM,
        scratch_shapes=[pltpu.SemaphoreType.DMA],
        compiler_params=params(SCOPED),
    )(tokens, expert_ids.T, route_weight.T)
    blocks, done = pl.pallas_call(
        load_kernel,
        out_shape=(
            pltpu.VMEM((early, width, step), jnp.bfloat16),
            jax.ShapeDtypeStruct((8, LANES), jnp.float32),
        ),
        in_specs=[ANY],
        out_specs=(VMEM, VMEM),
        scratch_shapes=[pltpu.SemaphoreType.DMA((early,))],
        compiler_params=params(SCOPED),
        cost_estimate=pl.CostEstimate(flops=0, transcendentals=0, bytes_accessed=2 * early * width * step),
    )(w_up)
    blocks = pltpu.with_memory_space_constraint(blocks, pltpu.VMEM)

    if n_ep <= 4:
        parts = {0: packed}
        for bits in reversed(range(1, n_ep)):
            parts[bits] = flip(packed, "ep", bits)
        parts = [parts[bits] for bits in range(n_ep)]
        parts = [lax.optimization_barrier((part, done))[0] for part in parts]
        parts = parts + [shift(part, "dp", j) for j in range(1, n_dp) for part in parts]
    else:
        parts = [lax.all_gather(packed, ("ep", "dp"), axis=0, tiled=True)]

    late = max(1, count - early)
    results = pl.pallas_call(
        functools.partial(expert_kernel, pieces, len(parts)),
        out_shape=(
            *(pltpu.VMEM((n_tp, rows, piece), jnp.bfloat16) for _ in range(n_dp)),
            pltpu.VMEM((rows, piece), jnp.bfloat16),
            pltpu.VMEM(w_qkv.shape, jnp.bfloat16),
        ),
        in_specs=[VMEM] * (len(parts) + 1) + [ANY] * 3,
        out_specs=tuple(VMEM for _ in range(n_dp + 2)),
        scratch_shapes=[
            pltpu.VMEM((rows, width + LANES), jnp.float32),
            pltpu.VMEM((rows, width + LANES), jnp.bfloat16),
            pltpu.VMEM((rows, cols), jnp.bfloat16),
            pltpu.VMEM((late, width, step), jnp.bfloat16),
            pltpu.VMEM((ring, cols, part_width), jnp.bfloat16),
            pltpu.SemaphoreType.DMA((late,)),
            pltpu.SemaphoreType.DMA((ring,)),
            pltpu.SemaphoreType.DMA,
        ],
        compiler_params=params(SCOPED),
        cost_estimate=pl.CostEstimate(
            flops=4 * rows * cols * width, transcendentals=rows * cols, bytes_accessed=2 * cols * width
        ),
    )(*parts, blocks, w_up, w_down, w_qkv)
    outs, own, qkv_weights = results[:n_dp], results[n_dp], results[n_dp + 1]

    total = outs[0].astype(jnp.float32)
    for j in range(1, n_dp):
        total = total + shift(outs[j], "dp", j).astype(jnp.float32)
    here = total[0]
    for j in range(1, n_tp):
        here = here + shift(total[j].astype(jnp.bfloat16), "tp", j).astype(jnp.float32)
    bit = 1
    while bit < n_ep:
        here = here + flip(here.astype(jnp.bfloat16), "ep", bit).astype(jnp.float32)
        bit *= 2
    mixed = here + own.astype(jnp.float32)
    gain = lax.dynamic_slice_in_dim(norm_gain, dp_index * piece, piece, 0)
    scaled = (mixed * gain[None, :]).astype(jnp.bfloat16)
    features = [scaled] + [shift(scaled, "dp", j) for j in range(1, n_dp)]
    out_cols = w_qkv.shape[1]
    share = rows // n_tp
    projected = pl.pallas_call(
        functools.partial(project_kernel, pieces),
        out_shape=(
            jax.ShapeDtypeStruct((share, out_cols), jnp.float32),
            jax.ShapeDtypeStruct((share, LANES), jnp.float32),
            *(jax.ShapeDtypeStruct((share, out_cols + LANES), jnp.bfloat16) for _ in range(n_tp - 1)),
        ),
        in_specs=[VMEM] * (n_dp + 2),
        out_specs=tuple(VMEM for _ in range(n_tp + 1)),
        scratch_shapes=[pltpu.VMEM((rows, out_cols + LANES), jnp.float32)],
        compiler_params=params(16),
    )(*features, (1.0 / norm_gain)[None, :], pltpu.with_memory_space_constraint(qkv_weights, pltpu.VMEM))
    total, squares = projected[0], projected[1]
    for j in range(1, n_tp):
        received = shift(projected[1 + j], "tp", j).astype(jnp.float32)
        total = total + received[:, :out_cols]
        squares = squares + received[:, out_cols:]
    scale = lax.rsqrt(jnp.sum(squares[:, :3], axis=1, keepdims=True) / width + EPSILON)
    return (total * scale).astype(jnp.bfloat16)


def solution(mesh):
    return jax.shard_map(
        body,
        mesh=mesh,
        in_specs=(
            P(("group", "ep", "dp"), None),
            P("tp"),
            P(("group", "ep", "dp"), None),
            P(("group", "ep", "dp"), None),
            P(None, ("ep", "tp", "dp")),
            P(("ep", "tp", "dp"), None),
            P("tp", ("ep", "dp")),
        ),
        out_specs=P(("group", "tp"), ("ep", "dp")),
        check_vma=False,
    )
```

time: 113 us -> 81.1 us (0.72)
  local copies, waits for them, and re-layouts: 28.6 us -> 2.99 us
  blocking collectives: 18.4 us -> 0 us
  starting transfers between devices: 7.06 us -> 14.2 us
  Pallas kernels: 31.5 us -> 34.7 us
    unnamed x13 -> x28, local copies, waits for them, and re-layouts: 28.5 us -> 2.89 us
    all_gather x1 -> x0, blocking collectives: 18.4 us -> none  [body(): gathered = lax.all_gather(packed, ('ep', 'dp'), axis=0, tiled=True)]
    ppermute x2 -> x5, starting transfers between devices: 3.46 us -> 9.29 us  [flip(): return lax.ppermute(x, axis, [(i, i ^ bits) for i in range(size)])]
    pallas_call x3, Pallas kernels: 31.4 us -> 34.5 us  [the longest x1 25 us: body(): pl.pallas_call(functools.partial(expert_kernel, pieces, len(parts)), out_...]
    ppermute x4 -> x8, starting transfers between devices: 3.6 us -> 4.88 us  [shift(): return lax.ppermute(x, axis, [(i, (i + by) % size) for i in range(size)])]
    ppermute x2 -> x5, waiting for transfers between devices: 13.5 us -> 13.9 us  [flip(): return lax.ppermute(x, axis, [(i, i ^ bits) for i in range(size)])]
    ppermute x4 -> x8, waiting for transfers between devices: 11.5 us -> 11.9 us  [shift(): return lax.ppermute(x, axis, [(i, (i + by) % size) for i in range(size)])]
  transfers between devices with their start and end apart: 6 -> 13, of which waited for: 6 -> 10; matrix products, arithmetic and copies ran while one was open for 0% -> 0% of each run, Pallas kernels for 0% -> 11%
where the time goes in v2:
time: 81.1 us; the launch traced here: 80.9 us
  Pallas kernels  34.7 us (43%)
  waiting for transfers between devices  25.8 us (32%)
  starting transfers between devices  14.2 us (18%)
  other arithmetic  3.05 us (4%)
  local copies, waits for them, and re-layouts  2.99 us (4%)
    pallas_call x1, Pallas kernels, body(): pl.pallas_call(functools.partial(expert_kernel, pieces, len(parts)), out_...  25 us
    ppermute x5, waiting for transfers between devices, flip(): return lax.ppermute(x, axis, [(i, i ^ bits) for i in range(size)])  13.9 us
    ppermute x8, waiting for transfers between devices, shift(): return lax.ppermute(x, axis, [(i, (i + by) % size) for i in range(size)])  11.9 us
    ppermute x5, starting transfers between devices, flip(): return lax.ppermute(x, axis, [(i, i ^ bits) for i in range(size)])  9.29 us
    pallas_call x1, Pallas kernels, body(): pl.pallas_call(load_kernel, out_shape=(pltpu.VMEM((early, width, step), j...  8.86 us
    ppermute x8, starting transfers between devices, shift(): return lax.ppermute(x, axis, [(i, (i + by) % size) for i in range(size)])  4.88 us
    unnamed x28, local copies, waits for them, and re-layouts  2.89 us
  transfers between devices with their start and end apart: 13, of which 10 were waited for; matrix products, arithmetic and copies ran while one was open for 0% of the time, Pallas kernels for 11%

profile of v2, /device:TPU:0, one launch (start us, length us, event | category | flops | bytes accessed | tf_op | source)
XLA Modules:
  0.0 80.9 jit_solution(14999625920041653127)
XLA Ops:
  0.0 0.9 %copy-done.1 = bf16[8,6144]{1,0:T(8,128)(2,1)S(1)} copy-done((bf16[8,6144]{1,0:T(8,128)(2,1)S(1)}, bf16[8,6144]{1,0:T(8,128)(2,1)}, u32[]{:S(2)}) %copy-start.1) | copy-done | bytes 98328
  0.9 0.7 copy-done.2
  1.6 0.7 copy-done.3
  2.5 3.1 %collective-permute-start = (bf16[8,6272]{1,0:T(8,128)(2,1)S(1)}, bf16[8,6272]{1,0:T(8,128)(2,1)S(1)}, u32[]{:S(2)}, u32[]{:S(2)}) collective-permute-start(bf16[8,6272]{1,0:T(8,128)(2,1)S(1)} %shard_map.73.refs_0_), channel_id=1, source_target_pairs={{0,4},{4,0},{8,12},{12,8},{1,5},{5,1},{9,13},{13,9},{2,6},{6,2},{1... | collective-permute-start | bytes 301064 | tf_op jit(solution)/shard_map/ppermute | solution.py:186
  5.6 2.6 %collective-permute-start.1 = (bf16[8,6272]{1,0:T(8,128)(2,1)S(1)}, bf16[8,6272]{1,0:T(8,128)(2,1)S(1)}, u32[]{:S(2)}, u32[]{:S(2)}) collective-permute-start(bf16[8,6272]{1,0:T(8,128)(2,1)S(1)} %shard_map.73.refs_0_), channel_id=1, source_target_pairs={{0,8},{4,12},{8,0},{12,4},{1,9},{5,13},{9,1},{13,5},{2,10},{6,14},... | collective-permute-start | bytes 301064 | tf_op jit(solution)/shard_map/ppermute | solution.py:186
  8.2 8.9 %shard_map.74 = (bf16[4,6144,512]{2,1,0:T(8,128)(2,1)S(1)}, f32[8,128]{1,0:T(8,128)}) custom-call(bf16[6144,3072]{1,0:T(8,128)(2,1)} %refs_9_.1), custom_call_target="tpu_custom_call" | custom-call | bytes 25165824 | tf_op jit(solution)/shard_map/pallas_call | solution.py:216
  17.1 0.5 collective-permute-start.4
  17.7 0.4 collective-permute-start.6
  19.7 25.0 %shard_map.75 = (bf16[2,64,1536]{2,1,0:T(8,128)(2,1)S(1)}, bf16[2,64,1536]{2,1,0:T(8,128)(2,1)S(1)}, bf16[64,1536]{1,0:T(8,128)(2,1)S(1)}, bf16[3072,512]{1,0:T(8,128)(2,1)S(1)}) custom-call(bf16[8,6272]{1,0:T(8,128)(2,1)} %copy-done, bf16[8,6272]{1,0:T(8,128)(2,1)} %copy-done.6, bf16[8,6272]{1,0:T(8,128)(2,1)} %copy-done.7, bf16[8,6272]{1,0:T(8,128)(2,1)} %copy-done.8, ...), custom_call_target="tpu_custom_call" | custom-call | flops 4831838208 | bytes 37748736 | tf_op jit(solution)/shard_map/pallas_call | solution.py:241
  44.7 0.6 collective-permute-start.7
  45.3 1.3 %collective-permute-done.7 = bf16[2,64,1536]{2,1,0:T(8,128)(2,1)S(1)} collective-permute-done((bf16[2,64,1536]{2,1,0:T(8,128)(2,1)S(1)}, bf16[2,64,1536]{2,1,0:T(8,128)(2,1)S(1)}, u32[]{:S(2)}, u32[]{:S(2)}) %collective-permute-start.7) | collective-permute-done | bytes 393248 | tf_op jit(solution)/shard_map/ppermute | solution.py:181
  46.8 1.7 %collective-permute-start.8 = (bf16[64,1536]{1,0:T(8,128)(2,1)S(1)}, bf16[64,1536]{1,0:T(8,128)(2,1)S(1)}, u32[]{:S(2)}, u32[]{:S(2)}) collective-permute-start(bf16[64,1536]{1,0:T(8,128)(2,1)S(1)} %fusion.2), channel_id=1, source_target_pairs={{0,2},{2,0},{1,3},{3,1},{4,6},{6,4},{5,7},{7,5},{8,10},{10,8},{9,1... | collective-permute-start | bytes 589832 | tf_op jit(solution)/shard_map/ppermute | solution.py:181
  48.5 5.5 %collective-permute-done.8 = bf16[64,1536]{1,0:T(8,128)(2,1)S(1)} collective-permute-done((bf16[64,1536]{1,0:T(8,128)(2,1)S(1)}, bf16[64,1536]{1,0:T(8,128)(2,1)S(1)}, u32[]{:S(2)}, u32[]{:S(2)}) %collective-permute-start.8) | collective-permute-done | bytes 196640 | tf_op jit(solution)/shard_map/ppermute | solution.py:181
  54.1 1.0 %collective-permute-start.9 = (bf16[64,1536]{1,0:T(8,128)(2,1)S(1)}, bf16[64,1536]{1,0:T(8,128)(2,1)S(1)}, u32[]{:S(2)}, u32[]{:S(2)}) collective-permute-start(bf16[64,1536]{1,0:T(8,128)(2,1)S(1)} %fusion.3), channel_id=1, source_target_pairs={{0,4},{4,0},{8,12},{12,8},{1,5},{5,1},{9,13},{13,9},{2,6},{6,2},{1... | collective-permute-start | bytes 589832 | tf_op jit(solution)/shard_map/ppermute | solution.py:186
  55.0 5.5 %collective-permute-done.9 = bf16[64,1536]{1,0:T(8,128)(2,1)S(1)} collective-permute-done((bf16[64,1536]{1,0:T(8,128)(2,1)S(1)}, bf16[64,1536]{1,0:T(8,128)(2,1)S(1)}, u32[]{:S(2)}, u32[]{:S(2)}) %collective-permute-start.9) | collective-permute-done | bytes 196640 | tf_op jit(solution)/shard_map/ppermute | solution.py:186
  60.5 0.8 fusion.1
  61.3 2.6 %collective-permute-start.10 = (bf16[64,1536]{1,0:T(8,128)(2,1)}, bf16[64,1536]{1,0:T(8,128)(2,1)}, u32[]{:S(2)}, u32[]{:S(2)}) collective-permute-start(bf16[64,1536]{1,0:T(8,128)(2,1)} %fusion.1), channel_id=1, source_target_pairs={{0,8},{4,12},{8,0},{12,4},{1,9},{5,13},{9,1},{13,5},{2,10},{6,14},... | collective-permute-start | bytes 589832 | tf_op jit(solution)/shard_map/ppermute | solution.py:186
  64.0 8.5 %collective-permute-done.10 = bf16[64,1536]{1,0:T(8,128)(2,1)} collective-permute-done((bf16[64,1536]{1,0:T(8,128)(2,1)}, bf16[64,1536]{1,0:T(8,128)(2,1)}, u32[]{:S(2)}, u32[]{:S(2)}) %collective-permute-start.10) | collective-permute-done | bytes 196640 | tf_op jit(solution)/shard_map/ppermute | solution.py:186
  72.5 1.3 %multiply_convert_fusion.refs_0_ = bf16[64,1536]{1,0:T(8,128)(2,1)S(1)} fusion(bf16[64,1536]{1,0:T(8,128)(2,1)S(1)} %get-tuple-element.26, bf16[64,1536]{1,0:T(8,128)(2,1)} %collective-permute-done.10, bf16[64,1536]{1,0:T(8,128)(2,1)} %copy-done.5, f32[1536]{0:T(1024)S(1)} %dynamic_slice.3, bf16[64,1536]{1,0:T(8,128)(2,1)S(1)} %collective-permute-done.8, ...), kind=kLoop, calls=%fused_computation.4 | loop fusion | flops 983040 | bytes 1382400 | tf_op jit(solution)/shard_map/convert_element_type | solution.py:279
  73.9 1.4 %collective-permute-done.11.refs_1_ = bf16[64,1536]{1,0:T(8,128)(2,1)S(1)} collective-permute-done((bf16[64,1536]{1,0:T(8,128)(2,1)S(1)}, bf16[64,1536]{1,0:T(8,128)(2,1)S(1)}, u32[]{:S(2)}, u32[]{:S(2)}) %collective-permute-start.11) | collective-permute-done | bytes 196640 | tf_op jit(solution)/shard_map/ppermute | solution.py:181
  75.3 0.7 shard_map.76
  76.0 1.5 %collective-permute-start.12 = (bf16[32,640]{1,0:T(8,128)(2,1)S(1)}, bf16[32,640]{1,0:T(8,128)(2,1)S(1)}, u32[]{:S(2)}, u32[]{:S(2)}) collective-permute-start(bf16[32,640]{1,0:T(8,128)(2,1)S(1)} %get-tuple-element.29), channel_id=1, source_target_pairs={{0,2},{2,0},{1,3},{3,1},{4,6},{6,4},{5,7},{7,5},{8,10},{10,8},{9,1... | collective-permute-start | bytes 122888 | tf_op jit(solution)/shard_map/ppermute | solution.py:181
  77.5 2.6 %collective-permute-done.12 = bf16[32,640]{1,0:T(8,128)(2,1)S(1)} collective-permute-done((bf16[32,640]{1,0:T(8,128)(2,1)S(1)}, bf16[32,640]{1,0:T(8,128)(2,1)S(1)}, u32[]{:S(2)}, u32[]{:S(2)}) %collective-permute-start.12) | collective-permute-done | bytes 40992 | tf_op jit(solution)/shard_map/ppermute | solution.py:181
  80.2 0.7 fusion.5
  (46 shorter events, 2.4 us)
Async XLA Ops:
  0.0 0.9 %copy-start.1 = (bf16[8,6144]{1,0:T(8,128)(2,1)S(1)}, bf16[8,6144]{1,0:T(8,128)(2,1)}, u32[]{:S(2)}) copy-start(bf16[8,6144]{1,0:T(8,128)(2,1)} %tokens_ref.1) | copy-start | bytes 294916
  0.9 0.7 copy-start.2
  1.6 0.7 copy-start.3
  2.5 16.6 %copy-start = (bf16[8,6272]{1,0:T(8,128)(2,1)}, bf16[8,6272]{1,0:T(8,128)(2,1)S(1)}, u32[]{:S(2)}) copy-start(bf16[8,6272]{1,0:T(8,128)(2,1)S(1)} %shard_map.73.refs_0_) | copy-start | bytes 301060
  2.5 14.6 %collective-permute-start = (bf16[8,6272]{1,0:T(8,128)(2,1)S(1)}, bf16[8,6272]{1,0:T(8,128)(2,1)S(1)}, u32[]{:S(2)}, u32[]{:S(2)}) collective-permute-start(bf16[8,6272]{1,0:T(8,128)(2,1)S(1)} %shard_map.73.refs_0_), channel_id=1, source_target_pairs={{0,4},{4,0},{8,12},{12,8},{1,5},{5,1},{9,13},{13,9},{2,6},{6,2},{1... | collective-permute-start | bytes 301064 | tf_op jit(solution)/shard_map/ppermute | solution.py:186
  5.6 12.0 %collective-permute-start.1 = (bf16[8,6272]{1,0:T(8,128)(2,1)S(1)}, bf16[8,6272]{1,0:T(8,128)(2,1)S(1)}, u32[]{:S(2)}, u32[]{:S(2)}) collective-permute-start(bf16[8,6272]{1,0:T(8,128)(2,1)S(1)} %shard_map.73.refs_0_), channel_id=1, source_target_pairs={{0,8},{4,12},{8,0},{12,4},{1,9},{5,13},{9,1},{13,5},{2,10},{6,14},... | collective-permute-start | bytes 301064 | tf_op jit(solution)/shard_map/ppermute | solution.py:186
  8.2 9.6 %collective-permute-start.2 = (bf16[8,6272]{1,0:T(8,128)(2,1)S(1)}, bf16[8,6272]{1,0:T(8,128)(2,1)S(1)}, u32[]{:S(2)}, u32[]{:S(2)}) collective-permute-start(bf16[8,6272]{1,0:T(8,128)(2,1)S(1)} %shard_map.73.refs_0_), channel_id=1, source_target_pairs={{0,12},{4,8},{8,4},{12,0},{1,13},{5,9},{9,5},{13,1},{2,14},{6,10},... | collective-permute-start | bytes 301064 | tf_op jit(solution)/shard_map/ppermute | solution.py:186
  17.0 1.4 %collective-permute-start.3 = (bf16[8,6272]{1,0:T(8,128)(2,1)S(1)}, bf16[8,6272]{1,0:T(8,128)(2,1)S(1)}, u32[]{:S(2)}, u32[]{:S(2)}) collective-permute-start(bf16[8,6272]{1,0:T(8,128)(2,1)S(1)} %shard_map.73.refs_0_), channel_id=1, source_target_pairs={{0,1},{1,0},{2,3},{3,2},{4,5},{5,4},{6,7},{7,6},{8,9},{9,8},{10,11... | collective-permute-start | bytes 301064 | tf_op jit(solution)/shard_map/ppermute | solution.py:181
  17.1 2.0 %copy-start.6 = (bf16[8,6272]{1,0:T(8,128)(2,1)}, bf16[8,6272]{1,0:T(8,128)(2,1)S(1)}, u32[]{:S(2)}) copy-start(bf16[8,6272]{1,0:T(8,128)(2,1)S(1)} %collective-permute-done.refs_1_) | copy-start | bytes 301060
  17.1 1.4 %collective-permute-start.4 = (bf16[8,6272]{1,0:T(8,128)(2,1)S(1)}, bf16[8,6272]{1,0:T(8,128)(2,1)S(1)}, u32[]{:S(2)}, u32[]{:S(2)}) collective-permute-start(bf16[8,6272]{1,0:T(8,128)(2,1)S(1)} %collective-permute-done.refs_1_), channel_id=1, source_target_pairs={{0,1},{1,0},{2,3},{3,2},{4,5},{5,4},{6,7},{7,6},{8,9},{9,8},{10,11... | collective-permute-start | bytes 301064 | tf_op jit(solution)/shard_map/ppermute | solution.py:181
  17.6 1.5 %copy-start.7 = (bf16[8,6272]{1,0:T(8,128)(2,1)}, bf16[8,6272]{1,0:T(8,128)(2,1)S(1)}, u32[]{:S(2)}) copy-start(bf16[8,6272]{1,0:T(8,128)(2,1)S(1)} %collective-permute-done.1.refs_2_) | copy-start | bytes 301060
  17.6 1.3 %collective-permute-start.5 = (bf16[8,6272]{1,0:T(8,128)(2,1)S(1)}, bf16[8,6272]{1,0:T(8,128)(2,1)S(1)}, u32[]{:S(2)}, u32[]{:S(2)}) collective-permute-start(bf16[8,6272]{1,0:T(8,128)(2,1)S(1)} %collective-permute-done.1.refs_2_), channel_id=1, source_target_pairs={{0,1},{1,0},{2,3},{3,2},{4,5},{5,4},{6,7},{7,6},{8,9},{9,8},{10,11... | collective-permute-start | bytes 301064 | tf_op jit(solution)/shard_map/ppermute | solution.py:181
  17.7 1.4 %copy-start.8 = (bf16[8,6272]{1,0:T(8,128)(2,1)}, bf16[8,6272]{1,0:T(8,128)(2,1)S(1)}, u32[]{:S(2)}) copy-start(bf16[8,6272]{1,0:T(8,128)(2,1)S(1)} %collective-permute-done.2.refs_3_) | copy-start | bytes 301060
  17.7 1.4 %collective-permute-start.6 = (bf16[8,6272]{1,0:T(8,128)(2,1)S(1)}, bf16[8,6272]{1,0:T(8,128)(2,1)S(1)}, u32[]{:S(2)}, u32[]{:S(2)}) collective-permute-start(bf16[8,6272]{1,0:T(8,128)(2,1)S(1)} %collective-permute-done.2.refs_3_), channel_id=1, source_target_pairs={{0,1},{1,0},{2,3},{3,2},{4,5},{5,4},{6,7},{7,6},{8,9},{9,8},{10,11... | collective-permute-start | bytes 301064 | tf_op jit(solution)/shard_map/ppermute | solution.py:181
  18.4 0.7 copy-start.9
  19.7 44.2 %copy-start.13 = (f32[3072]{0:T(1024)S(1)}, f32[3072]{0:T(1024)}, u32[]{:S(2)}) copy-start(f32[3072]{0:T(1024)} %param.8) | copy-start | bytes 36868
  44.7 1.9 %collective-permute-start.7 = (bf16[2,64,1536]{2,1,0:T(8,128)(2,1)S(1)}, bf16[2,64,1536]{2,1,0:T(8,128)(2,1)S(1)}, u32[]{:S(2)}, u32[]{:S(2)}) collective-permute-start(bf16[2,64,1536]{2,1,0:T(8,128)(2,1)S(1)} %get-tuple-element.25), channel_id=1, source_target_pairs={{0,1},{1,0},{2,3},{3,2},{4,5},{5,4},{6,7},{7,6},{8,9},{9,8},{10,11... | collective-permute-start | bytes 1179656 | tf_op jit(solution)/shard_map/ppermute | solution.py:181
  46.7 13.8 %copy-start.4 = (f32[2,64,1536]{2,1,0:T(8,128)}, f32[2,64,1536]{2,1,0:T(8,128)S(1)}, u32[]{:S(2)}) copy-start(f32[2,64,1536]{2,1,0:T(8,128)S(1)} %convert_add_fusion) | copy-start | bytes 2359300
  46.8 7.2 %collective-permute-start.8 = (bf16[64,1536]{1,0:T(8,128)(2,1)S(1)}, bf16[64,1536]{1,0:T(8,128)(2,1)S(1)}, u32[]{:S(2)}, u32[]{:S(2)}) collective-permute-start(bf16[64,1536]{1,0:T(8,128)(2,1)S(1)} %fusion.2), channel_id=1, source_target_pairs={{0,2},{2,0},{1,3},{3,1},{4,6},{6,4},{5,7},{7,5},{8,10},{10,8},{9,1... | collective-permute-start | bytes 589832 | tf_op jit(solution)/shard_map/ppermute | solution.py:181
  54.1 6.4 %collective-permute-start.9 = (bf16[64,1536]{1,0:T(8,128)(2,1)S(1)}, bf16[64,1536]{1,0:T(8,128)(2,1)S(1)}, u32[]{:S(2)}, u32[]{:S(2)}) collective-permute-start(bf16[64,1536]{1,0:T(8,128)(2,1)S(1)} %fusion.3), channel_id=1, source_target_pairs={{0,4},{4,0},{8,12},{12,8},{1,5},{5,1},{9,13},{13,9},{2,6},{6,2},{1... | collective-permute-start | bytes 589832 | tf_op jit(solution)/shard_map/ppermute | solution.py:186
  60.5 0.8 copy-start.5
  61.3 11.2 %collective-permute-start.10 = (bf16[64,1536]{1,0:T(8,128)(2,1)}, bf16[64,1536]{1,0:T(8,128)(2,1)}, u32[]{:S(2)}, u32[]{:S(2)}) collective-permute-start(bf16[64,1536]{1,0:T(8,128)(2,1)} %fusion.1), channel_id=1, source_target_pairs={{0,8},{4,12},{8,0},{12,4},{1,9},{5,13},{9,1},{13,5},{2,10},{6,14},... | collective-permute-start | bytes 589832 | tf_op jit(solution)/shard_map/ppermute | solution.py:186
  73.8 1.5 %collective-permute-start.11 = (bf16[64,1536]{1,0:T(8,128)(2,1)S(1)}, bf16[64,1536]{1,0:T(8,128)(2,1)S(1)}, u32[]{:S(2)}, u32[]{:S(2)}) collective-permute-start(bf16[64,1536]{1,0:T(8,128)(2,1)S(1)} %multiply_convert_fusion.refs_0_), channel_id=1, source_target_pairs={{0,1},{1,0},{2,3},{3,2},{4,5},{5,4},{6,7},{7,6},{8,9},{9,8},{10,11... | collective-permute-start | bytes 589832 | tf_op jit(solution)/shard_map/ppermute | solution.py:181
  76.0 4.1 %collective-permute-start.12 = (bf16[32,640]{1,0:T(8,128)(2,1)S(1)}, bf16[32,640]{1,0:T(8,128)(2,1)S(1)}, u32[]{:S(2)}, u32[]{:S(2)}) collective-permute-start(bf16[32,640]{1,0:T(8,128)(2,1)S(1)} %get-tuple-element.29), channel_id=1, source_target_pairs={{0,2},{2,0},{1,3},{3,1},{4,6},{6,4},{5,7},{7,5},{8,10},{10,8},{9,1... | collective-permute-start | bytes 122888 | tf_op jit(solution)/shard_map/ppermute | solution.py:181
  (3 other events, 1.9 us)

commit v3 on v2

v3 whole, which is shorter than its diff:
```python
import functools

import jax
import jax.numpy as jnp
from jax import lax
from jax.experimental import pallas as pl
from jax.experimental.pallas import tpu as pltpu
from jax.sharding import PartitionSpec as P

FF = 6144
EXPERTS = 8
EPSILON = 1e-05
LANES = 128
MIB = 1 << 20


def expert_index(col_count):
    place = lax.axis_index("ep") * lax.axis_size("tp") + lax.axis_index("tp")
    place = place * lax.axis_size("dp") + lax.axis_index("dp")
    return place * col_count // FF


def pack_kernel(tokens_ref, ids_ref, weight_ref, out_ref, ids, weight, sem):
    rows, width = tokens_ref.shape
    copies = [
        pltpu.make_async_copy(ids_ref, ids, sem.at[0]),
        pltpu.make_async_copy(weight_ref, weight, sem.at[1]),
        pltpu.make_async_copy(tokens_ref, out_ref.at[:, pl.ds(0, width)], sem.at[2]),
    ]
    for copy in copies:
        copy.start()
    copies[0].wait()
    copies[1].wait()
    gates = (weight[...] / jnp.sum(weight[...], axis=0, keepdims=True)).astype(jnp.bfloat16)
    gates = gates.astype(jnp.float32)
    row = lax.broadcasted_iota(jnp.int32, (rows, rows), 0)
    same = row == lax.broadcasted_iota(jnp.int32, (rows, rows), 1)
    column = lax.broadcasted_iota(jnp.int32, (rows, LANES), 1)
    spread = jnp.zeros((rows, LANES), jnp.float32)
    for k in range(ids.shape[0]):
        named = jnp.sum(jnp.where(same, ids[k : k + 1, :], 0), axis=1, keepdims=True)
        gate = jnp.sum(jnp.where(same, gates[k : k + 1, :], 0.0), axis=1, keepdims=True)
        spread += jnp.where(column == named, gate, 0.0)
    out_ref[:, width:] = spread.astype(jnp.bfloat16)
    copies[2].wait()


def up_plan(cols):
    step = 512 if cols % 512 == 0 else cols
    count = cols // step
    return step, count, max(1, count - 2)


def down_plan(width, cols, pieces):
    n_tp, n_dp = pieces
    piece = width // (n_tp * n_dp)
    parts = max(1, -(-piece // 512))
    plan = [(jt, jd, part) for jd in reversed(range(n_dp)) for jt in reversed(range(n_tp)) for part in range(parts)]
    step, _, early = up_plan(cols)
    fits = piece // parts == step and width % cols == 0
    slots = max(1, len(plan) - early * (width // cols), 5) if fits else len(plan)
    return piece, piece // parts, plan, min(slots, len(plan))


def own_place(pieces, jt=0, jd=0):
    n_tp, n_dp = pieces
    at_tp = lax.rem(lax.axis_index("tp") + jt, n_tp)
    at_dp = lax.rem(lax.axis_index("dp") + jd, n_dp)
    return at_tp * n_dp + at_dp


def load_kernel(w_up_ref, blocks_ref, done_ref, sem):
    count, _, step = blocks_ref.shape
    copies = [
        pltpu.make_async_copy(w_up_ref.at[:, pl.ds(b * step, step)], blocks_ref.at[b], sem.at[b])
        for b in range(count)
    ]
    for copy in copies:
        copy.start()
    for copy in copies:
        copy.wait()
    done_ref[...] = jnp.zeros_like(done_ref)


def expert_kernel(pieces, n_parts, *refs):
    n_tp, n_dp = pieces
    parts, refs = refs[:n_parts], refs[n_parts:]
    w_up_ref, w_down_ref, w_qkv_ref = refs[1:4]
    outs, refs = refs[4 : 4 + n_dp], refs[4 + n_dp :]
    own_ref, qkv_ref, early_ref, wide, x_ref, hidden, late_ref, slots = refs[:8]
    late_sem, slot_sem, qkv_sem = refs[8:]
    width, cols = w_up_ref.shape
    rows = x_ref.shape[0]
    step, count, early = up_plan(cols)
    piece, part_width, plan, own_slots = down_plan(width, cols, pieces)
    per_block = width // cols

    def fetch_up(b):
        return pltpu.make_async_copy(
            w_up_ref.at[:, pl.ds(b * step, step)], late_ref.at[b - early], late_sem.at[b - early]
        )

    def slot(at):
        if at < own_slots:
            return slots.at[at]
        block, part = divmod(at - own_slots, per_block)
        return early_ref.at[block, pl.ds(part * cols, cols), :]

    def fetch_down(at):
        jt, jd, part = plan[at]
        start = pl.multiple_of(own_place(pieces, jt, jd) * piece + part * part_width, LANES)
        return pltpu.make_async_copy(w_down_ref.at[:, pl.ds(start, part_width)], slot(at), slot_sem.at[at])

    fetch_qkv = pltpu.make_async_copy(w_qkv_ref, qkv_ref, qkv_sem)
    for b in range(early, count):
        fetch_up(b).start()
    for at in range(own_slots):
        fetch_down(at).start()

    each = parts[0].shape[0]
    per_dp = n_parts // n_dp
    if n_parts == 1:
        wide[...] = parts[0][...].astype(jnp.float32)
    for i, part in enumerate(parts if n_parts > 1 else ()):
        shift_dp, flip_ep = divmod(i, per_dp)
        from_ep = lax.axis_index("ep") ^ flip_ep
        from_dp = lax.rem(lax.axis_index("dp") + n_dp - shift_dp, n_dp)
        at = pl.multiple_of((from_ep * n_dp + from_dp) * each, each)
        wide[pl.ds(at, each), :] = part[...].astype(jnp.float32)
    x_ref[...] = wide[...].astype(jnp.bfloat16)
    share = own_ref.shape[0]
    own_ref[...] = wide[
        pl.ds(pl.multiple_of(lax.axis_index("ep") * share, share), share),
        pl.ds(pl.multiple_of(own_place(pieces) * piece, LANES), piece),
    ]

    following = own_slots
    for b in range(count):
        if b >= early:
            fetch_up(b).wait()
        block = early_ref[b] if b < early else late_ref[b - early]
        up = jnp.dot(x_ref[:, :width], block, preferred_element_type=jnp.float32)
        hidden[:, b * step : (b + 1) * step] = (up / (1.0 + jnp.exp(-up))).astype(jnp.bfloat16)
        while following < len(plan) and (following - own_slots) // per_block <= b:
            fetch_down(following).start()
            following += 1
    fetch_qkv.start()

    mine = expert_index(cols)
    column = lax.broadcasted_iota(jnp.int32, (rows, LANES), 1)
    gate = jnp.sum(
        jnp.where(column == mine, x_ref[:, width:].astype(jnp.float32), 0.0), axis=1, keepdims=True
    )
    for at, (jt, jd, part) in enumerate(plan):
        fetch_down(at).wait()
        value = jnp.dot(hidden[...], slot(at)[...], preferred_element_type=jnp.float32) * gate
        outs[jd][jt, :, part * part_width : (part + 1) * part_width] = value.astype(jnp.bfloat16)
    fetch_qkv.wait()


def split_kernel(pieces, *refs):
    n_tp, n_dp = pieces
    parts, (keep_ref, *sends) = refs[:n_dp], refs[n_dp:]
    share = keep_ref.shape[0]
    n_ep = parts[0].shape[1] // share
    targets = [(jt, e) for jt in reversed(range(n_tp)) for e in reversed(range(n_ep))]
    for jt, e in targets:
        at = pl.ds(pl.multiple_of((lax.axis_index("ep") ^ e) * share, share), share)
        total = parts[0][jt, at, :].astype(jnp.float32)
        for part in parts[1:]:
            total = total + part[jt, at, :].astype(jnp.float32)
        if (jt, e) == (0, 0):
            keep_ref[...] = total
        else:
            sends[targets.index((jt, e))][...] = total.astype(jnp.bfloat16)


def feature_kernel(keep_ref, own_ref, gain_ref, *refs):
    received, out_ref = refs[:-1], refs[-1]
    piece = out_ref.shape[1]
    total = keep_ref[...]
    for part in received:
        total = total + part[...].astype(jnp.float32)
    at = pl.ds(pl.multiple_of(lax.axis_index("dp") * piece, piece), piece)
    out_ref[...] = ((total + own_ref[...]) * gain_ref[:, at]).astype(jnp.bfloat16)


def project_kernel(pieces, n_blocks, *refs):
    n_tp, n_dp = pieces
    xs, refs = refs[: n_dp * n_blocks], refs[n_dp * n_blocks :]
    gain_ref, w_ref, keep_ref, square_ref = refs[:4]
    sends, (total_ref, x_ref) = refs[4 : 4 + n_tp - 1], refs[-2:]
    share, piece = xs[0].shape
    cols = w_ref.shape[1]
    total = None
    square = None
    for j in range(n_dp):
        for e in range(n_blocks):
            source = lax.axis_index("ep") ^ e if n_blocks > 1 else 0
            x_ref[j, pl.ds(pl.multiple_of(source * share, share), share), :] = xs[j * n_blocks + e][...]
        at = lax.rem(lax.axis_index("dp") + n_dp - j, n_dp)
        rows = pl.ds(pl.multiple_of(at * piece, piece), piece)
        x = x_ref[j]
        term = jnp.dot(x, w_ref[rows, :], preferred_element_type=jnp.float32)
        plain = x.astype(jnp.float32) / gain_ref[:, rows]
        part = jnp.sum(plain * plain, axis=1, keepdims=True)
        total = term if total is None else total + term
        square = part if square is None else square + part
    high = square.astype(jnp.bfloat16).astype(jnp.float32)
    middle = (square - high).astype(jnp.bfloat16).astype(jnp.float32)
    low = square - high - middle
    lane = lax.broadcasted_iota(jnp.int32, (square.shape[0], LANES), 1)
    tail = jnp.where(lane == 0, high, jnp.where(lane == 1, middle, jnp.where(lane == 2, low, 0.0)))
    total_ref[:, :cols] = total
    total_ref[:, cols:] = tail
    share = keep_ref.shape[0]
    tp_index = lax.axis_index("tp")
    mine = pl.ds(pl.multiple_of(tp_index * share, share), share)
    keep_ref[...] = total_ref[mine, :cols]
    square_ref[...] = total_ref[mine, cols:]
    for j, send_ref in enumerate(sends):
        theirs = lax.rem(tp_index + j + 1, n_tp)
        send_ref[...] = total_ref[pl.ds(pl.multiple_of(theirs * share, share), share), :].astype(jnp.bfloat16)


def shift(x, axis, by):
    size = lax.axis_size(axis)
    return lax.ppermute(x, axis, [(i, (i + by) % size) for i in range(size)])


def flip(x, axis, bits):
    size = lax.axis_size(axis)
    return lax.ppermute(x, axis, [(i, i ^ bits) for i in range(size)])


def send(x, bits, by):
    n_ep, n_tp = lax.axis_size("ep"), lax.axis_size("tp")
    pairs = [
        (e * n_tp + t, (e ^ bits) * n_tp + (t + by) % n_tp) for e in range(n_ep) for t in range(n_tp)
    ]
    return lax.ppermute(x, ("ep", "tp"), pairs)


VMEM = pl.BlockSpec(memory_space=pltpu.VMEM)
ANY = pl.BlockSpec(memory_space=pl.ANY)
SCOPED = 33


def params(mib):
    return pltpu.CompilerParams(vmem_limit_bytes=mib * MIB)


def body(tokens, norm_gain, expert_ids, route_weight, w_up, w_down, w_qkv):
    n_ep, n_tp, n_dp = (lax.axis_size(a) for a in ("ep", "tp", "dp"))
    rows_here, width = tokens.shape
    cols = w_up.shape[1]
    pieces = (n_tp, n_dp)
    rows = rows_here * n_ep * n_dp
    step, count, early = up_plan(cols)
    piece, part_width, plan, own_slots = down_plan(width, cols, pieces)

    packed = pl.pallas_call(
        pack_kernel,
        out_shape=jax.ShapeDtypeStruct((rows_here, width + LANES), jnp.bfloat16),
        in_specs=[ANY, ANY, ANY],
        out_specs=VMEM,
        scratch_shapes=[
            pltpu.VMEM(expert_ids.shape[::-1], jnp.int32),
            pltpu.VMEM(expert_ids.shape[::-1], jnp.float32),
            pltpu.SemaphoreType.DMA((3,)),
        ],
        compiler_params=params(SCOPED),
    )(tokens, expert_ids.T, route_weight.T)
    blocks, done = pl.pallas_call(
        load_kernel,
        out_shape=(
            pltpu.VMEM((early, width, step), jnp.bfloat16),
            jax.ShapeDtypeStruct((8, LANES), jnp.float32),
        ),
        in_specs=[ANY],
        out_specs=(VMEM, VMEM),
        scratch_shapes=[pltpu.SemaphoreType.DMA((early,))],
        compiler_params=params(SCOPED),
        cost_estimate=pl.CostEstimate(flops=0, transcendentals=0, bytes_accessed=2 * early * width * step),
    )(w_up)
    blocks = pltpu.with_memory_space_constraint(blocks, pltpu.VMEM)

    if n_ep <= 4:
        parts = {0: packed}
        for bits in reversed(range(1, n_ep)):
            parts[bits] = flip(packed, "ep", bits)
        parts = [parts[bits] for bits in range(n_ep)]
        parts = [lax.optimization_barrier((part, done))[0] for part in parts]
        parts = parts + [shift(part, "dp", j) for j in range(1, n_dp) for part in parts]
    else:
        parts = [lax.all_gather(packed, ("ep", "dp"), axis=0, tiled=True)]

    late = max(1, count - early)
    share = rows_here * n_dp
    results = pl.pallas_call(
        functools.partial(expert_kernel, pieces, len(parts)),
        out_shape=(
            *(pltpu.VMEM((n_tp, rows, piece), jnp.bfloat16) for _ in range(n_dp)),
            pltpu.VMEM((share, piece), jnp.float32),
            pltpu.VMEM(w_qkv.shape, jnp.bfloat16),
            pltpu.VMEM(blocks.shape, jnp.bfloat16),
        ),
        in_specs=[VMEM] * (len(parts) + 1) + [ANY] * 3,
        out_specs=tuple(VMEM for _ in range(n_dp + 3)),
        scratch_shapes=[
            pltpu.VMEM((rows, width + LANES), jnp.float32),
            pltpu.VMEM((rows, width + LANES), jnp.bfloat16),
            pltpu.VMEM((rows, cols), jnp.bfloat16),
            pltpu.VMEM((late, width, step), jnp.bfloat16),
            pltpu.VMEM((own_slots, cols, part_width), jnp.bfloat16),
            pltpu.SemaphoreType.DMA((late,)),
            pltpu.SemaphoreType.DMA((len(plan),)),
            pltpu.SemaphoreType.DMA,
        ],
        input_output_aliases={len(parts): n_dp + 2},
        compiler_params=params(SCOPED),
        cost_estimate=pl.CostEstimate(
            flops=4 * rows * cols * width, transcendentals=rows * cols, bytes_accessed=2 * cols * width
        ),
    )(*parts, blocks, w_up, w_down, w_qkv)
    outs, own, qkv_weights = results[:n_dp], results[n_dp], results[n_dp + 1]

    cores = [outs[0]] + [shift(outs[j], "dp", j) for j in range(1, n_dp)]
    if n_ep <= 4:
        targets = [(jt, e) for jt in reversed(range(n_tp)) for e in reversed(range(n_ep))][:-1]
        keep, *sends = pl.pallas_call(
            functools.partial(split_kernel, pieces),
            out_shape=(
                jax.ShapeDtypeStruct((share, piece), jnp.float32),
                *(jax.ShapeDtypeStruct((share, piece), jnp.bfloat16) for _ in targets),
            ),
            in_specs=[VMEM] * n_dp,
            out_specs=tuple(VMEM for _ in range(len(targets) + 1)),
            compiler_params=params(4),
        )(*cores)
        received = [send(x, e, jt) for x, (jt, e) in zip(sends, targets)]
    else:
        total = sum(core.astype(jnp.float32) for core in cores)
        here = total[0]
        for j in range(1, n_tp):
            here = here + shift(total[j].astype(jnp.bfloat16), "tp", j).astype(jnp.float32)
        keep = lax.psum_scatter(here, "ep", scatter_dimension=0, tiled=True)
        received = []
    gain = norm_gain[None, :]
    scaled = pl.pallas_call(
        feature_kernel,
        out_shape=jax.ShapeDtypeStruct((share, piece), jnp.bfloat16),
        in_specs=[VMEM] * (3 + len(received)),
        out_specs=VMEM,
        compiler_params=params(4),
    )(keep, own, gain, *received)
    if n_ep <= 4:
        features = {0: scaled}
        for bits in reversed(range(1, n_ep)):
            features[bits] = flip(scaled, "ep", bits)
        features = [features[bits] for bits in range(n_ep)]
    else:
        features = [lax.all_gather(scaled, "ep", axis=0, tiled=True)]
    n_blocks = len(features)
    features = features + [shift(x, "dp", j) for j in range(1, n_dp) for x in features]
    out_cols = w_qkv.shape[1]
    share = rows // n_tp
    projected = pl.pallas_call(
        functools.partial(project_kernel, pieces, n_blocks),
        out_shape=(
            jax.ShapeDtypeStruct((share, out_cols), jnp.float32),
            jax.ShapeDtypeStruct((share, LANES), jnp.float32),
            *(jax.ShapeDtypeStruct((share, out_cols + LANES), jnp.bfloat16) for _ in range(n_tp - 1)),
        ),
        in_specs=[VMEM] * (len(features) + 2),
        out_specs=tuple(VMEM for _ in range(n_tp + 1)),
        scratch_shapes=[
            pltpu.VMEM((rows, out_cols + LANES), jnp.float32),
            pltpu.VMEM((n_dp, rows, piece), jnp.bfloat16),
        ],
        compiler_params=params(16),
    )(*features, gain, pltpu.with_memory_space_constraint(qkv_weights, pltpu.VMEM))
    total, squares = projected[0], projected[1]
    for j in range(1, n_tp):
        received = shift(projected[1 + j], "tp", j).astype(jnp.float32)
        total = total + received[:, :out_cols]
        squares = squares + received[:, out_cols:]
    scale = lax.rsqrt(jnp.sum(squares[:, :3], axis=1, keepdims=True) / width + EPSILON)
    return (total * scale).astype(jnp.bfloat16)


def solution(mesh):
    return jax.shard_map(
        body,
        mesh=mesh,
        in_specs=(
            P(("group", "ep", "dp"), None),
            P("tp"),
            P(("group", "ep", "dp"), None),
            P(("group", "ep", "dp"), None),
            P(None, ("ep", "tp", "dp")),
            P(("ep", "tp", "dp"), None),
            P("tp", ("ep", "dp")),
        ),
        out_specs=P(("group", "tp"), ("ep", "dp")),
        check_vma=False,
    )
```

time: 81.1 us -> 77.5 us (0.956)
  waiting for transfers between devices: 25.8 us -> 12.7 us
  starting transfers between devices: 14.2 us -> 25.3 us
  other arithmetic: 3.05 us -> 0.82 us
    ppermute x0 -> x7, starting transfers between devices: none -> 11.5 us  [send(): return lax.ppermute(x, ('ep', 'tp'), pairs)]
    ppermute x5 -> x6, waiting for transfers between devices: 13.9 us -> 2.85 us  [flip(): return lax.ppermute(x, axis, [(i, i ^ bits) for i in range(size)])]
    ppermute x8 -> x10, waiting for transfers between devices: 11.9 us -> 5.79 us  [shift(): return lax.ppermute(x, axis, [(i, (i + by) % size) for i in range(size)])]
    ppermute x0 -> x7, waiting for transfers between devices: none -> 4.04 us  [send(): return lax.ppermute(x, ('ep', 'tp'), pairs)]
    convert_element_type x3 -> x0, other arithmetic: 2.13 us -> none  [the longest x1 1.32 us: body(): scaled = (mixed * gain[None, :]).astype(jnp.bfloat16)]
    ppermute x8 -> x10, starting transfers between devices: 4.88 us -> 3.52 us  [shift(): return lax.ppermute(x, axis, [(i, (i + by) % size) for i in range(size)])]
    ppermute x5 -> x6, starting transfers between devices: 9.29 us -> 10.2 us  [flip(): return lax.ppermute(x, axis, [(i, i ^ bits) for i in range(size)])]
    unnamed x28 -> x24, local copies, waits for them, and re-layouts: 2.89 us -> 2.89 us
  transfers between devices with their start and end apart: 13 -> 23, of which waited for: 10 -> 13; matrix products, arithmetic and copies ran while one was open for 0% -> 0% of each run, Pallas kernels for 11% -> 11%
where the time goes in v3:
time: 77.5 us; the launch traced here: 77.3 us
  Pallas kernels  35.5 us (46%)
  starting transfers between devices  25.3 us (33%)
  waiting for transfers between devices  12.7 us (16%)
  local copies, waits for them, and re-layouts  2.89 us (4%)
  other arithmetic  0.82 us (1%)
    pallas_call x1, Pallas kernels, body(): pl.pallas_call(functools.partial(expert_kernel, pieces, len(parts)), out_...  25.5 us
    ppermute x7, starting transfers between devices, send(): return lax.ppermute(x, ('ep', 'tp'), pairs)  11.5 us
    ppermute x6, starting transfers between devices, flip(): return lax.ppermute(x, axis, [(i, i ^ bits) for i in range(size)])  10.2 us
    pallas_call x1, Pallas kernels, body(): pl.pallas_call(load_kernel, out_shape=(pltpu.VMEM((early, width, step), j...  8.86 us
    ppermute x10, waiting for transfers between devices, shift(): return lax.ppermute(x, axis, [(i, (i + by) % size) for i in range(size)])  5.79 us
    ppermute x7, waiting for transfers between devices, send(): return lax.ppermute(x, ('ep', 'tp'), pairs)  4.04 us
    ppermute x10, starting transfers between devices, shift(): return lax.ppermute(x, axis, [(i, (i + by) % size) for i in range(size)])  3.52 us
    unnamed x24, local copies, waits for them, and re-layouts  2.89 us
  transfers between devices with their start and end apart: 23, of which 13 were waited for; matrix products, arithmetic and copies ran while one was open for 0% of the time, Pallas kernels for 11%

profile of v3, /device:TPU:0, one launch (start us, length us, event | category | flops | bytes accessed | tf_op | source)
XLA Modules:
  0.0 77.3 jit_solution(11981396158362391331)
XLA Ops:
  0.0 0.9 %copy-done.1 = bf16[8,6144]{1,0:T(8,128)(2,1)S(1)} copy-done((bf16[8,6144]{1,0:T(8,128)(2,1)S(1)}, bf16[8,6144]{1,0:T(8,128)(2,1)}, u32[]{:S(2)}) %copy-start.1) | copy-done | bytes 98328
  0.9 0.7 copy-done.3
  1.6 0.7 copy-done.4
  2.5 5.1 %collective-permute-start.2 = (bf16[8,6272]{1,0:T(8,128)(2,1)S(1)}, bf16[8,6272]{1,0:T(8,128)(2,1)S(1)}, u32[]{:S(2)}, u32[]{:S(2)}) collective-permute-start(bf16[8,6272]{1,0:T(8,128)(2,1)S(1)} %shard_map.73.refs_0_), channel_id=1, source_target_pairs={{0,12},{4,8},{8,4},{12,0},{1,13},{5,9},{9,5},{13,1},{2,14},{6,10},... | collective-permute-start | bytes 301064 | tf_op jit(solution)/shard_map/ppermute | solution.py:233
  7.6 0.6 collective-permute-start
  8.3 8.9 %shard_map.74 = (bf16[4,6144,512]{2,1,0:T(8,128)(2,1)S(1)}, f32[8,128]{1,0:T(8,128)}) custom-call(bf16[6144,3072]{1,0:T(8,128)(2,1)} %refs_9_.1), custom_call_target="tpu_custom_call" | custom-call | bytes 25165824 | tf_op jit(solution)/shard_map/pallas_call | solution.py:274
  17.3 0.5 collective-permute-start.4
  19.9 25.5 %shard_map.75 = (bf16[2,64,1536]{2,1,0:T(8,128)(2,1)S(1)}, bf16[2,64,1536]{2,1,0:T(8,128)(2,1)S(1)}, f32[16,1536]{1,0:T(8,128)S(1)}, bf16[3072,512]{1,0:T(8,128)(2,1)S(1)}, bf16[4,6144,512]{2,1,0:T(8,128)(2,1)S(1)}) custom-call(bf16[8,6272]{1,0:T(8,128)(2,1)} %copy-done, bf16[8,6272]{1,0:T(8,128)(2,1)} %copy-done.7, ...), custom_call_target="tpu_custom_call", output_to_operand_aliasing={{4}: (8, {})} | custom-call | flops 4831838208 | bytes 37748736 | tf_op jit(solution)/shard_map/pallas_call | solution.py:300
  45.9 1.4 %collective-permute-done.7.refs_1_ = bf16[2,64,1536]{2,1,0:T(8,128)(2,1)S(1)} collective-permute-done((bf16[2,64,1536]{2,1,0:T(8,128)(2,1)S(1)}, bf16[2,64,1536]{2,1,0:T(8,128)(2,1)S(1)}, u32[]{:S(2)}, u32[]{:S(2)}) %collective-permute-start.7) | collective-permute-done | bytes 393248 | tf_op jit(solution)/shard_map/ppermute | solution.py:228
  47.3 4.8 %collective-permute-start.8 = (bf16[16,1536]{1,0:T(8,128)(2,1)S(1)}, bf16[16,1536]{1,0:T(8,128)(2,1)S(1)}, u32[]{:S(2)}, u32[]{:S(2)}) collective-permute-start(bf16[16,1536]{1,0:T(8,128)(2,1)S(1)} %get-tuple-element.36), channel_id=1, source_target_pairs={{0,14},{2,12},{4,10},{6,8},{8,6},{10,4},{12,2},{14,0},{1,15},{3,13... | collective-permute-start | bytes 147464 | tf_op jit(solution)/shard_map/ppermute | solution.py:241
  52.1 1.7 %collective-permute-start.10 = (bf16[16,1536]{1,0:T(8,128)(2,1)S(1)}, bf16[16,1536]{1,0:T(8,128)(2,1)S(1)}, u32[]{:S(2)}, u32[]{:S(2)}) collective-permute-start(bf16[16,1536]{1,0:T(8,128)(2,1)S(1)} %get-tuple-element.38), channel_id=1, source_target_pairs={{0,6},{2,4},{4,2},{6,0},{8,14},{10,12},{12,10},{14,8},{1,7},{3,5},... | collective-permute-start | bytes 147464 | tf_op jit(solution)/shard_map/ppermute | solution.py:241
  54.2 3.7 %collective-permute-start.12 = (bf16[16,1536]{1,0:T(8,128)(2,1)S(1)}, bf16[16,1536]{1,0:T(8,128)(2,1)S(1)}, u32[]{:S(2)}, u32[]{:S(2)}) collective-permute-start(bf16[16,1536]{1,0:T(8,128)(2,1)S(1)} %get-tuple-element.40), channel_id=1, source_target_pairs={{0,12},{2,14},{4,8},{6,10},{8,4},{10,6},{12,0},{14,2},{1,13},{3,15... | collective-permute-start | bytes 147464 | tf_op jit(solution)/shard_map/ppermute | solution.py:241
  58.2 0.9 %collective-permute-start.14 = (bf16[16,1536]{1,0:T(8,128)(2,1)S(1)}, bf16[16,1536]{1,0:T(8,128)(2,1)S(1)}, u32[]{:S(2)}, u32[]{:S(2)}) collective-permute-start(bf16[16,1536]{1,0:T(8,128)(2,1)S(1)} %get-tuple-element.42), channel_id=1, source_target_pairs={{0,4},{2,6},{4,0},{6,2},{8,12},{10,14},{12,8},{14,10},{1,5},{3,7},... | collective-permute-start | bytes 147464 | tf_op jit(solution)/shard_map/ppermute | solution.py:241
  59.2 1.4 %collective-permute-done.12.refs_4_ = bf16[16,1536]{1,0:T(8,128)(2,1)S(1)} collective-permute-done((bf16[16,1536]{1,0:T(8,128)(2,1)S(1)}, bf16[16,1536]{1,0:T(8,128)(2,1)S(1)}, u32[]{:S(2)}, u32[]{:S(2)}) %collective-permute-start.12) | collective-permute-done | bytes 49184 | tf_op jit(solution)/shard_map/ppermute | solution.py:241
  60.6 2.3 %collective-permute-done.13.refs_5_ = bf16[16,1536]{1,0:T(8,128)(2,1)S(1)} collective-permute-done((bf16[16,1536]{1,0:T(8,128)(2,1)S(1)}, bf16[16,1536]{1,0:T(8,128)(2,1)S(1)}, u32[]{:S(2)}, u32[]{:S(2)}) %collective-permute-start.13) | collective-permute-done | bytes 49184 | tf_op jit(solution)/shard_map/ppermute | solution.py:241
  63.0 1.8 %collective-permute-start.17 = (bf16[16,1536]{1,0:T(8,128)(2,1)S(1)}, bf16[16,1536]{1,0:T(8,128)(2,1)S(1)}, u32[]{:S(2)}, u32[]{:S(2)}) collective-permute-start(bf16[16,1536]{1,0:T(8,128)(2,1)S(1)} %shard_map.77.refs_0_), channel_id=1, source_target_pairs={{0,12},{4,8},{8,4},{12,0},{1,13},{5,9},{9,5},{13,1},{2,14},{6,10},... | collective-permute-start | bytes 147464 | tf_op jit(solution)/shard_map/ppermute | solution.py:233
  65.2 2.3 %collective-permute-start.15 = (bf16[16,1536]{1,0:T(8,128)(2,1)S(1)}, bf16[16,1536]{1,0:T(8,128)(2,1)S(1)}, u32[]{:S(2)}, u32[]{:S(2)}) collective-permute-start(bf16[16,1536]{1,0:T(8,128)(2,1)S(1)} %shard_map.77.refs_0_), channel_id=1, source_target_pairs={{0,4},{4,0},{8,12},{12,8},{1,5},{5,1},{9,13},{13,9},{2,6},{6,2},{1... | collective-permute-start | bytes 147464 | tf_op jit(solution)/shard_map/ppermute | solution.py:233
  67.4 1.5 %collective-permute-done.17.refs_3_ = bf16[16,1536]{1,0:T(8,128)(2,1)S(1)} collective-permute-done((bf16[16,1536]{1,0:T(8,128)(2,1)S(1)}, bf16[16,1536]{1,0:T(8,128)(2,1)S(1)}, u32[]{:S(2)}, u32[]{:S(2)}) %collective-permute-start.17) | collective-permute-done | bytes 49184 | tf_op jit(solution)/shard_map/ppermute | solution.py:233
  68.9 1.3 %collective-permute-done.16.refs_2_ = bf16[16,1536]{1,0:T(8,128)(2,1)S(1)} collective-permute-done((bf16[16,1536]{1,0:T(8,128)(2,1)S(1)}, bf16[16,1536]{1,0:T(8,128)(2,1)S(1)}, u32[]{:S(2)}, u32[]{:S(2)}) %collective-permute-start.16) | collective-permute-done | bytes 49184 | tf_op jit(solution)/shard_map/ppermute | solution.py:233
  70.8 0.7 collective-permute-done.20.refs_6_
  71.7 0.7 shard_map.78
  72.4 1.5 %collective-permute-start.22 = (bf16[32,640]{1,0:T(8,128)(2,1)S(1)}, bf16[32,640]{1,0:T(8,128)(2,1)S(1)}, u32[]{:S(2)}, u32[]{:S(2)}) collective-permute-start(bf16[32,640]{1,0:T(8,128)(2,1)S(1)} %get-tuple-element.45), channel_id=1, source_target_pairs={{0,2},{2,0},{1,3},{3,1},{4,6},{6,4},{5,7},{7,5},{8,10},{10,8},{9,1... | collective-permute-start | bytes 122888 | tf_op jit(solution)/shard_map/ppermute | solution.py:228
  73.8 2.6 %collective-permute-done.22 = bf16[32,640]{1,0:T(8,128)(2,1)S(1)} collective-permute-done((bf16[32,640]{1,0:T(8,128)(2,1)S(1)}, bf16[32,640]{1,0:T(8,128)(2,1)S(1)}, u32[]{:S(2)}, u32[]{:S(2)}) %collective-permute-start.22) | collective-permute-done | bytes 40992 | tf_op jit(solution)/shard_map/ppermute | solution.py:228
  76.6 0.7 fusion.1
  (57 shorter events, 4.9 us)
Async XLA Ops:
  2.5 14.7 %collective-permute-start.2 = (bf16[8,6272]{1,0:T(8,128)(2,1)S(1)}, bf16[8,6272]{1,0:T(8,128)(2,1)S(1)}, u32[]{:S(2)}, u32[]{:S(2)}) collective-permute-start(bf16[8,6272]{1,0:T(8,128)(2,1)S(1)} %shard_map.73.refs_0_), channel_id=1, source_target_pairs={{0,12},{4,8},{8,4},{12,0},{1,13},{5,9},{9,5},{13,1},{2,14},{6,10},... | collective-permute-start | bytes 301064 | tf_op jit(solution)/shard_map/ppermute | solution.py:233
  7.6 9.6 %collective-permute-start.1 = (bf16[8,6272]{1,0:T(8,128)(2,1)S(1)}, bf16[8,6272]{1,0:T(8,128)(2,1)S(1)}, u32[]{:S(2)}, u32[]{:S(2)}) collective-permute-start(bf16[8,6272]{1,0:T(8,128)(2,1)S(1)} %shard_map.73.refs_0_), channel_id=1, source_target_pairs={{0,8},{4,12},{8,0},{12,4},{1,9},{5,13},{9,1},{13,5},{2,10},{6,14},... | collective-permute-start | bytes 301064 | tf_op jit(solution)/shard_map/ppermute | solution.py:233
  7.6 9.6 %collective-permute-start = (bf16[8,6272]{1,0:T(8,128)(2,1)S(1)}, bf16[8,6272]{1,0:T(8,128)(2,1)S(1)}, u32[]{:S(2)}, u32[]{:S(2)}) collective-permute-start(bf16[8,6272]{1,0:T(8,128)(2,1)S(1)} %shard_map.73.refs_0_), channel_id=1, source_target_pairs={{0,4},{4,0},{8,12},{12,8},{1,5},{5,1},{9,13},{13,9},{2,6},{6,2},{1... | collective-permute-start | bytes 301064 | tf_op jit(solution)/shard_map/ppermute | solution.py:233
  17.1 1.4 %collective-permute-start.3 = (bf16[8,6272]{1,0:T(8,128)(2,1)S(1)}, bf16[8,6272]{1,0:T(8,128)(2,1)S(1)}, u32[]{:S(2)}, u32[]{:S(2)}) collective-permute-start(bf16[8,6272]{1,0:T(8,128)(2,1)S(1)} %shard_map.73.refs_0_), channel_id=1, source_target_pairs={{0,1},{1,0},{2,3},{3,2},{4,5},{5,4},{6,7},{7,6},{8,9},{9,8},{10,11... | collective-permute-start | bytes 301064 | tf_op jit(solution)/shard_map/ppermute | solution.py:228
  17.3 1.5 %collective-permute-start.4 = (bf16[8,6272]{1,0:T(8,128)(2,1)S(1)}, bf16[8,6272]{1,0:T(8,128)(2,1)S(1)}, u32[]{:S(2)}, u32[]{:S(2)}) collective-permute-start(bf16[8,6272]{1,0:T(8,128)(2,1)S(1)} %collective-permute-done.refs_1_), channel_id=1, source_target_pairs={{0,1},{1,0},{2,3},{3,2},{4,5},{5,4},{6,7},{7,6},{8,9},{9,8},{10,11... | collective-permute-start | bytes 301064 | tf_op jit(solution)/shard_map/ppermute | solution.py:228
  17.8 1.3 %collective-permute-start.5 = (bf16[8,6272]{1,0:T(8,128)(2,1)S(1)}, bf16[8,6272]{1,0:T(8,128)(2,1)S(1)}, u32[]{:S(2)}, u32[]{:S(2)}) collective-permute-start(bf16[8,6272]{1,0:T(8,128)(2,1)S(1)} %collective-permute-done.1.refs_2_), channel_id=1, source_target_pairs={{0,1},{1,0},{2,3},{3,2},{4,5},{5,4},{6,7},{7,6},{8,9},{9,8},{10,11... | collective-permute-start | bytes 301064 | tf_op jit(solution)/shard_map/ppermute | solution.py:228
  17.9 1.4 %collective-permute-start.6 = (bf16[8,6272]{1,0:T(8,128)(2,1)S(1)}, bf16[8,6272]{1,0:T(8,128)(2,1)S(1)}, u32[]{:S(2)}, u32[]{:S(2)}) collective-permute-start(bf16[8,6272]{1,0:T(8,128)(2,1)S(1)} %collective-permute-done.2.refs_3_), channel_id=1, source_target_pairs={{0,1},{1,0},{2,3},{3,2},{4,5},{5,4},{6,7},{7,6},{8,9},{9,8},{10,11... | collective-permute-start | bytes 301064 | tf_op jit(solution)/shard_map/ppermute | solution.py:228
  19.9 43.0 %copy-start.2 = (f32[3072]{0:T(1024)S(1)}, f32[3072]{0:T(1024)}, u32[]{:S(2)}) copy-start(f32[3072]{0:T(1024)} %param.8) | copy-start | bytes 36868
  45.5 1.8 %collective-permute-start.7 = (bf16[2,64,1536]{2,1,0:T(8,128)(2,1)S(1)}, bf16[2,64,1536]{2,1,0:T(8,128)(2,1)S(1)}, u32[]{:S(2)}, u32[]{:S(2)}) collective-permute-start(bf16[2,64,1536]{2,1,0:T(8,128)(2,1)S(1)} %get-tuple-element.33), channel_id=1, source_target_pairs={{0,1},{1,0},{2,3},{3,2},{4,5},{5,4},{6,7},{7,6},{8,9},{9,8},{10,11... | collective-permute-start | bytes 1179656 | tf_op jit(solution)/shard_map/ppermute | solution.py:228
  47.3 10.6 %collective-permute-start.8 = (bf16[16,1536]{1,0:T(8,128)(2,1)S(1)}, bf16[16,1536]{1,0:T(8,128)(2,1)S(1)}, u32[]{:S(2)}, u32[]{:S(2)}) collective-permute-start(bf16[16,1536]{1,0:T(8,128)(2,1)S(1)} %get-tuple-element.36), channel_id=1, source_target_pairs={{0,14},{2,12},{4,10},{6,8},{8,6},{10,4},{12,2},{14,0},{1,15},{3,13... | collective-permute-start | bytes 147464 | tf_op jit(solution)/shard_map/ppermute | solution.py:241
  52.1 6.1 %collective-permute-start.9 = (bf16[16,1536]{1,0:T(8,128)(2,1)S(1)}, bf16[16,1536]{1,0:T(8,128)(2,1)S(1)}, u32[]{:S(2)}, u32[]{:S(2)}) collective-permute-start(bf16[16,1536]{1,0:T(8,128)(2,1)S(1)} %get-tuple-element.37), channel_id=1, source_target_pairs={{0,10},{2,8},{4,14},{6,12},{8,2},{10,0},{12,6},{14,4},{1,11},{3,9}... | collective-permute-start | bytes 147464 | tf_op jit(solution)/shard_map/ppermute | solution.py:241
  52.1 7.1 %collective-permute-start.10 = (bf16[16,1536]{1,0:T(8,128)(2,1)S(1)}, bf16[16,1536]{1,0:T(8,128)(2,1)S(1)}, u32[]{:S(2)}, u32[]{:S(2)}) collective-permute-start(bf16[16,1536]{1,0:T(8,128)(2,1)S(1)} %get-tuple-element.38), channel_id=1, source_target_pairs={{0,6},{2,4},{4,2},{6,0},{8,14},{10,12},{12,10},{14,8},{1,7},{3,5},... | collective-permute-start | bytes 147464 | tf_op jit(solution)/shard_map/ppermute | solution.py:241
  53.8 5.4 %collective-permute-start.11 = (bf16[16,1536]{1,0:T(8,128)(2,1)S(1)}, bf16[16,1536]{1,0:T(8,128)(2,1)S(1)}, u32[]{:S(2)}, u32[]{:S(2)}) collective-permute-start(bf16[16,1536]{1,0:T(8,128)(2,1)S(1)} %get-tuple-element.39), channel_id=1, source_target_pairs={{0,2},{2,0},{4,6},{6,4},{8,10},{10,8},{12,14},{14,12},{1,3},{3,1},... | collective-permute-start | bytes 147464 | tf_op jit(solution)/shard_map/ppermute | solution.py:241
  54.2 6.4 %collective-permute-start.12 = (bf16[16,1536]{1,0:T(8,128)(2,1)S(1)}, bf16[16,1536]{1,0:T(8,128)(2,1)S(1)}, u32[]{:S(2)}, u32[]{:S(2)}) collective-permute-start(bf16[16,1536]{1,0:T(8,128)(2,1)S(1)} %get-tuple-element.40), channel_id=1, source_target_pairs={{0,12},{2,14},{4,8},{6,10},{8,4},{10,6},{12,0},{14,2},{1,13},{3,15... | collective-permute-start | bytes 147464 | tf_op jit(solution)/shard_map/ppermute | solution.py:241
  57.9 5.0 %collective-permute-start.13 = (bf16[16,1536]{1,0:T(8,128)(2,1)S(1)}, bf16[16,1536]{1,0:T(8,128)(2,1)S(1)}, u32[]{:S(2)}, u32[]{:S(2)}) collective-permute-start(bf16[16,1536]{1,0:T(8,128)(2,1)S(1)} %get-tuple-element.41), channel_id=1, source_target_pairs={{0,8},{2,10},{4,12},{6,14},{8,0},{10,2},{12,4},{14,6},{1,9},{3,11}... | collective-permute-start | bytes 147464 | tf_op jit(solution)/shard_map/ppermute | solution.py:241
  58.2 4.7 %collective-permute-start.14 = (bf16[16,1536]{1,0:T(8,128)(2,1)S(1)}, bf16[16,1536]{1,0:T(8,128)(2,1)S(1)}, u32[]{:S(2)}, u32[]{:S(2)}) collective-permute-start(bf16[16,1536]{1,0:T(8,128)(2,1)S(1)} %get-tuple-element.42), channel_id=1, source_target_pairs={{0,4},{2,6},{4,0},{6,2},{8,12},{10,14},{12,8},{14,10},{1,5},{3,7},... | collective-permute-start | bytes 147464 | tf_op jit(solution)/shard_map/ppermute | solution.py:241
  63.0 6.0 %collective-permute-start.17 = (bf16[16,1536]{1,0:T(8,128)(2,1)S(1)}, bf16[16,1536]{1,0:T(8,128)(2,1)S(1)}, u32[]{:S(2)}, u32[]{:S(2)}) collective-permute-start(bf16[16,1536]{1,0:T(8,128)(2,1)S(1)} %shard_map.77.refs_0_), channel_id=1, source_target_pairs={{0,12},{4,8},{8,4},{12,0},{1,13},{5,9},{9,5},{13,1},{2,14},{6,10},... | collective-permute-start | bytes 147464 | tf_op jit(solution)/shard_map/ppermute | solution.py:233
  64.8 5.5 %collective-permute-start.16 = (bf16[16,1536]{1,0:T(8,128)(2,1)S(1)}, bf16[16,1536]{1,0:T(8,128)(2,1)S(1)}, u32[]{:S(2)}, u32[]{:S(2)}) collective-permute-start(bf16[16,1536]{1,0:T(8,128)(2,1)S(1)} %shard_map.77.refs_0_), channel_id=1, source_target_pairs={{0,8},{4,12},{8,0},{12,4},{1,9},{5,13},{9,1},{13,5},{2,10},{6,14},... | collective-permute-start | bytes 147464 | tf_op jit(solution)/shard_map/ppermute | solution.py:233
  65.2 5.1 %collective-permute-start.15 = (bf16[16,1536]{1,0:T(8,128)(2,1)S(1)}, bf16[16,1536]{1,0:T(8,128)(2,1)S(1)}, u32[]{:S(2)}, u32[]{:S(2)}) collective-permute-start(bf16[16,1536]{1,0:T(8,128)(2,1)S(1)} %shard_map.77.refs_0_), channel_id=1, source_target_pairs={{0,4},{4,0},{8,12},{12,8},{1,5},{5,1},{9,13},{13,9},{2,6},{6,2},{1... | collective-permute-start | bytes 147464 | tf_op jit(solution)/shard_map/ppermute | solution.py:233
  67.4 3.4 %collective-permute-start.18 = (bf16[16,1536]{1,0:T(8,128)(2,1)S(1)}, bf16[16,1536]{1,0:T(8,128)(2,1)S(1)}, u32[]{:S(2)}, u32[]{:S(2)}) collective-permute-start(bf16[16,1536]{1,0:T(8,128)(2,1)S(1)} %shard_map.77.refs_0_), channel_id=1, source_target_pairs={{0,1},{1,0},{2,3},{3,2},{4,5},{5,4},{6,7},{7,6},{8,9},{9,8},{10,11... | collective-permute-start | bytes 147464 | tf_op jit(solution)/shard_map/ppermute | solution.py:228
  68.9 1.9 %collective-permute-start.21 = (bf16[16,1536]{1,0:T(8,128)(2,1)S(1)}, bf16[16,1536]{1,0:T(8,128)(2,1)S(1)}, u32[]{:S(2)}, u32[]{:S(2)}) collective-permute-start(bf16[16,1536]{1,0:T(8,128)(2,1)S(1)} %collective-permute-done.17.refs_3_), channel_id=1, source_target_pairs={{0,1},{1,0},{2,3},{3,2},{4,5},{5,4},{6,7},{7,6},{8,9},{9,8},{10,11... | collective-permute-start | bytes 147464 | tf_op jit(solution)/shard_map/ppermute | solution.py:228
  70.3 1.2 %collective-permute-start.20 = (bf16[16,1536]{1,0:T(8,128)(2,1)S(1)}, bf16[16,1536]{1,0:T(8,128)(2,1)S(1)}, u32[]{:S(2)}, u32[]{:S(2)}) collective-permute-start(bf16[16,1536]{1,0:T(8,128)(2,1)S(1)} %collective-permute-done.16.refs_2_), channel_id=1, source_target_pairs={{0,1},{1,0},{2,3},{3,2},{4,5},{5,4},{6,7},{7,6},{8,9},{9,8},{10,11... | collective-permute-start | bytes 147464 | tf_op jit(solution)/shard_map/ppermute | solution.py:228
  70.3 1.4 %collective-permute-start.19 = (bf16[16,1536]{1,0:T(8,128)(2,1)S(1)}, bf16[16,1536]{1,0:T(8,128)(2,1)S(1)}, u32[]{:S(2)}, u32[]{:S(2)}) collective-permute-start(bf16[16,1536]{1,0:T(8,128)(2,1)S(1)} %collective-permute-done.15.refs_1_), channel_id=1, source_target_pairs={{0,1},{1,0},{2,3},{3,2},{4,5},{5,4},{6,7},{7,6},{8,9},{9,8},{10,11... | collective-permute-start | bytes 147464 | tf_op jit(solution)/shard_map/ppermute | solution.py:228
  72.4 4.1 %collective-permute-start.22 = (bf16[32,640]{1,0:T(8,128)(2,1)S(1)}, bf16[32,640]{1,0:T(8,128)(2,1)S(1)}, u32[]{:S(2)}, u32[]{:S(2)}) collective-permute-start(bf16[32,640]{1,0:T(8,128)(2,1)S(1)} %get-tuple-element.45), channel_id=1, source_target_pairs={{0,2},{2,0},{1,3},{3,1},{4,6},{6,4},{5,7},{7,5},{8,10},{10,8},{9,1... | collective-permute-start | bytes 122888 | tf_op jit(solution)/shard_map/ppermute | solution.py:228
  (11 other events, 27.9 us)

commit v4 on v3

v4 whole, which is shorter than its diff:
```python
import functools

import jax
import jax.numpy as jnp
from jax import lax
from jax.experimental import pallas as pl
from jax.experimental.pallas import tpu as pltpu
from jax.sharding import PartitionSpec as P

FF = 6144
EXPERTS = 8
EPSILON = 1e-05
LANES = 128
MIB = 1 << 20


def expert_index(col_count):
    place = lax.axis_index("ep") * lax.axis_size("tp") + lax.axis_index("tp")
    place = place * lax.axis_size("dp") + lax.axis_index("dp")
    return place * col_count // FF


def pack_kernel(tokens_ref, ids_ref, weight_ref, out_ref, ids, weight, sem):
    rows, width = tokens_ref.shape
    copies = [
        pltpu.make_async_copy(ids_ref, ids, sem.at[0]),
        pltpu.make_async_copy(weight_ref, weight, sem.at[1]),
        pltpu.make_async_copy(tokens_ref, out_ref.at[:, pl.ds(0, width)], sem.at[2]),
    ]
    for copy in copies:
        copy.start()
    copies[0].wait()
    copies[1].wait()
    gates = (weight[...] / jnp.sum(weight[...], axis=0, keepdims=True)).astype(jnp.bfloat16)
    gates = gates.astype(jnp.float32)
    row = lax.broadcasted_iota(jnp.int32, (rows, rows), 0)
    same = row == lax.broadcasted_iota(jnp.int32, (rows, rows), 1)
    column = lax.broadcasted_iota(jnp.int32, (rows, LANES), 1)
    spread = jnp.zeros((rows, LANES), jnp.float32)
    for k in range(ids.shape[0]):
        named = jnp.sum(jnp.where(same, ids[k : k + 1, :], 0), axis=1, keepdims=True)
        gate = jnp.sum(jnp.where(same, gates[k : k + 1, :], 0.0), axis=1, keepdims=True)
        spread += jnp.where(column == named, gate, 0.0)
    out_ref[:, width:] = spread.astype(jnp.bfloat16)
    copies[2].wait()


def up_plan(cols):
    step = 512 if cols % 512 == 0 else cols
    count = cols // step
    early = max(1, count - 2)
    first = max(1, early - 1)
    return step, [group for group in (range(0, first), range(first, early)) if len(group)], count - early


def down_plan(width, pieces):
    n_tp, n_dp = pieces
    piece = width // (n_tp * n_dp)
    parts = max(1, -(-piece // 512))
    return piece, parts, [(jt, jd) for jt in reversed(range(n_tp)) for jd in reversed(range(n_dp))]


def own_place(pieces, jt=0, jd=0):
    n_tp, n_dp = pieces
    at_tp = lax.rem(lax.axis_index("tp") + jt, n_tp)
    at_dp = lax.rem(lax.axis_index("dp") + jd, n_dp)
    return at_tp * n_dp + at_dp


def load_kernel(group, *refs):
    w_up_ref, (blocks_ref, done_ref, sem) = refs[0], refs[-3:]
    step = blocks_ref.shape[2]
    copies = [
        pltpu.make_async_copy(w_up_ref.at[:, pl.ds(b * step, step)], blocks_ref.at[b], sem.at[b - group[0]])
        for b in group
    ]
    for copy in copies:
        copy.start()
    for copy in copies:
        copy.wait()
    done_ref[...] = jnp.zeros_like(done_ref)


def stack_kernel(*refs):
    for i, part in enumerate(refs[:-1]):
        refs[-1][i] = part[...]


def gather_kernel(pieces, *refs):
    n_dp = pieces[1]
    parts, (x_ref, own_ref, wide) = refs[1:-3], refs[-3:]
    n_blocks, each, _ = parts[0].shape
    for j, part in enumerate(parts):
        from_dp = lax.rem(lax.axis_index("dp") + n_dp - j, n_dp)
        for e in range(n_blocks):
            if n_blocks == 1:
                at = 0
            else:
                at = pl.multiple_of(((lax.axis_index("ep") ^ e) * n_dp + from_dp) * each, each)
            wide[pl.ds(at, each), :] = part[e].astype(jnp.float32)
    x_ref[...] = wide[...].astype(jnp.bfloat16)
    share, piece = own_ref.shape
    own_ref[...] = wide[
        pl.ds(pl.multiple_of(lax.axis_index("ep") * share, share), share),
        pl.ds(pl.multiple_of(own_place(pieces) * piece, LANES), piece),
    ]


def down_copy(pieces, stage, part, w_down_ref, slots, sem):
    width = w_down_ref.shape[1]
    piece, parts, plan = down_plan(width, pieces)
    jt, jd = plan[stage]
    part_width = piece // parts
    start = pl.multiple_of(own_place(pieces, jt, jd) * piece + part * part_width, LANES)
    return pltpu.make_async_copy(w_down_ref.at[:, pl.ds(start, part_width)], slots.at[part], sem.at[part])


def up_kernel(pieces, blocks_ref, x_ref, *refs):
    w_up_ref, w_down_ref, hidden_ref, gate_ref, out_ref, next_ref, late, slots = refs[:8]
    late_sem, slot_sem, next_sem = refs[8:]
    width, cols = w_up_ref.shape
    rows = x_ref.shape[0]
    step, _, n_late = up_plan(cols)
    parts = slots.shape[0]
    early = blocks_ref.shape[0]

    def late_copy(b):
        start = pl.multiple_of((early + b) * step, step)
        return pltpu.make_async_copy(w_up_ref.at[:, pl.ds(start, step)], late.at[b], late_sem.at[b])

    @pl.loop(0, n_late)
    def _(b):
        late_copy(b).start()

    @pl.loop(0, parts)
    def _(part):
        down_copy(pieces, 0, part, w_down_ref, slots, slot_sem).start()

    @pl.loop(0, parts)
    def _(part):
        down_copy(pieces, 1, part, w_down_ref, next_ref, next_sem).start()

    def activate(b, block):
        up = jnp.dot(x_ref[:, :width], block, preferred_element_type=jnp.float32)
        at = pl.multiple_of(b * step, LANES if step % LANES == 0 else step)
        hidden_ref[:, pl.ds(at, step)] = (up / (1.0 + jnp.exp(-up))).astype(jnp.bfloat16)

    @pl.loop(0, early)
    def _(b):
        activate(b, blocks_ref[b])

    @pl.loop(0, n_late)
    def _(b):
        late_copy(b).wait()
        activate(early + b, late[b])

    mine = expert_index(cols)
    column = lax.broadcasted_iota(jnp.int32, (rows, LANES), 1)
    gate = jnp.sum(
        jnp.where(column == mine, x_ref[:, width:].astype(jnp.float32), 0.0), axis=1, keepdims=True
    )
    gate_ref[...] = jnp.broadcast_to(gate, gate_ref.shape)

    @pl.loop(0, parts)
    def _(part):
        down_copy(pieces, 0, part, w_down_ref, slots, slot_sem).wait()
        work_part(part, hidden_ref, gate_ref, slots, out_ref)

    @pl.loop(0, parts)
    def _(part):
        down_copy(pieces, 1, part, w_down_ref, next_ref, next_sem).wait()


def work_part(part, hidden_ref, gate_ref, slots, out_ref):
    part_width = slots.shape[2]
    value = jnp.dot(hidden_ref[...], slots[part], preferred_element_type=jnp.float32) * gate_ref[:, :1]
    at = pl.multiple_of(part * part_width, LANES)
    out_ref[:, pl.ds(at, part_width)] = value.astype(out_ref.dtype)


def down_kernel(pieces, stage, hidden_ref, gate_ref, slots, w_down_ref, out_ref, next_ref, sem):
    parts = slots.shape[0]

    @pl.loop(0, parts)
    def _(part):
        down_copy(pieces, stage + 1, part, w_down_ref, next_ref, sem).start()

    @pl.loop(0, parts)
    def _(part):
        work_part(part, hidden_ref, gate_ref, slots, out_ref)

    @pl.loop(0, parts)
    def _(part):
        down_copy(pieces, stage + 1, part, w_down_ref, next_ref, sem).wait()


def last_down_kernel(pieces, hidden_ref, gate_ref, first_ref, w_down_ref, *refs):
    n_dp = pieces[1]
    outs, (slots, sem) = refs[:n_dp], refs[n_dp:]
    parts = first_ref.shape[0]
    before = len(down_plan(w_down_ref.shape[1], pieces)[2]) - n_dp
    for j in range(1, n_dp):

        @pl.loop(0, parts)
        def _(part, j=j):
            down_copy(pieces, before + j, part, w_down_ref, slots.at[j - 1], sem.at[j - 1]).start()

    @pl.loop(0, parts)
    def _(part):
        work_part(part, hidden_ref, gate_ref, first_ref, outs[0])

    for j in range(1, n_dp):

        @pl.loop(0, parts)
        def _(part, j=j):
            down_copy(pieces, before + j, part, w_down_ref, slots.at[j - 1], sem.at[j - 1]).wait()
            work_part(part, hidden_ref, gate_ref, slots.at[j - 1], outs[j])


def add_kernel(*refs):
    total = refs[0][...].astype(jnp.float32)
    for part in refs[1:-1]:
        total = total + part[...].astype(jnp.float32)
    refs[-1][...] = total.astype(refs[-1].dtype)


def split_kernel(n_in, *refs):
    parts, (keep_ref, *sends) = refs[:n_in], refs[n_in:]
    share = keep_ref.shape[0]
    for e in reversed(range(len(sends) + 1)):
        at = pl.ds(pl.multiple_of((lax.axis_index("ep") ^ e) * share, share), share)
        total = parts[0][at, :].astype(jnp.float32)
        for part in parts[1:]:
            total = total + part[at, :].astype(jnp.float32)
        if e:
            sends[e - 1][...] = total.astype(jnp.bfloat16)
        else:
            keep_ref[...] = total


def feature_kernel(keep_ref, own_ref, gain_ref, *refs):
    received, out_ref = refs[:-1], refs[-1]
    piece = out_ref.shape[1]
    total = keep_ref[...]
    for part in received:
        total = total + part[...].astype(jnp.float32)
    at = pl.ds(pl.multiple_of(lax.axis_index("dp") * piece, piece), piece)
    out_ref[...] = ((total + own_ref[...]) * gain_ref[:, at]).astype(jnp.bfloat16)


def order_kernel(*refs):
    blocks, out_ref = refs[:-1], refs[-1]
    share = blocks[0].shape[0]
    for e, block in enumerate(blocks):
        at = pl.multiple_of((lax.axis_index("ep") ^ e) * share, share)
        out_ref[pl.ds(at, share), :] = block[...]


def project_piece(n_dp, j, x_ref, gain_ref, w_ref):
    piece = x_ref.shape[1]
    at = lax.rem(lax.axis_index("dp") + n_dp - j, n_dp)
    rows = pl.ds(pl.multiple_of(at * piece, piece), piece)
    x = x_ref[...]
    plain = x.astype(jnp.float32) / gain_ref[:, rows]
    product = jnp.dot(x, w_ref[rows, :], preferred_element_type=jnp.float32)
    return product, jnp.sum(plain * plain, axis=1, keepdims=True)


def first_project_kernel(n_dp, x_ref, gain_ref, w_ref, out_ref):
    cols = w_ref.shape[1]
    product, square = project_piece(n_dp, 0, x_ref, gain_ref, w_ref)
    out_ref[:, :cols] = product
    out_ref[:, cols:] = jnp.broadcast_to(square, (square.shape[0], LANES))


def project_kernel(pieces, *refs):
    n_tp, n_dp = pieces
    others, refs = refs[: n_dp - 1], refs[n_dp - 1 :]
    first_ref, gain_ref, w_ref, keep_ref, square_ref = refs[:5]
    sends, total_ref = refs[5:-1], refs[-1]
    cols = w_ref.shape[1]
    total = first_ref[:, :cols]
    square = first_ref[:, cols : cols + 1]
    for j, x_ref in enumerate(others):
        term, part = project_piece(n_dp, j + 1, x_ref, gain_ref, w_ref)
        total = total + term
        square = square + part
    high = square.astype(jnp.bfloat16).astype(jnp.float32)
    middle = (square - high).astype(jnp.bfloat16).astype(jnp.float32)
    low = square - high - middle
    lane = lax.broadcasted_iota(jnp.int32, (square.shape[0], LANES), 1)
    tail = jnp.where(lane == 0, high, jnp.where(lane == 1, middle, jnp.where(lane == 2, low, 0.0)))
    total_ref[:, :cols] = total
    total_ref[:, cols:] = tail
    share = keep_ref.shape[0]
    tp_index = lax.axis_index("tp")
    mine = pl.ds(pl.multiple_of(tp_index * share, share), share)
    keep_ref[...] = total_ref[mine, :cols]
    square_ref[...] = total_ref[mine, cols:]
    for j, send_ref in enumerate(sends):
        theirs = lax.rem(tp_index + j + 1, n_tp)
        send_ref[...] = total_ref[pl.ds(pl.multiple_of(theirs * share, share), share), :].astype(jnp.bfloat16)


def shift(x, axis, by):
    size = lax.axis_size(axis)
    return lax.ppermute(x, axis, [(i, (i + by) % size) for i in range(size)])


def flip(x, axis, bits):
    size = lax.axis_size(axis)
    return lax.ppermute(x, axis, [(i, i ^ bits) for i in range(size)])


VMEM = pl.BlockSpec(memory_space=pltpu.VMEM)
ANY = pl.BlockSpec(memory_space=pl.ANY)
SCOPED = 24
SHARE = 1000


def params(mib):
    return pltpu.CompilerParams(vmem_limit_bytes=mib * MIB)


def cost(flops, bytes_accessed):
    return pl.CostEstimate(flops=flops // SHARE, transcendentals=0, bytes_accessed=bytes_accessed // SHARE)


def in_vmem(x):
    return pltpu.with_memory_space_constraint(x, pltpu.VMEM)


def body(tokens, norm_gain, expert_ids, route_weight, w_up, w_down, w_qkv):
    n_ep, n_tp, n_dp = (lax.axis_size(a) for a in ("ep", "tp", "dp"))
    rows_here, width = tokens.shape
    cols = w_up.shape[1]
    pieces = (n_tp, n_dp)
    rows = rows_here * n_ep * n_dp
    share = rows_here * n_dp
    step, groups, n_late = up_plan(cols)
    piece, n_parts, plan = down_plan(width, pieces)
    part_width = piece // n_parts
    direct = n_ep <= 4

    packed = pl.pallas_call(
        pack_kernel,
        out_shape=jax.ShapeDtypeStruct((rows_here, width + LANES), jnp.bfloat16),
        in_specs=[ANY, ANY, ANY],
        out_specs=VMEM,
        scratch_shapes=[
            pltpu.VMEM(expert_ids.shape[::-1], jnp.int32),
            pltpu.VMEM(expert_ids.shape[::-1], jnp.float32),
            pltpu.SemaphoreType.DMA((3,)),
        ],
        compiler_params=params(2),
    )(*(pltpu.with_memory_space_constraint(x, pltpu.HBM) for x in (tokens, expert_ids.T, route_weight.T)))

    def following(x, after):
        return lax.optimization_barrier((x, after))[0]

    early = sum(len(group) for group in groups)

    def load(group, after, *blocks):
        weights = following(w_up, after)
        return pl.pallas_call(
            functools.partial(load_kernel, group),
            out_shape=(
                pltpu.VMEM((early, width, step), jnp.bfloat16),
                jax.ShapeDtypeStruct((8, LANES), jnp.float32),
            ),
            in_specs=[ANY] + [VMEM] * len(blocks),
            out_specs=(VMEM, VMEM),
            scratch_shapes=[pltpu.SemaphoreType.DMA((len(group),))],
            input_output_aliases={1: 0} if blocks else {},
            compiler_params=params(SCOPED),
            cost_estimate=cost(0, 2 * len(group) * width * step),
        )(weights, *(in_vmem(block) for block in blocks))

    blocks, done = load(groups[0], packed)
    if direct:
        parts = [packed] + [None] * (n_ep - 1)
        for bits in reversed(range(1, n_ep)):
            parts[bits] = flip(packed, "ep", bits)
        parts = [following(part, done) for part in parts]
        stacked = pl.pallas_call(
            stack_kernel,
            out_shape=jax.ShapeDtypeStruct((n_ep, rows_here, width + LANES), jnp.bfloat16),
            in_specs=[VMEM] * n_ep,
            out_specs=VMEM,
            compiler_params=params(4),
        )(*parts)
        if len(groups) > 1:
            blocks, done = load(groups[1], stacked, blocks)
        parts = [stacked] + [following(shift(stacked, "dp", j), done) for j in range(1, n_dp)]
    else:
        for group in groups[1:]:
            blocks, done = load(group, done, blocks)
        parts = [lax.all_gather(packed, ("ep", "dp"), axis=0, tiled=True)[None]]

    x, own = pl.pallas_call(
        functools.partial(gather_kernel, pieces),
        out_shape=(
            pltpu.VMEM((rows, width + LANES), jnp.bfloat16),
            jax.ShapeDtypeStruct((share, piece), jnp.float32),
        ),
        in_specs=[VMEM] * (len(parts) + 1),
        out_specs=(VMEM, VMEM),
        scratch_shapes=[pltpu.VMEM((rows, width + LANES), jnp.float32)],
        compiler_params=params(SCOPED),
    )(in_vmem(blocks), *parts)

    units = pltpu.VMEM((n_parts, cols, part_width), jnp.bfloat16)
    hidden, gate, out, slots = pl.pallas_call(
        functools.partial(up_kernel, pieces),
        out_shape=(
            pltpu.VMEM((rows, cols), jnp.bfloat16),
            pltpu.VMEM((rows, LANES), jnp.float32),
            pltpu.VMEM((rows, piece), jnp.bfloat16),
            units,
        ),
        in_specs=[VMEM] * 2 + [ANY] * 2,
        out_specs=(VMEM,) * 4,
        scratch_shapes=[
            pltpu.VMEM((max(1, n_late), width, step), jnp.bfloat16),
            units,
            pltpu.SemaphoreType.DMA((max(1, n_late),)),
            pltpu.SemaphoreType.DMA((n_parts,)),
            pltpu.SemaphoreType.DMA((n_parts,)),
        ],
        compiler_params=params(SCOPED),
        cost_estimate=cost(2 * rows * cols * (width + piece), 24 * MIB),
    )(in_vmem(blocks), in_vmem(x), w_up, w_down)

    received = []
    gathering = [shift(out, "dp", plan[0][1])] if plan[0][1] else []
    after = out
    shared = dict(compiler_params=params(12), cost_estimate=cost(2 * rows * cols * piece, 2 * cols * piece))
    for stage in range(1, len(plan) - n_dp):
        jt, jd = plan[stage]
        out, slots = pl.pallas_call(
            functools.partial(down_kernel, pieces, stage),
            out_shape=(pltpu.VMEM((rows, piece), jnp.bfloat16 if jd else jnp.float32), units),
            in_specs=[VMEM] * 3 + [ANY],
            out_specs=(VMEM,) * 2,
            scratch_shapes=[pltpu.SemaphoreType.DMA((n_parts,))],
            **shared,
        )(in_vmem(hidden), in_vmem(gate), in_vmem(slots), following(w_down, after))
        if jd:
            gathering.append(shift(out, "dp", jd))
        else:
            after = pl.pallas_call(
                add_kernel,
                out_shape=jax.ShapeDtypeStruct((rows, piece), jnp.bfloat16),
                in_specs=[VMEM] * (1 + len(gathering)),
                out_specs=VMEM,
                compiler_params=params(4),
            )(out, *gathering)
            received.append(shift(after, "tp", jt))
            gathering = []
    *outs, out = pl.pallas_call(
        functools.partial(last_down_kernel, pieces),
        out_shape=tuple(
            pltpu.VMEM((rows, piece), jnp.bfloat16 if jd else jnp.float32) for jd in reversed(range(n_dp))
        ),
        in_specs=[VMEM] * 3 + [ANY],
        out_specs=(VMEM,) * n_dp,
        scratch_shapes=[
            pltpu.VMEM((max(1, n_dp - 1), n_parts, cols, part_width), jnp.bfloat16),
            pltpu.SemaphoreType.DMA((max(1, n_dp - 1), n_parts)),
        ],
        **shared,
    )(in_vmem(hidden), in_vmem(gate), in_vmem(slots), following(w_down, after))
    gathering = [shift(x, "dp", plan[len(plan) - n_dp + j][1]) for j, x in enumerate(outs)]
    kept = pl.pallas_call(
        add_kernel,
        out_shape=jax.ShapeDtypeStruct((rows, piece), jnp.float32),
        in_specs=[VMEM] * (1 + len(received)),
        out_specs=VMEM,
        compiler_params=params(4),
    )(out, *received)
    arrived = [kept, *gathering]
    if direct:
        keep, *sends = pl.pallas_call(
            functools.partial(split_kernel, len(arrived)),
            out_shape=(
                jax.ShapeDtypeStruct((share, piece), jnp.float32),
                *(jax.ShapeDtypeStruct((share, piece), jnp.bfloat16) for _ in range(n_ep - 1)),
            ),
            in_specs=[VMEM] * len(arrived),
            out_specs=(VMEM,) * n_ep,
            compiler_params=params(4),
        )(*arrived)
        received = [flip(sends[bits - 1], "ep", bits) for bits in reversed(range(1, n_ep))]
    else:
        total = sum(x.astype(jnp.float32) for x in arrived)
        keep = lax.psum_scatter(total, "ep", scatter_dimension=0, tiled=True)
        received = []
    gain = norm_gain[None, :]
    scaled = pl.pallas_call(
        feature_kernel,
        out_shape=jax.ShapeDtypeStruct((share, piece), jnp.bfloat16),
        in_specs=[VMEM] * (3 + len(received)),
        out_specs=VMEM,
        compiler_params=params(4),
    )(keep, own, gain, *received)
    if direct:
        blocks = [scaled] + [None] * (n_ep - 1)
        for bits in reversed(range(1, n_ep)):
            blocks[bits] = flip(scaled, "ep", bits)
        mine = pl.pallas_call(
            order_kernel,
            out_shape=jax.ShapeDtypeStruct((rows, piece), jnp.bfloat16),
            in_specs=[VMEM] * n_ep,
            out_specs=VMEM,
            compiler_params=params(4),
        )(*blocks)
    else:
        mine = lax.all_gather(scaled, "ep", axis=0, tiled=True)
    others = [shift(mine, "dp", j) for j in range(1, n_dp)]
    out_cols = w_qkv.shape[1]
    share = rows // n_tp
    first = pl.pallas_call(
        functools.partial(first_project_kernel, n_dp),
        out_shape=jax.ShapeDtypeStruct((rows, out_cols + LANES), jnp.float32),
        in_specs=[VMEM] * 3,
        out_specs=VMEM,
        compiler_params=params(12),
    )(mine, gain, w_qkv)
    projected = pl.pallas_call(
        functools.partial(project_kernel, pieces),
        out_shape=(
            jax.ShapeDtypeStruct((share, out_cols), jnp.float32),
            jax.ShapeDtypeStruct((share, LANES), jnp.float32),
            *(jax.ShapeDtypeStruct((share, out_cols + LANES), jnp.bfloat16) for _ in range(n_tp - 1)),
        ),
        in_specs=[VMEM] * (n_dp + 2),
        out_specs=tuple(VMEM for _ in range(n_tp + 1)),
        scratch_shapes=[pltpu.VMEM((rows, out_cols + LANES), jnp.float32)],
        compiler_params=params(12),
    )(*others, first, gain, w_qkv)
    total, squares = projected[0], projected[1]
    for j in range(1, n_tp):
        received = shift(projected[1 + j], "tp", j).astype(jnp.float32)
        total = total + received[:, :out_cols]
        squares = squares + received[:, out_cols:]
    scale = lax.rsqrt(jnp.sum(squares[:, :3], axis=1, keepdims=True) / width + EPSILON)
    return (total * scale).astype(jnp.bfloat16)


def solution(mesh):
    return jax.shard_map(
        body,
        mesh=mesh,
        in_specs=(
            P(("group", "ep", "dp"), None),
            P("tp"),
            P(("group", "ep", "dp"), None),
            P(("group", "ep", "dp"), None),
            P(None, ("ep", "tp", "dp")),
            P(("ep", "tp", "dp"), None),
            P("tp", ("ep", "dp")),
        ),
        out_specs=P(("group", "tp"), ("ep", "dp")),
        check_vma=False,
    )
```

time: 77.5 us -> 63.5 us (0.82)
  starting transfers between devices: 25.3 us -> 17.9 us
  Pallas kernels: 35.5 us -> 31.3 us
  local copies, waits for them, and re-layouts: 2.89 us -> 0.02 us
    ppermute x7 -> x0, starting transfers between devices: 11.5 us -> none  [send(): return lax.ppermute(x, ('ep', 'tp'), pairs)]
    pallas_call x4 -> x13, Pallas kernels: 35.2 us -> 30.3 us  [the longest x2 10.6 us: load(): pl.pallas_call(functools.partial(load_kernel, group), out_shape=(pltpu.VM...]
    ppermute x6 -> x9, waiting for transfers between devices: 2.85 us -> 7.59 us  [flip(): return lax.ppermute(x, axis, [(i, i ^ bits) for i in range(size)])]
    ppermute x6 -> x9, starting transfers between devices: 10.2 us -> 14.7 us  [flip(): return lax.ppermute(x, axis, [(i, i ^ bits) for i in range(size)])]
    ppermute x7 -> x0, waiting for transfers between devices: 4.04 us -> none  [send(): return lax.ppermute(x, ('ep', 'tp'), pairs)]
    unnamed x24 -> x4, local copies, waits for them, and re-layouts: 2.89 us -> 0.01 us
    ppermute x10 -> x6, starting transfers between devices: 3.52 us -> 3.26 us  [shift(): return lax.ppermute(x, axis, [(i, (i + by) % size) for i in range(size)])]
    ppermute x10 -> x6, waiting for transfers between devices: 5.79 us -> 5.54 us  [shift(): return lax.ppermute(x, axis, [(i, (i + by) % size) for i in range(size)])]
  transfers between devices with their start and end apart: 23 -> 15, of which waited for: 13 -> 10; matrix products, arithmetic and copies ran while one was open for 0% -> 0% of each run, Pallas kernels for 11% -> 31%
where the time goes in v4:
time: 63.5 us; the launch traced here: 63.3 us
  Pallas kernels  31.3 us (49%)
  starting transfers between devices  17.9 us (28%)
  waiting for transfers between devices  13.1 us (21%)
  other arithmetic  0.82 us (1%)
    ppermute x9, starting transfers between devices, flip(): return lax.ppermute(x, axis, [(i, i ^ bits) for i in range(size)])  14.7 us
    pallas_call x2, Pallas kernels, load(): pl.pallas_call(functools.partial(load_kernel, group), out_shape=(pltpu.VM...  10.6 us
    pallas_call x1, Pallas kernels, body(): pl.pallas_call(functools.partial(up_kernel, pieces), out_shape=(pltpu.VME...  10.2 us
    ppermute x9, waiting for transfers between devices, flip(): return lax.ppermute(x, axis, [(i, i ^ bits) for i in range(size)])  7.59 us
    ppermute x6, waiting for transfers between devices, shift(): return lax.ppermute(x, axis, [(i, (i + by) % size) for i in range(size)])  5.54 us
    pallas_call x1, Pallas kernels, body(): pl.pallas_call(functools.partial(last_down_kernel, pieces), out_shape=tup...  4.47 us
    pallas_call x1, Pallas kernels, body(): pl.pallas_call(functools.partial(down_kernel, pieces, stage), out_shape=(...  3.81 us
    ppermute x6, starting transfers between devices, shift(): return lax.ppermute(x, axis, [(i, (i + by) % size) for i in range(size)])  3.26 us
  transfers between devices with their start and end apart: 15, of which 10 were waited for; matrix products, arithmetic and copies ran while one was open for 0% of the time, Pallas kernels for 31%

profile of v4, /device:TPU:0, one launch (start us, length us, event | category | flops | bytes accessed | tf_op | source)
XLA Modules:
  0.0 63.3 jit_solution(13933015551901048641)
XLA Ops:
  0.0 0.9 %shard_map.73.refs_0_ = bf16[8,6272]{1,0:T(8,128)(2,1)S(1)} custom-call(bf16[8,6144]{1,0:T(8,128)(2,1)} %tokens_ref.1, s32[4,8]{1,0:T(4,128)} %bitcast.6, f32[4,8]{1,0:T(4,128)} %bitcast.7), custom_call_target="tpu_custom_call" | custom-call | tf_op jit(solution)/shard_map/pallas_call | solution.py:345
  1.0 5.1 %collective-permute-start.2 = (bf16[8,6272]{1,0:T(8,128)(2,1)S(1)}, bf16[8,6272]{1,0:T(8,128)(2,1)S(1)}, u32[]{:S(2)}, u32[]{:S(2)}) collective-permute-start(bf16[8,6272]{1,0:T(8,128)(2,1)S(1)} %shard_map.73.refs_0_), channel_id=1, source_target_pairs={{0,12},{4,8},{8,4},{12,0},{1,13},{5,9},{9,5},{13,1},{2,14},{6,10},... | collective-permute-start | bytes 301064 | tf_op jit(solution)/shard_map/ppermute | solution.py:312
  6.1 0.6 %collective-permute-start = (bf16[8,6272]{1,0:T(8,128)(2,1)S(1)}, bf16[8,6272]{1,0:T(8,128)(2,1)S(1)}, u32[]{:S(2)}, u32[]{:S(2)}) collective-permute-start(bf16[8,6272]{1,0:T(8,128)(2,1)S(1)} %shard_map.73.refs_0_), channel_id=1, source_target_pairs={{0,4},{4,0},{8,12},{12,8},{1,5},{5,1},{9,13},{13,9},{2,6},{6,2},{1... | collective-permute-start | bytes 301064 | tf_op jit(solution)/shard_map/ppermute | solution.py:312
  6.7 7.0 %shard_map.74 = (bf16[4,6144,512]{2,1,0:T(8,128)(2,1)S(1)}, f32[8,128]{1,0:T(8,128)}) custom-call(bf16[6144,3072]{1,0:T(8,128)(2,1)} %refs_0_.3), custom_call_target="tpu_custom_call" | custom-call | bytes 18874 | tf_op jit(solution)/shard_map/pallas_call | solution.py:365
  13.8 0.7 %collective-permute-done.1.refs_2_ = bf16[8,6272]{1,0:T(8,128)(2,1)S(1)} collective-permute-done((bf16[8,6272]{1,0:T(8,128)(2,1)S(1)}, bf16[8,6272]{1,0:T(8,128)(2,1)S(1)}, u32[]{:S(2)}, u32[]{:S(2)}) %collective-permute-start.1) | collective-permute-done | bytes 100384 | tf_op jit(solution)/shard_map/ppermute | solution.py:312
  14.6 3.6 %shard_map.76 = (bf16[4,6144,512]{2,1,0:T(8,128)(2,1)S(1)}, f32[8,128]{1,0:T(8,128)}) custom-call(bf16[6144,3072]{1,0:T(8,128)(2,1)} %refs_0_.3, bf16[4,6144,512]{2,1,0:T(8,128)(2,1)S(1)} %get-tuple-element.40.refs_1_), custom_call_target="tpu_custom_call", output_to_operand_aliasing={{0}: (1, {})} | custom-call | bytes 6291 | tf_op jit(solution)/shard_map/pallas_call | solution.py:365
  18.4 10.2 %shard_map.78 = (bf16[64,3072]{1,0:T(8,128)(2,1)S(1)}, f32[64,128]{1,0:T(8,128)S(1)}, bf16[64,1536]{1,0:T(8,128)(2,1)S(1)}, bf16[3,3072,512]{2,1,0:T(8,128)(2,1)S(1)}) custom-call(bf16[4,6144,512]{2,1,0:T(8,128)(2,1)S(1)} %get-tuple-element.41.refs_0_.blocks_ref, bf16[64,6272]{1,0:T(8,128)(2,1)S(1)} %get-tuple-element.42.x_ref, bf16[6144,3072]{1,0:T(8,128)(2,1)} %refs_0_.3, ...), custom_call_target="tpu_custom_call" | custom-call | flops 3019898 | bytes 25165 | tf_op jit(solution)/shard_map/pallas_call | solution.py:413
  29.2 3.8 %shard_map.79 = (f32[64,1536]{1,0:T(8,128)S(1)}, bf16[3,3072,512]{2,1,0:T(8,128)(2,1)S(1)}) custom-call(bf16[64,3072]{1,0:T(8,128)(2,1)S(1)} %get-tuple-element.43.hidden_ref, f32[64,128]{1,0:T(8,128)S(1)} %get-tuple-element.44.gate_ref, bf16[3,3072,512]{2,1,0:T(8,128)(2,1)S(1)} %get-tuple-element.45.slots, bf16[3072,6144]{1,0:T(8,128)(2,1)} %w_down_ref.1), custom_call_target="tpu_custom_call" | custom-call | flops 603979 | bytes 9437 | tf_op jit(solution)/shard_map/pallas_call | solution.py:440
  33.1 1.6 %collective-permute-start.5 = (bf16[64,1536]{1,0:T(8,128)(2,1)S(1)}, bf16[64,1536]{1,0:T(8,128)(2,1)S(1)}, u32[]{:S(2)}, u32[]{:S(2)}) collective-permute-start(bf16[64,1536]{1,0:T(8,128)(2,1)S(1)} %shard_map.80), channel_id=1, source_target_pairs={{0,2},{2,0},{1,3},{3,1},{4,6},{6,4},{5,7},{7,5},{8,10},{10,8},{9,1... | collective-permute-start | bytes 589832 | tf_op jit(solution)/shard_map/ppermute | solution.py:307
  34.6 4.5 %shard_map.81 = (bf16[64,1536]{1,0:T(8,128)(2,1)S(1)}, f32[64,1536]{1,0:T(8,128)S(1)}) custom-call(bf16[64,3072]{1,0:T(8,128)(2,1)S(1)} %get-tuple-element.43.hidden_ref, f32[64,128]{1,0:T(8,128)S(1)} %get-tuple-element.44.gate_ref, bf16[3,3072,512]{2,1,0:T(8,128)(2,1)S(1)} %get-tuple-element.48.first_ref, bf16[3072,6144]{1,0:T(8,128)(2,1)} %w_down_ref.1), custom_call_target="tpu_custom_call" | custom-call | flops 603979 | bytes 9437 | tf_op jit(solution)/shard_map/pallas_call | solution.py:460
  39.2 0.8 %collective-permute-done.5.refs_1_ = bf16[64,1536]{1,0:T(8,128)(2,1)S(1)} collective-permute-done((bf16[64,1536]{1,0:T(8,128)(2,1)S(1)}, bf16[64,1536]{1,0:T(8,128)(2,1)S(1)}, u32[]{:S(2)}, u32[]{:S(2)}) %collective-permute-start.5) | collective-permute-done | bytes 196640 | tf_op jit(solution)/shard_map/ppermute | solution.py:307
  40.0 0.6 collective-permute-done.6.refs_1_
  40.7 3.1 %collective-permute-start.7 = (bf16[16,1536]{1,0:T(8,128)(2,1)S(1)}, bf16[16,1536]{1,0:T(8,128)(2,1)S(1)}, u32[]{:S(2)}, u32[]{:S(2)}) collective-permute-start(bf16[16,1536]{1,0:T(8,128)(2,1)S(1)} %get-tuple-element.55), channel_id=1, source_target_pairs={{0,12},{4,8},{8,4},{12,0},{1,13},{5,9},{9,5},{13,1},{2,14},{6,10},... | collective-permute-start | bytes 147464 | tf_op jit(solution)/shard_map/ppermute | solution.py:312
  43.8 1.4 %collective-permute-start.9 = (bf16[16,1536]{1,0:T(8,128)(2,1)S(1)}, bf16[16,1536]{1,0:T(8,128)(2,1)S(1)}, u32[]{:S(2)}, u32[]{:S(2)}) collective-permute-start(bf16[16,1536]{1,0:T(8,128)(2,1)S(1)} %get-tuple-element.57), channel_id=1, source_target_pairs={{0,4},{4,0},{8,12},{12,8},{1,5},{5,1},{9,13},{13,9},{2,6},{6,2},{1... | collective-permute-start | bytes 147464 | tf_op jit(solution)/shard_map/ppermute | solution.py:312
  45.1 1.8 %collective-permute-done.7.refs_0_ = bf16[16,1536]{1,0:T(8,128)(2,1)S(1)} collective-permute-done((bf16[16,1536]{1,0:T(8,128)(2,1)S(1)}, bf16[16,1536]{1,0:T(8,128)(2,1)S(1)}, u32[]{:S(2)}, u32[]{:S(2)}) %collective-permute-start.7) | collective-permute-done | bytes 49184 | tf_op jit(solution)/shard_map/ppermute | solution.py:312
  46.9 1.9 %collective-permute-done.8.refs_1_ = bf16[16,1536]{1,0:T(8,128)(2,1)S(1)} collective-permute-done((bf16[16,1536]{1,0:T(8,128)(2,1)S(1)}, bf16[16,1536]{1,0:T(8,128)(2,1)S(1)}, u32[]{:S(2)}, u32[]{:S(2)}) %collective-permute-start.8) | collective-permute-done | bytes 49184 | tf_op jit(solution)/shard_map/ppermute | solution.py:312
  48.9 2.2 %collective-permute-start.12 = (bf16[16,1536]{1,0:T(8,128)(2,1)S(1)}, bf16[16,1536]{1,0:T(8,128)(2,1)S(1)}, u32[]{:S(2)}, u32[]{:S(2)}) collective-permute-start(bf16[16,1536]{1,0:T(8,128)(2,1)S(1)} %shard_map.84.refs_0_), channel_id=1, source_target_pairs={{0,12},{4,8},{8,4},{12,0},{1,13},{5,9},{9,5},{13,1},{2,14},{6,10},... | collective-permute-start | bytes 147464 | tf_op jit(solution)/shard_map/ppermute | solution.py:312
  51.3 2.1 %collective-permute-start.10 = (bf16[16,1536]{1,0:T(8,128)(2,1)S(1)}, bf16[16,1536]{1,0:T(8,128)(2,1)S(1)}, u32[]{:S(2)}, u32[]{:S(2)}) collective-permute-start(bf16[16,1536]{1,0:T(8,128)(2,1)S(1)} %shard_map.84.refs_0_), channel_id=1, source_target_pairs={{0,4},{4,0},{8,12},{12,8},{1,5},{5,1},{9,13},{13,9},{2,6},{6,2},{1... | collective-permute-start | bytes 147464 | tf_op jit(solution)/shard_map/ppermute | solution.py:312
  53.4 1.9 %collective-permute-done.12.refs_3_ = bf16[16,1536]{1,0:T(8,128)(2,1)S(1)} collective-permute-done((bf16[16,1536]{1,0:T(8,128)(2,1)S(1)}, bf16[16,1536]{1,0:T(8,128)(2,1)S(1)}, u32[]{:S(2)}, u32[]{:S(2)}) %collective-permute-start.12) | collective-permute-done | bytes 49184 | tf_op jit(solution)/shard_map/ppermute | solution.py:312
  55.2 1.2 %collective-permute-done.11.refs_2_ = bf16[16,1536]{1,0:T(8,128)(2,1)S(1)} collective-permute-done((bf16[16,1536]{1,0:T(8,128)(2,1)S(1)}, bf16[16,1536]{1,0:T(8,128)(2,1)S(1)}, u32[]{:S(2)}, u32[]{:S(2)}) %collective-permute-start.11) | collective-permute-done | bytes 49184 | tf_op jit(solution)/shard_map/ppermute | solution.py:312
  57.0 1.0 %collective-permute-done.13.refs_0_ = bf16[64,1536]{1,0:T(8,128)(2,1)S(1)} collective-permute-done((bf16[64,1536]{1,0:T(8,128)(2,1)S(1)}, bf16[64,1536]{1,0:T(8,128)(2,1)S(1)}, u32[]{:S(2)}, u32[]{:S(2)}) %collective-permute-start.13) | collective-permute-done | bytes 196640 | tf_op jit(solution)/shard_map/ppermute | solution.py:307
  58.4 0.9 %collective-permute-start.14 = (bf16[32,640]{1,0:T(8,128)(2,1)S(1)}, bf16[32,640]{1,0:T(8,128)(2,1)S(1)}, u32[]{:S(2)}, u32[]{:S(2)}) collective-permute-start(bf16[32,640]{1,0:T(8,128)(2,1)S(1)} %get-tuple-element.59), channel_id=1, source_target_pairs={{0,2},{2,0},{1,3},{3,1},{4,6},{6,4},{5,7},{7,5},{8,10},{10,8},{9,1... | collective-permute-start | bytes 122888 | tf_op jit(solution)/shard_map/ppermute | solution.py:307
  59.4 3.1 %collective-permute-done.14 = bf16[32,640]{1,0:T(8,128)(2,1)S(1)} collective-permute-done((bf16[32,640]{1,0:T(8,128)(2,1)S(1)}, bf16[32,640]{1,0:T(8,128)(2,1)S(1)}, u32[]{:S(2)}, u32[]{:S(2)}) %collective-permute-start.14) | collective-permute-done | bytes 40992 | tf_op jit(solution)/shard_map/ppermute | solution.py:307
  62.7 0.7 %fusion.1 = bf16[32,512]{1,0:T(8,128)(2,1)} fusion(f32[32,512]{1,0:T(8,128)S(1)} %get-tuple-element.58, f32[32,640]{1,0:T(8,128)S(1)} %convert_element_type.6, f32[32]{0:T(128)S(1)} %add_rsqrt_fusion), kind=kLoop, calls=%fused_computation.2 | loop fusion | flops 49152 | bytes 163968 | tf_op jit(solution)/shard_map/convert_element_type | solution.py:547
  (30 shorter events, 2.3 us)
Async XLA Ops:
  1.0 12.8 %collective-permute-start.2 = (bf16[8,6272]{1,0:T(8,128)(2,1)S(1)}, bf16[8,6272]{1,0:T(8,128)(2,1)S(1)}, u32[]{:S(2)}, u32[]{:S(2)}) collective-permute-start(bf16[8,6272]{1,0:T(8,128)(2,1)S(1)} %shard_map.73.refs_0_), channel_id=1, source_target_pairs={{0,12},{4,8},{8,4},{12,0},{1,13},{5,9},{9,5},{13,1},{2,14},{6,10},... | collective-permute-start | bytes 301064 | tf_op jit(solution)/shard_map/ppermute | solution.py:312
  6.1 8.4 %collective-permute-start.1 = (bf16[8,6272]{1,0:T(8,128)(2,1)S(1)}, bf16[8,6272]{1,0:T(8,128)(2,1)S(1)}, u32[]{:S(2)}, u32[]{:S(2)}) collective-permute-start(bf16[8,6272]{1,0:T(8,128)(2,1)S(1)} %shard_map.73.refs_0_), channel_id=1, source_target_pairs={{0,8},{4,12},{8,0},{12,4},{1,9},{5,13},{9,1},{13,5},{2,10},{6,14},... | collective-permute-start | bytes 301064 | tf_op jit(solution)/shard_map/ppermute | solution.py:312
  6.1 8.4 %collective-permute-start = (bf16[8,6272]{1,0:T(8,128)(2,1)S(1)}, bf16[8,6272]{1,0:T(8,128)(2,1)S(1)}, u32[]{:S(2)}, u32[]{:S(2)}) collective-permute-start(bf16[8,6272]{1,0:T(8,128)(2,1)S(1)} %shard_map.73.refs_0_), channel_id=1, source_target_pairs={{0,4},{4,0},{8,12},{12,8},{1,5},{5,1},{9,13},{13,9},{2,6},{6,2},{1... | collective-permute-start | bytes 301064 | tf_op jit(solution)/shard_map/ppermute | solution.py:312
  14.5 3.7 %collective-permute-start.3 = (bf16[4,8,6272]{2,1,0:T(8,128)(2,1)S(1)}, bf16[4,8,6272]{2,1,0:T(8,128)(2,1)S(1)}, u32[]{:S(2)}, u32[]{:S(2)}) collective-permute-start(bf16[4,8,6272]{2,1,0:T(8,128)(2,1)S(1)} %shard_map.75.refs_1_), channel_id=1, source_target_pairs={{0,1},{1,0},{2,3},{3,2},{4,5},{5,4},{6,7},{7,6},{8,9},{9,8},{10,11... | collective-permute-start | bytes 1204232 | tf_op jit(solution)/shard_map/ppermute | solution.py:307
  28.6 4.4 %collective-permute-start.4 = (bf16[64,1536]{1,0:T(8,128)(2,1)S(1)}, bf16[64,1536]{1,0:T(8,128)(2,1)S(1)}, u32[]{:S(2)}, u32[]{:S(2)}) collective-permute-start(bf16[64,1536]{1,0:T(8,128)(2,1)S(1)} %get-tuple-element.46), channel_id=1, source_target_pairs={{0,1},{1,0},{2,3},{3,2},{4,5},{5,4},{6,7},{7,6},{8,9},{9,8},{10,11... | collective-permute-start | bytes 589832 | tf_op jit(solution)/shard_map/ppermute | solution.py:307
  33.0 15.9 %copy-start.1 = (f32[3072]{0:T(1024)S(1)}, f32[3072]{0:T(1024)}, u32[]{:S(2)}) copy-start(f32[3072]{0:T(1024)} %param.8) | copy-start | bytes 36868
  33.1 23.5 %copy-start = (bf16[3072,512]{1,0:T(8,128)(2,1)S(1)}, bf16[3072,512]{1,0:T(8,128)(2,1)}, u32[]{:S(2)}) copy-start(bf16[3072,512]{1,0:T(8,128)(2,1)} %refs_3_.1) | copy-start | bytes 9437188
  33.1 6.9 %collective-permute-start.5 = (bf16[64,1536]{1,0:T(8,128)(2,1)S(1)}, bf16[64,1536]{1,0:T(8,128)(2,1)S(1)}, u32[]{:S(2)}, u32[]{:S(2)}) collective-permute-start(bf16[64,1536]{1,0:T(8,128)(2,1)S(1)} %shard_map.80), channel_id=1, source_target_pairs={{0,2},{2,0},{1,3},{3,1},{4,6},{6,4},{5,7},{7,5},{8,10},{10,8},{9,1... | collective-permute-start | bytes 589832 | tf_op jit(solution)/shard_map/ppermute | solution.py:307
  39.1 1.5 %collective-permute-start.6 = (bf16[64,1536]{1,0:T(8,128)(2,1)S(1)}, bf16[64,1536]{1,0:T(8,128)(2,1)S(1)}, u32[]{:S(2)}, u32[]{:S(2)}) collective-permute-start(bf16[64,1536]{1,0:T(8,128)(2,1)S(1)} %get-tuple-element.52), channel_id=1, source_target_pairs={{0,1},{1,0},{2,3},{3,2},{4,5},{5,4},{6,7},{7,6},{8,9},{9,8},{10,11... | collective-permute-start | bytes 589832 | tf_op jit(solution)/shard_map/ppermute | solution.py:307
  40.7 6.3 %collective-permute-start.7 = (bf16[16,1536]{1,0:T(8,128)(2,1)S(1)}, bf16[16,1536]{1,0:T(8,128)(2,1)S(1)}, u32[]{:S(2)}, u32[]{:S(2)}) collective-permute-start(bf16[16,1536]{1,0:T(8,128)(2,1)S(1)} %get-tuple-element.55), channel_id=1, source_target_pairs={{0,12},{4,8},{8,4},{12,0},{1,13},{5,9},{9,5},{13,1},{2,14},{6,10},... | collective-permute-start | bytes 147464 | tf_op jit(solution)/shard_map/ppermute | solution.py:312
  43.8 5.0 %collective-permute-start.8 = (bf16[16,1536]{1,0:T(8,128)(2,1)S(1)}, bf16[16,1536]{1,0:T(8,128)(2,1)S(1)}, u32[]{:S(2)}, u32[]{:S(2)}) collective-permute-start(bf16[16,1536]{1,0:T(8,128)(2,1)S(1)} %get-tuple-element.56), channel_id=1, source_target_pairs={{0,8},{4,12},{8,0},{12,4},{1,9},{5,13},{9,1},{13,5},{2,10},{6,14},... | collective-permute-start | bytes 147464 | tf_op jit(solution)/shard_map/ppermute | solution.py:312
  43.8 5.1 %collective-permute-start.9 = (bf16[16,1536]{1,0:T(8,128)(2,1)S(1)}, bf16[16,1536]{1,0:T(8,128)(2,1)S(1)}, u32[]{:S(2)}, u32[]{:S(2)}) collective-permute-start(bf16[16,1536]{1,0:T(8,128)(2,1)S(1)} %get-tuple-element.57), channel_id=1, source_target_pairs={{0,4},{4,0},{8,12},{12,8},{1,5},{5,1},{9,13},{13,9},{2,6},{6,2},{1... | collective-permute-start | bytes 147464 | tf_op jit(solution)/shard_map/ppermute | solution.py:312
  48.9 6.3 %collective-permute-start.12 = (bf16[16,1536]{1,0:T(8,128)(2,1)S(1)}, bf16[16,1536]{1,0:T(8,128)(2,1)S(1)}, u32[]{:S(2)}, u32[]{:S(2)}) collective-permute-start(bf16[16,1536]{1,0:T(8,128)(2,1)S(1)} %shard_map.84.refs_0_), channel_id=1, source_target_pairs={{0,12},{4,8},{8,4},{12,0},{1,13},{5,9},{9,5},{13,1},{2,14},{6,10},... | collective-permute-start | bytes 147464 | tf_op jit(solution)/shard_map/ppermute | solution.py:312
  51.2 5.3 %collective-permute-start.11 = (bf16[16,1536]{1,0:T(8,128)(2,1)S(1)}, bf16[16,1536]{1,0:T(8,128)(2,1)S(1)}, u32[]{:S(2)}, u32[]{:S(2)}) collective-permute-start(bf16[16,1536]{1,0:T(8,128)(2,1)S(1)} %shard_map.84.refs_0_), channel_id=1, source_target_pairs={{0,8},{4,12},{8,0},{12,4},{1,9},{5,13},{9,1},{13,5},{2,10},{6,14},... | collective-permute-start | bytes 147464 | tf_op jit(solution)/shard_map/ppermute | solution.py:312
  51.3 5.2 %collective-permute-start.10 = (bf16[16,1536]{1,0:T(8,128)(2,1)S(1)}, bf16[16,1536]{1,0:T(8,128)(2,1)S(1)}, u32[]{:S(2)}, u32[]{:S(2)}) collective-permute-start(bf16[16,1536]{1,0:T(8,128)(2,1)S(1)} %shard_map.84.refs_0_), channel_id=1, source_target_pairs={{0,4},{4,0},{8,12},{12,8},{1,5},{5,1},{9,13},{13,9},{2,6},{6,2},{1... | collective-permute-start | bytes 147464 | tf_op jit(solution)/shard_map/ppermute | solution.py:312
  56.5 1.5 %collective-permute-start.13 = (bf16[64,1536]{1,0:T(8,128)(2,1)S(1)}, bf16[64,1536]{1,0:T(8,128)(2,1)S(1)}, u32[]{:S(2)}, u32[]{:S(2)}) collective-permute-start(bf16[64,1536]{1,0:T(8,128)(2,1)S(1)} %shard_map.85.x_ref), channel_id=1, source_target_pairs={{0,1},{1,0},{2,3},{3,2},{4,5},{5,4},{6,7},{7,6},{8,9},{9,8},{10,11... | collective-permute-start | bytes 589832 | tf_op jit(solution)/shard_map/ppermute | solution.py:307
  58.4 4.1 %collective-permute-start.14 = (bf16[32,640]{1,0:T(8,128)(2,1)S(1)}, bf16[32,640]{1,0:T(8,128)(2,1)S(1)}, u32[]{:S(2)}, u32[]{:S(2)}) collective-permute-start(bf16[32,640]{1,0:T(8,128)(2,1)S(1)} %get-tuple-element.59), channel_id=1, source_target_pairs={{0,2},{2,0},{1,3},{3,1},{4,6},{6,4},{5,7},{7,5},{8,10},{10,8},{9,1... | collective-permute-start | bytes 122888 | tf_op jit(solution)/shard_map/ppermute | solution.py:307

commit v5 on v4

--- a/solution.py
+++ b/solution.py
@@ -46,11 +46,10 @@
 
 
 def up_plan(cols):
-    step = 512 if cols % 512 == 0 else cols
+    step = 1024 if cols % 1024 == 0 else cols
     count = cols // step
-    early = max(1, count - 2)
-    first = max(1, early - 1)
-    return step, [group for group in (range(0, first), range(first, early)) if len(group)], count - early
+    early = max(1, count - 1)
+    return step, [range(0, early)], count - early
 
 
 def down_plan(width, pieces):
@@ -106,13 +105,12 @@
     ]
 
 
-def down_copy(pieces, stage, part, w_down_ref, slots, sem):
-    width = w_down_ref.shape[1]
-    piece, parts, plan = down_plan(width, pieces)
+def down_copy(pieces, stage, part, w_down_ref, slot, sem):
+    piece, parts, plan = down_plan(w_down_ref.shape[1], pieces)
     jt, jd = plan[stage]
     part_width = piece // parts
     start = pl.multiple_of(own_place(pieces, jt, jd) * piece + part * part_width, LANES)
-    return pltpu.make_async_copy(w_down_ref.at[:, pl.ds(start, part_width)], slots.at[part], sem.at[part])
+    return pltpu.make_async_copy(w_down_ref.at[:, pl.ds(start, part_width)], slot, sem)
 
 
 def up_kernel(pieces, blocks_ref, x_ref, *refs):
@@ -134,11 +132,11 @@
 
     @pl.loop(0, parts)
     def _(part):
-        down_copy(pieces, 0, part, w_down_ref, slots, slot_sem).start()
+        down_copy(pieces, 0, part, w_down_ref, slots.at[part], slot_sem.at[part]).start()
 
     @pl.loop(0, parts)
     def _(part):
-        down_copy(pieces, 1, part, w_down_ref, next_ref, next_sem).start()
+        down_copy(pieces, 1, part, w_down_ref, next_ref.at[part], next_sem.at[part]).start()
 
     def activate(b, block):
         up = jnp.dot(x_ref[:, :width], block, preferred_element_type=jnp.float32)
@@ -163,58 +161,62 @@
 
     @pl.loop(0, parts)
     def _(part):
-        down_copy(pieces, 0, part, w_down_ref, slots, slot_sem).wait()
-        work_part(part, hidden_ref, gate_ref, slots, out_ref)
+        down_copy(pieces, 0, part, w_down_ref, slots.at[part], slot_sem.at[part]).wait()
+        work_part(part, hidden_ref, gate_ref, slots[part], out_ref)
 
     @pl.loop(0, parts)
     def _(part):
-        down_copy(pieces, 1, part, w_down_ref, next_ref, next_sem).wait()
-
-
-def work_part(part, hidden_ref, gate_ref, slots, out_ref):
-    part_width = slots.shape[2]
-    value = jnp.dot(hidden_ref[...], slots[part], preferred_element_type=jnp.float32) * gate_ref[:, :1]
+        down_copy(pieces, 1, part, w_down_ref, next_ref.at[part], next_sem.at[part]).wait()
+
+
+def work_part(part, hidden_ref, gate_ref, block, out_ref):
+    part_width = block.shape[1]
+    value = jnp.dot(hidden_ref[...], block, preferred_element_type=jnp.float32) * gate_ref[:, :1]
     at = pl.multiple_of(part * part_width, LANES)
     out_ref[:, pl.ds(at, part_width)] = value.astype(out_ref.dtype)
 
 
 def down_kernel(pieces, stage, hidden_ref, gate_ref, slots, w_down_ref, out_ref, next_ref, sem):
-    parts = slots.shape[0]
-
-    @pl.loop(0, parts)
-    def _(part):
-        down_copy(pieces, stage + 1, part, w_down_ref, next_ref, sem).start()
-
-    @pl.loop(0, parts)
-    def _(part):
-        work_part(part, hidden_ref, gate_ref, slots, out_ref)
-
-    @pl.loop(0, parts)
-    def _(part):
-        down_copy(pieces, stage + 1, part, w_down_ref, next_ref, sem).wait()
+    @pl.loop(0, next_ref.shape[0])
+    def _(part):
+        down_copy(pieces, stage + 1, part, w_down_ref, next_ref.at[part], sem.at[part]).start()
+
+    @pl.loop(0, slots.shape[0])
+    def _(part):
+        work_part(part, hidden_ref, gate_ref, slots[part], out_ref)
+
+    @pl.loop(0, next_ref.shape[0])
+    def _(part):
+        down_copy(pieces, stage + 1, part, w_down_ref, next_ref.at[part], sem.at[part]).wait()
 
 
 def last_down_kernel(pieces, hidden_ref, gate_ref, first_ref, w_down_ref, *refs):
     n_dp = pieces[1]
     outs, (slots, sem) = refs[:n_dp], refs[n_dp:]
-    parts = first_ref.shape[0]
-    before = len(down_plan(w_down_ref.shape[1], pieces)[2]) - n_dp
-    for j in range(1, n_dp):
-
-        @pl.loop(0, parts)
+    held = first_ref.shape[0]
+    _, parts, plan = down_plan(w_down_ref.shape[1], pieces)
+    before = len(plan) - n_dp
+
+    def copy(j, part):
+        at = j * parts + part - held
+        return down_copy(pieces, before + j, part, w_down_ref, slots.at[at], sem.at[at])
+
+    for j in range(n_dp):
+
+        @pl.loop(held if j == 0 else 0, parts)
         def _(part, j=j):
-            down_copy(pieces, before + j, part, w_down_ref, slots.at[j - 1], sem.at[j - 1]).start()
-
-    @pl.loop(0, parts)
-    def _(part):
-        work_part(part, hidden_ref, gate_ref, first_ref, outs[0])
-
-    for j in range(1, n_dp):
-
-        @pl.loop(0, parts)
+            copy(j, part).start()
+
+    @pl.loop(0, held)
+    def _(part):
+        work_part(part, hidden_ref, gate_ref, first_ref[part], outs[0])
+
+    for j in range(n_dp):
+
+        @pl.loop(held if j == 0 else 0, parts)
         def _(part, j=j):
-            down_copy(pieces, before + j, part, w_down_ref, slots.at[j - 1], sem.at[j - 1]).wait()
-            work_part(part, hidden_ref, gate_ref, slots.at[j - 1], outs[j])
+            copy(j, part).wait()
+            work_part(part, hidden_ref, gate_ref, slots[j * parts + part - held], outs[j])
 
 
 def add_kernel(*refs):
@@ -261,7 +263,7 @@
     at = lax.rem(lax.axis_index("dp") + n_dp - j, n_dp)
     rows = pl.ds(pl.multiple_of(at * piece, piece), piece)
     x = x_ref[...]
-    plain = x.astype(jnp.float32) / gain_ref[:, rows]
+    plain = x.astype(jnp.float32) * (1.0 / gain_ref[:, rows])
     product = jnp.dot(x, w_ref[rows, :], preferred_element_type=jnp.float32)
     return product, jnp.sum(plain * plain, axis=1, keepdims=True)
 
@@ -312,6 +314,10 @@
     return lax.ppermute(x, axis, [(i, i ^ bits) for i in range(size)])
 
 
+def exchange_order(n_ep):
+    return sorted(range(1, n_ep), key=lambda bits: (bits < n_ep // 2, bits))
+
+
 VMEM = pl.BlockSpec(memory_space=pltpu.VMEM)
 ANY = pl.BlockSpec(memory_space=pl.ANY)
 SCOPED = 24
@@ -379,7 +385,7 @@
     blocks, done = load(groups[0], packed)
     if direct:
         parts = [packed] + [None] * (n_ep - 1)
-        for bits in reversed(range(1, n_ep)):
+        for bits in exchange_order(n_ep):
             parts[bits] = flip(packed, "ep", bits)
         parts = [following(part, done) for part in parts]
         stacked = pl.pallas_call(
@@ -434,15 +440,19 @@
     received = []
     gathering = [shift(out, "dp", plan[0][1])] if plan[0][1] else []
     after = out
-    shared = dict(compiler_params=params(12), cost_estimate=cost(2 * rows * cols * piece, 2 * cols * piece))
+    shared = dict(compiler_params=params(14), cost_estimate=cost(2 * rows * cols * piece, 2 * cols * piece))
     for stage in range(1, len(plan) - n_dp):
         jt, jd = plan[stage]
+        loaded = n_parts
         out, slots = pl.pallas_call(
             functools.partial(down_kernel, pieces, stage),
-            out_shape=(pltpu.VMEM((rows, piece), jnp.bfloat16 if jd else jnp.float32), units),
+            out_shape=(
+                pltpu.VMEM((rows, piece), jnp.bfloat16 if jd else jnp.float32),
+                pltpu.VMEM((loaded, cols, part_width), jnp.bfloat16),
+            ),
             in_specs=[VMEM] * 3 + [ANY],
             out_specs=(VMEM,) * 2,
-            scratch_shapes=[pltpu.SemaphoreType.DMA((n_parts,))],
+            scratch_shapes=[pltpu.SemaphoreType.DMA((loaded,))],
             **shared,
         )(in_vmem(hidden), in_vmem(gate), in_vmem(slots), following(w_down, after))
         if jd:
@@ -465,8 +475,8 @@
         in_specs=[VMEM] * 3 + [ANY],
         out_specs=(VMEM,) * n_dp,
         scratch_shapes=[
-            pltpu.VMEM((max(1, n_dp - 1), n_parts, cols, part_width), jnp.bfloat16),
-            pltpu.SemaphoreType.DMA((max(1, n_dp - 1), n_parts)),
+            pltpu.VMEM((n_dp * n_parts - slots.shape[0], cols, part_width), jnp.bfloat16),
+            pltpu.SemaphoreType.DMA((n_dp * n_parts - slots.shape[0],)),
         ],
         **shared,
     )(in_vmem(hidden), in_vmem(gate), in_vmem(slots), following(w_down, after))
@@ -490,7 +500,7 @@
             out_specs=(VMEM,) * n_ep,
             compiler_params=params(4),
         )(*arrived)
-        received = [flip(sends[bits - 1], "ep", bits) for bits in reversed(range(1, n_ep))]
+        received = [flip(sends[bits - 1], "ep", bits) for bits in exchange_order(n_ep)]
     else:
         total = sum(x.astype(jnp.float32) for x in arrived)
         keep = lax.psum_scatter(total, "ep", scatter_dimension=0, tiled=True)
@@ -505,7 +515,7 @@
     )(keep, own, gain, *received)
     if direct:
         blocks = [scaled] + [None] * (n_ep - 1)
-        for bits in reversed(range(1, n_ep)):
+        for bits in exchange_order(n_ep):
             blocks[bits] = flip(scaled, "ep", bits)
         mine = pl.pallas_call(
             order_kernel,

time: 63.5 us -> 62.7 us (0.987)
  Pallas kernels: 31.3 us -> 29.4 us
  waiting for transfers between devices: 13.1 us -> 14.6 us
    pallas_call x2 -> x1, Pallas kernels: 10.6 us -> 8.78 us  [load(): pl.pallas_call(functools.partial(load_kernel, group), out_shape=(pltpu.VM...]
    ppermute x6, waiting for transfers between devices: 5.54 us -> 7.23 us  [shift(): return lax.ppermute(x, axis, [(i, (i + by) % size) for i in range(size)])]
  transfers between devices with their start and end apart: 15 -> 15, of which waited for: 10 -> 9; matrix products, arithmetic and copies ran while one was open for 0% -> 0% of each run, Pallas kernels for 31% -> 28%
where the time goes in v5:
time: 62.7 us; the launch traced here: 62.5 us
  Pallas kernels  29.4 us (47%)
  starting transfers between devices  17.5 us (28%)
  waiting for transfers between devices  14.6 us (23%)
  other arithmetic  0.82 us (1%)
    ppermute x9, starting transfers between devices, flip(): return lax.ppermute(x, axis, [(i, i ^ bits) for i in range(size)])  14.4 us
    pallas_call x1, Pallas kernels, body(): pl.pallas_call(functools.partial(up_kernel, pieces), out_shape=(pltpu.VME...  10.1 us
    pallas_call x1, Pallas kernels, load(): pl.pallas_call(functools.partial(load_kernel, group), out_shape=(pltpu.VM...  8.78 us
    ppermute x9, waiting for transfers between devices, flip(): return lax.ppermute(x, axis, [(i, i ^ bits) for i in range(size)])  7.36 us
    ppermute x6, waiting for transfers between devices, shift(): return lax.ppermute(x, axis, [(i, (i + by) % size) for i in range(size)])  7.23 us
    pallas_call x1, Pallas kernels, body(): pl.pallas_call(functools.partial(last_down_kernel, pieces), out_shape=tup...  4.47 us
    pallas_call x1, Pallas kernels, body(): pl.pallas_call(functools.partial(down_kernel, pieces, stage), out_shape=(...  3.81 us
    ppermute x6, starting transfers between devices, shift(): return lax.ppermute(x, axis, [(i, (i + by) % size) for i in range(size)])  3.09 us
  transfers between devices with their start and end apart: 15, of which 9 were waited for; matrix products, arithmetic and copies ran while one was open for 0% of the time, Pallas kernels for 28%

profile of v5, /device:TPU:0, one launch (start us, length us, event | category | flops | bytes accessed | tf_op | source)
XLA Modules:
  0.0 62.5 jit_solution(13566095101002188616)
XLA Ops:
  0.0 0.9 %shard_map.73.refs_0_ = bf16[8,6272]{1,0:T(8,128)(2,1)S(1)} custom-call(bf16[8,6144]{1,0:T(8,128)(2,1)} %tokens_ref.1, s32[4,8]{1,0:T(4,128)} %bitcast.6, f32[4,8]{1,0:T(4,128)} %bitcast.7), custom_call_target="tpu_custom_call" | custom-call | tf_op jit(solution)/shard_map/pallas_call | solution.py:351
  1.0 5.1 %collective-permute-start.2 = (bf16[8,6272]{1,0:T(8,128)(2,1)S(1)}, bf16[8,6272]{1,0:T(8,128)(2,1)S(1)}, u32[]{:S(2)}, u32[]{:S(2)}) collective-permute-start(bf16[8,6272]{1,0:T(8,128)(2,1)S(1)} %shard_map.73.refs_0_), channel_id=1, source_target_pairs={{0,12},{4,8},{8,4},{12,0},{1,13},{5,9},{9,5},{13,1},{2,14},{6,10},... | collective-permute-start | bytes 301064 | tf_op jit(solution)/shard_map/ppermute | solution.py:314
  6.1 0.6 %collective-permute-start = (bf16[8,6272]{1,0:T(8,128)(2,1)S(1)}, bf16[8,6272]{1,0:T(8,128)(2,1)S(1)}, u32[]{:S(2)}, u32[]{:S(2)}) collective-permute-start(bf16[8,6272]{1,0:T(8,128)(2,1)S(1)} %shard_map.73.refs_0_), channel_id=1, source_target_pairs={{0,4},{4,0},{8,12},{12,8},{1,5},{5,1},{9,13},{13,9},{2,6},{6,2},{1... | collective-permute-start | bytes 301064 | tf_op jit(solution)/shard_map/ppermute | solution.py:314
  6.7 8.8 %shard_map.74 = (bf16[2,6144,1024]{2,1,0:T(8,128)(2,1)S(1)}, f32[8,128]{1,0:T(8,128)}) custom-call(bf16[6144,3072]{1,0:T(8,128)(2,1)} %refs_0_.2), custom_call_target="tpu_custom_call" | custom-call | bytes 25165 | tf_op jit(solution)/shard_map/pallas_call | solution.py:371
  15.7 1.7 %collective-permute-done.3.refs_2_ = bf16[4,8,6272]{2,1,0:T(8,128)(2,1)S(1)} collective-permute-done((bf16[4,8,6272]{2,1,0:T(8,128)(2,1)S(1)}, bf16[4,8,6272]{2,1,0:T(8,128)(2,1)S(1)}, u32[]{:S(2)}, u32[]{:S(2)}) %collective-permute-start.3) | collective-permute-done | bytes 401440 | tf_op jit(solution)/shard_map/ppermute | solution.py:309
  17.6 10.1 %shard_map.77 = (bf16[64,3072]{1,0:T(8,128)(2,1)S(1)}, f32[64,128]{1,0:T(8,128)S(1)}, bf16[64,1536]{1,0:T(8,128)(2,1)S(1)}, bf16[3,3072,512]{2,1,0:T(8,128)(2,1)S(1)}) custom-call(bf16[2,6144,1024]{2,1,0:T(8,128)(2,1)S(1)} %get-tuple-element.33.refs_0_.blocks_ref, bf16[64,6272]{1,0:T(8,128)(2,1)S(1)} %get-tuple-element.40.x_ref, bf16[6144,3072]{1,0:T(8,128)(2,1)} %refs_0_.2, ...), custom_call_target="tpu_custom_call" | custom-call | flops 3019898 | bytes 25165 | tf_op jit(solution)/shard_map/pallas_call | solution.py:419
  27.9 3.8 %shard_map.78 = (f32[64,1536]{1,0:T(8,128)S(1)}, bf16[3,3072,512]{2,1,0:T(8,128)(2,1)S(1)}) custom-call(bf16[64,3072]{1,0:T(8,128)(2,1)S(1)} %get-tuple-element.41.hidden_ref, f32[64,128]{1,0:T(8,128)S(1)} %get-tuple-element.42.gate_ref, bf16[3,3072,512]{2,1,0:T(8,128)(2,1)S(1)} %get-tuple-element.43.slots, bf16[3072,6144]{1,0:T(8,128)(2,1)} %w_down_ref.1), custom_call_target="tpu_custom_call" | custom-call | flops 603979 | bytes 9437 | tf_op jit(solution)/shard_map/pallas_call | solution.py:447
  31.8 1.7 %collective-permute-start.5 = (bf16[64,1536]{1,0:T(8,128)(2,1)S(1)}, bf16[64,1536]{1,0:T(8,128)(2,1)S(1)}, u32[]{:S(2)}, u32[]{:S(2)}) collective-permute-start(bf16[64,1536]{1,0:T(8,128)(2,1)S(1)} %shard_map.79), channel_id=1, source_target_pairs={{0,2},{2,0},{1,3},{3,1},{4,6},{6,4},{5,7},{7,5},{8,10},{10,8},{9,1... | collective-permute-start | bytes 589832 | tf_op jit(solution)/shard_map/ppermute | solution.py:309
  33.5 4.5 %shard_map.80 = (bf16[64,1536]{1,0:T(8,128)(2,1)S(1)}, f32[64,1536]{1,0:T(8,128)S(1)}) custom-call(bf16[64,3072]{1,0:T(8,128)(2,1)S(1)} %get-tuple-element.41.hidden_ref, f32[64,128]{1,0:T(8,128)S(1)} %get-tuple-element.42.gate_ref, bf16[3,3072,512]{2,1,0:T(8,128)(2,1)S(1)} %get-tuple-element.46.first_ref, bf16[3072,6144]{1,0:T(8,128)(2,1)} %w_down_ref.1), custom_call_target="tpu_custom_call" | custom-call | flops 603979 | bytes 9437 | tf_op jit(solution)/shard_map/pallas_call | solution.py:470
  38.2 0.9 %collective-permute-done.5.refs_1_ = bf16[64,1536]{1,0:T(8,128)(2,1)S(1)} collective-permute-done((bf16[64,1536]{1,0:T(8,128)(2,1)S(1)}, bf16[64,1536]{1,0:T(8,128)(2,1)S(1)}, u32[]{:S(2)}, u32[]{:S(2)}) %collective-permute-start.5) | collective-permute-done | bytes 196640 | tf_op jit(solution)/shard_map/ppermute | solution.py:309
  39.6 2.2 %collective-permute-start.7 = (bf16[16,1536]{1,0:T(8,128)(2,1)S(1)}, bf16[16,1536]{1,0:T(8,128)(2,1)S(1)}, u32[]{:S(2)}, u32[]{:S(2)}) collective-permute-start(bf16[16,1536]{1,0:T(8,128)(2,1)S(1)} %get-tuple-element.53), channel_id=1, source_target_pairs={{0,8},{4,12},{8,0},{12,4},{1,9},{5,13},{9,1},{13,5},{2,10},{6,14},... | collective-permute-start | bytes 147464 | tf_op jit(solution)/shard_map/ppermute | solution.py:314
  41.8 1.5 %collective-permute-start.8 = (bf16[16,1536]{1,0:T(8,128)(2,1)S(1)}, bf16[16,1536]{1,0:T(8,128)(2,1)S(1)}, u32[]{:S(2)}, u32[]{:S(2)}) collective-permute-start(bf16[16,1536]{1,0:T(8,128)(2,1)S(1)} %get-tuple-element.54), channel_id=1, source_target_pairs={{0,12},{4,8},{8,4},{12,0},{1,13},{5,9},{9,5},{13,1},{2,14},{6,10},... | collective-permute-start | bytes 147464 | tf_op jit(solution)/shard_map/ppermute | solution.py:314
  43.3 0.5 collective-permute-start.9
  43.8 1.9 %collective-permute-done.7.refs_0_ = bf16[16,1536]{1,0:T(8,128)(2,1)S(1)} collective-permute-done((bf16[16,1536]{1,0:T(8,128)(2,1)S(1)}, bf16[16,1536]{1,0:T(8,128)(2,1)S(1)}, u32[]{:S(2)}, u32[]{:S(2)}) %collective-permute-start.7) | collective-permute-done | bytes 49184 | tf_op jit(solution)/shard_map/ppermute | solution.py:314
  45.7 2.3 %collective-permute-done.8.refs_1_ = bf16[16,1536]{1,0:T(8,128)(2,1)S(1)} collective-permute-done((bf16[16,1536]{1,0:T(8,128)(2,1)S(1)}, bf16[16,1536]{1,0:T(8,128)(2,1)S(1)}, u32[]{:S(2)}, u32[]{:S(2)}) %collective-permute-start.8) | collective-permute-done | bytes 49184 | tf_op jit(solution)/shard_map/ppermute | solution.py:314
  48.0 2.7 %collective-permute-start.12 = (bf16[16,1536]{1,0:T(8,128)(2,1)S(1)}, bf16[16,1536]{1,0:T(8,128)(2,1)S(1)}, u32[]{:S(2)}, u32[]{:S(2)}) collective-permute-start(bf16[16,1536]{1,0:T(8,128)(2,1)S(1)} %shard_map.83.refs_0_), channel_id=1, source_target_pairs={{0,12},{4,8},{8,4},{12,0},{1,13},{5,9},{9,5},{13,1},{2,14},{6,10},... | collective-permute-start | bytes 147464 | tf_op jit(solution)/shard_map/ppermute | solution.py:314
  50.7 1.8 %collective-permute-start.10 = (bf16[16,1536]{1,0:T(8,128)(2,1)S(1)}, bf16[16,1536]{1,0:T(8,128)(2,1)S(1)}, u32[]{:S(2)}, u32[]{:S(2)}) collective-permute-start(bf16[16,1536]{1,0:T(8,128)(2,1)S(1)} %shard_map.83.refs_0_), channel_id=1, source_target_pairs={{0,4},{4,0},{8,12},{12,8},{1,5},{5,1},{9,13},{13,9},{2,6},{6,2},{1... | collective-permute-start | bytes 147464 | tf_op jit(solution)/shard_map/ppermute | solution.py:314
  52.4 1.6 %collective-permute-done.12.refs_3_ = bf16[16,1536]{1,0:T(8,128)(2,1)S(1)} collective-permute-done((bf16[16,1536]{1,0:T(8,128)(2,1)S(1)}, bf16[16,1536]{1,0:T(8,128)(2,1)S(1)}, u32[]{:S(2)}, u32[]{:S(2)}) %collective-permute-start.12) | collective-permute-done | bytes 49184 | tf_op jit(solution)/shard_map/ppermute | solution.py:314
  54.0 1.6 %collective-permute-done.11.refs_2_ = bf16[16,1536]{1,0:T(8,128)(2,1)S(1)} collective-permute-done((bf16[16,1536]{1,0:T(8,128)(2,1)S(1)}, bf16[16,1536]{1,0:T(8,128)(2,1)S(1)}, u32[]{:S(2)}, u32[]{:S(2)}) %collective-permute-start.11) | collective-permute-done | bytes 49184 | tf_op jit(solution)/shard_map/ppermute | solution.py:314
  56.2 1.0 %collective-permute-done.13.refs_0_ = bf16[64,1536]{1,0:T(8,128)(2,1)S(1)} collective-permute-done((bf16[64,1536]{1,0:T(8,128)(2,1)S(1)}, bf16[64,1536]{1,0:T(8,128)(2,1)S(1)}, u32[]{:S(2)}, u32[]{:S(2)}) %collective-permute-start.13) | collective-permute-done | bytes 196640 | tf_op jit(solution)/shard_map/ppermute | solution.py:309
  57.2 0.4 shard_map.86
  57.6 0.9 %collective-permute-start.14 = (bf16[32,640]{1,0:T(8,128)(2,1)S(1)}, bf16[32,640]{1,0:T(8,128)(2,1)S(1)}, u32[]{:S(2)}, u32[]{:S(2)}) collective-permute-start(bf16[32,640]{1,0:T(8,128)(2,1)S(1)} %get-tuple-element.57), channel_id=1, source_target_pairs={{0,2},{2,0},{1,3},{3,1},{4,6},{6,4},{5,7},{7,5},{8,10},{10,8},{9,1... | collective-permute-start | bytes 122888 | tf_op jit(solution)/shard_map/ppermute | solution.py:309
  58.5 3.2 %collective-permute-done.14 = bf16[32,640]{1,0:T(8,128)(2,1)S(1)} collective-permute-done((bf16[32,640]{1,0:T(8,128)(2,1)S(1)}, bf16[32,640]{1,0:T(8,128)(2,1)S(1)}, u32[]{:S(2)}, u32[]{:S(2)}) %collective-permute-start.14) | collective-permute-done | bytes 40992 | tf_op jit(solution)/shard_map/ppermute | solution.py:309
  61.8 0.7 %fusion.1 = bf16[32,512]{1,0:T(8,128)(2,1)} fusion(f32[32,512]{1,0:T(8,128)S(1)} %get-tuple-element.56, f32[32,640]{1,0:T(8,128)S(1)} %convert_element_type.6, f32[32]{0:T(128)S(1)} %add_rsqrt_fusion), kind=kLoop, calls=%fused_computation.2 | loop fusion | flops 49152 | bytes 163968 | tf_op jit(solution)/shard_map/convert_element_type | solution.py:557
  (29 shorter events, 1.9 us)
Async XLA Ops:
  1.0 14.5 %collective-permute-start.2 = (bf16[8,6272]{1,0:T(8,128)(2,1)S(1)}, bf16[8,6272]{1,0:T(8,128)(2,1)S(1)}, u32[]{:S(2)}, u32[]{:S(2)}) collective-permute-start(bf16[8,6272]{1,0:T(8,128)(2,1)S(1)} %shard_map.73.refs_0_), channel_id=1, source_target_pairs={{0,12},{4,8},{8,4},{12,0},{1,13},{5,9},{9,5},{13,1},{2,14},{6,10},... | collective-permute-start | bytes 301064 | tf_op jit(solution)/shard_map/ppermute | solution.py:314
  6.1 9.4 %collective-permute-start.1 = (bf16[8,6272]{1,0:T(8,128)(2,1)S(1)}, bf16[8,6272]{1,0:T(8,128)(2,1)S(1)}, u32[]{:S(2)}, u32[]{:S(2)}) collective-permute-start(bf16[8,6272]{1,0:T(8,128)(2,1)S(1)} %shard_map.73.refs_0_), channel_id=1, source_target_pairs={{0,8},{4,12},{8,0},{12,4},{1,9},{5,13},{9,1},{13,5},{2,10},{6,14},... | collective-permute-start | bytes 301064 | tf_op jit(solution)/shard_map/ppermute | solution.py:314
  6.1 9.5 %collective-permute-start = (bf16[8,6272]{1,0:T(8,128)(2,1)S(1)}, bf16[8,6272]{1,0:T(8,128)(2,1)S(1)}, u32[]{:S(2)}, u32[]{:S(2)}) collective-permute-start(bf16[8,6272]{1,0:T(8,128)(2,1)S(1)} %shard_map.73.refs_0_), channel_id=1, source_target_pairs={{0,4},{4,0},{8,12},{12,8},{1,5},{5,1},{9,13},{13,9},{2,6},{6,2},{1... | collective-permute-start | bytes 301064 | tf_op jit(solution)/shard_map/ppermute | solution.py:314
  15.6 1.8 %collective-permute-start.3 = (bf16[4,8,6272]{2,1,0:T(8,128)(2,1)S(1)}, bf16[4,8,6272]{2,1,0:T(8,128)(2,1)S(1)}, u32[]{:S(2)}, u32[]{:S(2)}) collective-permute-start(bf16[4,8,6272]{2,1,0:T(8,128)(2,1)S(1)} %shard_map.75.refs_1_), channel_id=1, source_target_pairs={{0,1},{1,0},{2,3},{3,2},{4,5},{5,4},{6,7},{7,6},{8,9},{9,8},{10,11... | collective-permute-start | bytes 1204232 | tf_op jit(solution)/shard_map/ppermute | solution.py:309
  27.7 4.0 %collective-permute-start.4 = (bf16[64,1536]{1,0:T(8,128)(2,1)S(1)}, bf16[64,1536]{1,0:T(8,128)(2,1)S(1)}, u32[]{:S(2)}, u32[]{:S(2)}) collective-permute-start(bf16[64,1536]{1,0:T(8,128)(2,1)S(1)} %get-tuple-element.44), channel_id=1, source_target_pairs={{0,1},{1,0},{2,3},{3,2},{4,5},{5,4},{6,7},{7,6},{8,9},{9,8},{10,11... | collective-permute-start | bytes 589832 | tf_op jit(solution)/shard_map/ppermute | solution.py:309
  31.8 16.2 %copy-start.1 = (f32[3072]{0:T(1024)S(1)}, f32[3072]{0:T(1024)}, u32[]{:S(2)}) copy-start(f32[3072]{0:T(1024)} %param.8) | copy-start | bytes 36868
  31.8 23.9 %copy-start = (bf16[3072,512]{1,0:T(8,128)(2,1)S(1)}, bf16[3072,512]{1,0:T(8,128)(2,1)}, u32[]{:S(2)}) copy-start(bf16[3072,512]{1,0:T(8,128)(2,1)} %refs_3_.1) | copy-start | bytes 9437188
  31.8 7.2 %collective-permute-start.5 = (bf16[64,1536]{1,0:T(8,128)(2,1)S(1)}, bf16[64,1536]{1,0:T(8,128)(2,1)S(1)}, u32[]{:S(2)}, u32[]{:S(2)}) collective-permute-start(bf16[64,1536]{1,0:T(8,128)(2,1)S(1)} %shard_map.79), channel_id=1, source_target_pairs={{0,2},{2,0},{1,3},{3,1},{4,6},{6,4},{5,7},{7,5},{8,10},{10,8},{9,1... | collective-permute-start | bytes 589832 | tf_op jit(solution)/shard_map/ppermute | solution.py:309
  38.0 1.5 %collective-permute-start.6 = (bf16[64,1536]{1,0:T(8,128)(2,1)S(1)}, bf16[64,1536]{1,0:T(8,128)(2,1)S(1)}, u32[]{:S(2)}, u32[]{:S(2)}) collective-permute-start(bf16[64,1536]{1,0:T(8,128)(2,1)S(1)} %get-tuple-element.50), channel_id=1, source_target_pairs={{0,1},{1,0},{2,3},{3,2},{4,5},{5,4},{6,7},{7,6},{8,9},{9,8},{10,11... | collective-permute-start | bytes 589832 | tf_op jit(solution)/shard_map/ppermute | solution.py:309
  39.6 6.1 %collective-permute-start.7 = (bf16[16,1536]{1,0:T(8,128)(2,1)S(1)}, bf16[16,1536]{1,0:T(8,128)(2,1)S(1)}, u32[]{:S(2)}, u32[]{:S(2)}) collective-permute-start(bf16[16,1536]{1,0:T(8,128)(2,1)S(1)} %get-tuple-element.53), channel_id=1, source_target_pairs={{0,8},{4,12},{8,0},{12,4},{1,9},{5,13},{9,1},{13,5},{2,10},{6,14},... | collective-permute-start | bytes 147464 | tf_op jit(solution)/shard_map/ppermute | solution.py:314
  41.8 6.2 %collective-permute-start.8 = (bf16[16,1536]{1,0:T(8,128)(2,1)S(1)}, bf16[16,1536]{1,0:T(8,128)(2,1)S(1)}, u32[]{:S(2)}, u32[]{:S(2)}) collective-permute-start(bf16[16,1536]{1,0:T(8,128)(2,1)S(1)} %get-tuple-element.54), channel_id=1, source_target_pairs={{0,12},{4,8},{8,4},{12,0},{1,13},{5,9},{9,5},{13,1},{2,14},{6,10},... | collective-permute-start | bytes 147464 | tf_op jit(solution)/shard_map/ppermute | solution.py:314
  43.3 4.6 %collective-permute-start.9 = (bf16[16,1536]{1,0:T(8,128)(2,1)S(1)}, bf16[16,1536]{1,0:T(8,128)(2,1)S(1)}, u32[]{:S(2)}, u32[]{:S(2)}) collective-permute-start(bf16[16,1536]{1,0:T(8,128)(2,1)S(1)} %get-tuple-element.55), channel_id=1, source_target_pairs={{0,4},{4,0},{8,12},{12,8},{1,5},{5,1},{9,13},{13,9},{2,6},{6,2},{1... | collective-permute-start | bytes 147464 | tf_op jit(solution)/shard_map/ppermute | solution.py:314
  48.0 6.0 %collective-permute-start.12 = (bf16[16,1536]{1,0:T(8,128)(2,1)S(1)}, bf16[16,1536]{1,0:T(8,128)(2,1)S(1)}, u32[]{:S(2)}, u32[]{:S(2)}) collective-permute-start(bf16[16,1536]{1,0:T(8,128)(2,1)S(1)} %shard_map.83.refs_0_), channel_id=1, source_target_pairs={{0,12},{4,8},{8,4},{12,0},{1,13},{5,9},{9,5},{13,1},{2,14},{6,10},... | collective-permute-start | bytes 147464 | tf_op jit(solution)/shard_map/ppermute | solution.py:314
  50.7 5.0 %collective-permute-start.11 = (bf16[16,1536]{1,0:T(8,128)(2,1)S(1)}, bf16[16,1536]{1,0:T(8,128)(2,1)S(1)}, u32[]{:S(2)}, u32[]{:S(2)}) collective-permute-start(bf16[16,1536]{1,0:T(8,128)(2,1)S(1)} %shard_map.83.refs_0_), channel_id=1, source_target_pairs={{0,8},{4,12},{8,0},{12,4},{1,9},{5,13},{9,1},{13,5},{2,10},{6,14},... | collective-permute-start | bytes 147464 | tf_op jit(solution)/shard_map/ppermute | solution.py:314
  50.7 5.0 %collective-permute-start.10 = (bf16[16,1536]{1,0:T(8,128)(2,1)S(1)}, bf16[16,1536]{1,0:T(8,128)(2,1)S(1)}, u32[]{:S(2)}, u32[]{:S(2)}) collective-permute-start(bf16[16,1536]{1,0:T(8,128)(2,1)S(1)} %shard_map.83.refs_0_), channel_id=1, source_target_pairs={{0,4},{4,0},{8,12},{12,8},{1,5},{5,1},{9,13},{13,9},{2,6},{6,2},{1... | collective-permute-start | bytes 147464 | tf_op jit(solution)/shard_map/ppermute | solution.py:314
  55.7 1.5 %collective-permute-start.13 = (bf16[64,1536]{1,0:T(8,128)(2,1)S(1)}, bf16[64,1536]{1,0:T(8,128)(2,1)S(1)}, u32[]{:S(2)}, u32[]{:S(2)}) collective-permute-start(bf16[64,1536]{1,0:T(8,128)(2,1)S(1)} %shard_map.84.x_ref), channel_id=1, source_target_pairs={{0,1},{1,0},{2,3},{3,2},{4,5},{5,4},{6,7},{7,6},{8,9},{9,8},{10,11... | collective-permute-start | bytes 589832 | tf_op jit(solution)/shard_map/ppermute | solution.py:309
  57.6 4.1 %collective-permute-start.14 = (bf16[32,640]{1,0:T(8,128)(2,1)S(1)}, bf16[32,640]{1,0:T(8,128)(2,1)S(1)}, u32[]{:S(2)}, u32[]{:S(2)}) collective-permute-start(bf16[32,640]{1,0:T(8,128)(2,1)S(1)} %get-tuple-element.57), channel_id=1, source_target_pairs={{0,2},{2,0},{1,3},{3,1},{4,6},{6,4},{5,7},{7,5},{8,10},{10,8},{9,1... | collective-permute-start | bytes 122888 | tf_op jit(solution)/shard_map/ppermute | solution.py:309

commit v6 on v5

--- a/solution.py
+++ b/solution.py
@@ -25,7 +25,14 @@
     copies = [
         pltpu.make_async_copy(ids_ref, ids, sem.at[0]),
         pltpu.make_async_copy(weight_ref, weight, sem.at[1]),
-        pltpu.make_async_copy(tokens_ref, out_ref.at[:, pl.ds(0, width)], sem.at[2]),
+        *(
+            pltpu.make_async_copy(
+                tokens_ref.at[:, pl.ds(i * width // 4, width // 4)],
+                out_ref.at[:, pl.ds(i * width // 4, width // 4)],
+                sem.at[2 + i],
+            )
+            for i in range(4)
+        ),
     ]
     for copy in copies:
         copy.start()
@@ -42,14 +49,15 @@
         gate = jnp.sum(jnp.where(same, gates[k : k + 1, :], 0.0), axis=1, keepdims=True)
         spread += jnp.where(column == named, gate, 0.0)
     out_ref[:, width:] = spread.astype(jnp.bfloat16)
-    copies[2].wait()
+    for copy in copies[2:]:
+        copy.wait()
 
 
 def up_plan(cols):
     step = 1024 if cols % 1024 == 0 else cols
     count = cols // step
     early = max(1, count - 1)
-    return step, [range(0, early)], count - early
+    return step, early, count - early
 
 
 def down_plan(width, pieces):
@@ -66,12 +74,11 @@
     return at_tp * n_dp + at_dp
 
 
-def load_kernel(group, *refs):
-    w_up_ref, (blocks_ref, done_ref, sem) = refs[0], refs[-3:]
-    step = blocks_ref.shape[2]
+def load_kernel(w_up_ref, blocks_ref, done_ref, sem):
+    count, _, step = blocks_ref.shape
     copies = [
-        pltpu.make_async_copy(w_up_ref.at[:, pl.ds(b * step, step)], blocks_ref.at[b], sem.at[b - group[0]])
-        for b in group
+        pltpu.make_async_copy(w_up_ref.at[:, pl.ds(b * step, step)], blocks_ref.at[b], sem.at[b])
+        for b in range(count)
     ]
     for copy in copies:
         copy.start()
@@ -80,9 +87,9 @@
     done_ref[...] = jnp.zeros_like(done_ref)
 
 
-def stack_kernel(*refs):
-    for i, part in enumerate(refs[:-1]):
-        refs[-1][i] = part[...]
+def stack_kernel(order, *refs):
+    for bits, part in zip((0, *order), refs):
+        refs[-1][bits] = part[...]
 
 
 def gather_kernel(pieces, *refs):
@@ -193,30 +200,33 @@
 def last_down_kernel(pieces, hidden_ref, gate_ref, first_ref, w_down_ref, *refs):
     n_dp = pieces[1]
     outs, (slots, sem) = refs[:n_dp], refs[n_dp:]
-    held = first_ref.shape[0]
-    _, parts, plan = down_plan(w_down_ref.shape[1], pieces)
+    piece, parts, plan = down_plan(w_down_ref.shape[1], pieces)
     before = len(plan) - n_dp
-
-    def copy(j, part):
-        at = j * parts + part - held
-        return down_copy(pieces, before + j, part, w_down_ref, slots.at[at], sem.at[at])
-
-    for j in range(n_dp):
-
-        @pl.loop(held if j == 0 else 0, parts)
-        def _(part, j=j):
-            copy(j, part).start()
-
-    @pl.loop(0, held)
+    count, _, cut_width = slots.shape
+    cuts = piece // cut_width
+
+    def copy(j, cut):
+        at = (j - 1) * cuts + cut
+        jt, jd = plan[before + j]
+        start = pl.multiple_of(own_place(pieces, jt, jd) * piece + cut * cut_width, LANES)
+        return pltpu.make_async_copy(w_down_ref.at[:, pl.ds(start, cut_width)], slots.at[at], sem.at[at])
+
+    for j in range(1, n_dp):
+
+        @pl.loop(0, cuts)
+        def _(cut, j=j):
+            copy(j, cut).start()
+
+    @pl.loop(0, parts)
     def _(part):
         work_part(part, hidden_ref, gate_ref, first_ref[part], outs[0])
 
-    for j in range(n_dp):
-
-        @pl.loop(held if j == 0 else 0, parts)
-        def _(part, j=j):
-            copy(j, part).wait()
-            work_part(part, hidden_ref, gate_ref, slots[j * parts + part - held], outs[j])
+    for j in range(1, n_dp):
+
+        @pl.loop(0, cuts)
+        def _(cut, j=j):
+            copy(j, cut).wait()
+            work_part(cut, hidden_ref, gate_ref, slots[(j - 1) * cuts + cut], outs[j])
 
 
 def add_kernel(*refs):
@@ -250,11 +260,11 @@
     out_ref[...] = ((total + own_ref[...]) * gain_ref[:, at]).astype(jnp.bfloat16)
 
 
-def order_kernel(*refs):
+def order_kernel(order, *refs):
     blocks, out_ref = refs[:-1], refs[-1]
     share = blocks[0].shape[0]
-    for e, block in enumerate(blocks):
-        at = pl.multiple_of((lax.axis_index("ep") ^ e) * share, share)
+    for bits, block in zip((0, *order), blocks):
+        at = pl.multiple_of((lax.axis_index("ep") ^ bits) * share, share)
         out_ref[pl.ds(at, share), :] = block[...]
 
 
@@ -304,6 +314,18 @@
         send_ref[...] = total_ref[pl.ds(pl.multiple_of(theirs * share, share), share), :].astype(jnp.bfloat16)
 
 
+def scale_kernel(width, keep_ref, square_ref, *refs):
+    received, out_ref = refs[:-1], refs[-1]
+    cols = out_ref.shape[1]
+    total = keep_ref[...]
+    squares = square_ref[...]
+    for part in received:
+        total = total + part[:, :cols].astype(jnp.float32)
+        squares = squares + part[:, cols:].astype(jnp.float32)
+    mean = jnp.sum(squares, axis=1, keepdims=True) / width
+    out_ref[...] = (total * lax.rsqrt(mean + EPSILON)).astype(out_ref.dtype)
+
+
 def shift(x, axis, by):
     size = lax.axis_size(axis)
     return lax.ppermute(x, axis, [(i, (i + by) % size) for i in range(size)])
@@ -343,7 +365,7 @@
     pieces = (n_tp, n_dp)
     rows = rows_here * n_ep * n_dp
     share = rows_here * n_dp
-    step, groups, n_late = up_plan(cols)
+    step, early, n_late = up_plan(cols)
     piece, n_parts, plan = down_plan(width, pieces)
     part_width = piece // n_parts
     direct = n_ep <= 4
@@ -356,7 +378,7 @@
         scratch_shapes=[
             pltpu.VMEM(expert_ids.shape[::-1], jnp.int32),
             pltpu.VMEM(expert_ids.shape[::-1], jnp.float32),
-            pltpu.SemaphoreType.DMA((3,)),
+            pltpu.SemaphoreType.DMA((6,)),
         ],
         compiler_params=params(2),
     )(*(pltpu.with_memory_space_constraint(x, pltpu.HBM) for x in (tokens, expert_ids.T, route_weight.T)))
@@ -364,44 +386,32 @@
     def following(x, after):
         return lax.optimization_barrier((x, after))[0]
 
-    early = sum(len(group) for group in groups)
-
-    def load(group, after, *blocks):
-        weights = following(w_up, after)
-        return pl.pallas_call(
-            functools.partial(load_kernel, group),
-            out_shape=(
-                pltpu.VMEM((early, width, step), jnp.bfloat16),
-                jax.ShapeDtypeStruct((8, LANES), jnp.float32),
-            ),
-            in_specs=[ANY] + [VMEM] * len(blocks),
-            out_specs=(VMEM, VMEM),
-            scratch_shapes=[pltpu.SemaphoreType.DMA((len(group),))],
-            input_output_aliases={1: 0} if blocks else {},
-            compiler_params=params(SCOPED),
-            cost_estimate=cost(0, 2 * len(group) * width * step),
-        )(weights, *(in_vmem(block) for block in blocks))
-
-    blocks, done = load(groups[0], packed)
+    blocks, done = pl.pallas_call(
+        load_kernel,
+        out_shape=(
+            pltpu.VMEM((early, width, step), jnp.bfloat16),
+            jax.ShapeDtypeStruct((8, LANES), jnp.float32),
+        ),
+        in_specs=[ANY],
+        out_specs=(VMEM, VMEM),
+        scratch_shapes=[pltpu.SemaphoreType.DMA((early,))],
+        compiler_params=params(SCOPED),
+        cost_estimate=cost(0, 2 * early * width * step),
+    )(following(w_up, packed))
     if direct:
-        parts = [packed] + [None] * (n_ep - 1)
-        for bits in exchange_order(n_ep):
-            parts[bits] = flip(packed, "ep", bits)
+        order = range(1, n_ep)
+        parts = [packed] + [flip(packed, "ep", bits) for bits in order]
         parts = [following(part, done) for part in parts]
         stacked = pl.pallas_call(
-            stack_kernel,
+            functools.partial(stack_kernel, order),
             out_shape=jax.ShapeDtypeStruct((n_ep, rows_here, width + LANES), jnp.bfloat16),
             in_specs=[VMEM] * n_ep,
             out_specs=VMEM,
             compiler_params=params(4),
         )(*parts)
-        if len(groups) > 1:
-            blocks, done = load(groups[1], stacked, blocks)
-        parts = [stacked] + [following(shift(stacked, "dp", j), done) for j in range(1, n_dp)]
+        parts = [stacked] + [shift(stacked, "dp", j) for j in range(1, n_dp)]
     else:
-        for group in groups[1:]:
-            blocks, done = load(group, done, blocks)
-        parts = [lax.all_gather(packed, ("ep", "dp"), axis=0, tiled=True)[None]]
+        parts = [following(lax.all_gather(packed, ("ep", "dp"), axis=0, tiled=True), done)[None]]
 
     x, own = pl.pallas_call(
         functools.partial(gather_kernel, pieces),
@@ -443,16 +453,15 @@
     shared = dict(compiler_params=params(14), cost_estimate=cost(2 * rows * cols * piece, 2 * cols * piece))
     for stage in range(1, len(plan) - n_dp):
         jt, jd = plan[stage]
-        loaded = n_parts
         out, slots = pl.pallas_call(
             functools.partial(down_kernel, pieces, stage),
             out_shape=(
                 pltpu.VMEM((rows, piece), jnp.bfloat16 if jd else jnp.float32),
-                pltpu.VMEM((loaded, cols, part_width), jnp.bfloat16),
+                units,
             ),
             in_specs=[VMEM] * 3 + [ANY],
             out_specs=(VMEM,) * 2,
-            scratch_shapes=[pltpu.SemaphoreType.DMA((loaded,))],
+            scratch_shapes=[pltpu.SemaphoreType.DMA((n_parts,))],
             **shared,
         )(in_vmem(hidden), in_vmem(gate), in_vmem(slots), following(w_down, after))
         if jd:
@@ -467,6 +476,8 @@
             )(out, *gathering)
             received.append(shift(after, "tp", jt))
             gathering = []
+    cut_width = part_width // 2 if part_width % (2 * LANES) == 0 else part_width
+    n_cuts = max(1, n_dp - 1) * (piece // cut_width)
     *outs, out = pl.pallas_call(
         functools.partial(last_down_kernel, pieces),
         out_shape=tuple(
@@ -475,8 +486,8 @@
         in_specs=[VMEM] * 3 + [ANY],
         out_specs=(VMEM,) * n_dp,
         scratch_shapes=[
-            pltpu.VMEM((n_dp * n_parts - slots.shape[0], cols, part_width), jnp.bfloat16),
-            pltpu.SemaphoreType.DMA((n_dp * n_parts - slots.shape[0],)),
+            pltpu.VMEM((n_cuts, cols, cut_width), jnp.bfloat16),
+            pltpu.SemaphoreType.DMA((n_cuts,)),
         ],
         **shared,
     )(in_vmem(hidden), in_vmem(gate), in_vmem(slots), following(w_down, after))
@@ -514,11 +525,10 @@
         compiler_params=params(4),
     )(keep, own, gain, *received)
     if direct:
-        blocks = [scaled] + [None] * (n_ep - 1)
-        for bits in exchange_order(n_ep):
-            blocks[bits] = flip(scaled, "ep", bits)
+        order = range(1, n_ep)
+        blocks = [scaled] + [flip(scaled, "ep", bits) for bits in order]
         mine = pl.pallas_call(
-            order_kernel,
+            functools.partial(order_kernel, order),
             out_shape=jax.ShapeDtypeStruct((rows, piece), jnp.bfloat16),
             in_specs=[VMEM] * n_ep,
             out_specs=VMEM,
@@ -548,13 +558,14 @@
         scratch_shapes=[pltpu.VMEM((rows, out_cols + LANES), jnp.float32)],
         compiler_params=params(12),
     )(*others, first, gain, w_qkv)
-    total, squares = projected[0], projected[1]
-    for j in range(1, n_tp):
-        received = shift(projected[1 + j], "tp", j).astype(jnp.float32)
-        total = total + received[:, :out_cols]
-        squares = squares + received[:, out_cols:]
-    scale = lax.rsqrt(jnp.sum(squares[:, :3], axis=1, keepdims=True) / width + EPSILON)
-    return (total * scale).astype(jnp.bfloat16)
+    received = [shift(projected[1 + j], "tp", j) for j in range(1, n_tp)]
+    return pl.pallas_call(
+        functools.partial(scale_kernel, width),
+        out_shape=jax.ShapeDtypeStruct((share, out_cols), jnp.bfloat16),
+        in_specs=[VMEM] * (n_tp + 1),
+        out_specs=VMEM,
+        compiler_params=params(4),
+    )(*projected[:2], *received)
 
 
 def solution(mesh):

time: 62.7 us -> 62.4 us (level)
  other arithmetic: 0.82 us -> 0 us
    pallas_call x3 -> x4, Pallas kernels: 8.83 us -> 9.54 us  [the longest x1 8.78 us: body(): pl.pallas_call(load_kernel, out_shape=(pltpu.VMEM((early, width, step), j...]
    convert_element_type x2 -> x0, other arithmetic: 0.7 us -> none  [the longest x1 0.69 us: body(): return (total * scale).astype(jnp.bfloat16)]
where the time goes in v6:
time: 62.4 us; the launch traced here: 62.2 us
  Pallas kernels  29.9 us (48%)
  starting transfers between devices  17.5 us (28%)
  waiting for transfers between devices  14.7 us (24%)
    ppermute x9, starting transfers between devices, flip(): return lax.ppermute(x, axis, [(i, i ^ bits) for i in range(size)])  14.4 us
    pallas_call x1, Pallas kernels, body(): pl.pallas_call(functools.partial(up_kernel, pieces), out_shape=(pltpu.VME...  10.1 us
    pallas_call x1, Pallas kernels, body(): pl.pallas_call(load_kernel, out_shape=(pltpu.VMEM((early, width, step), j...  8.78 us
    ppermute x9, waiting for transfers between devices, flip(): return lax.ppermute(x, axis, [(i, i ^ bits) for i in range(size)])  7.36 us
    ppermute x6, waiting for transfers between devices, shift(): return lax.ppermute(x, axis, [(i, (i + by) % size) for i in range(size)])  7.32 us
    pallas_call x1, Pallas kernels, body(): pl.pallas_call(functools.partial(last_down_kernel, pieces), out_shape=tup...  4.39 us
    pallas_call x1, Pallas kernels, body(): pl.pallas_call(functools.partial(down_kernel, pieces, stage), out_shape=(...  3.81 us
    ppermute x6, starting transfers between devices, shift(): return lax.ppermute(x, axis, [(i, (i + by) % size) for i in range(size)])  3.01 us
  transfers between devices with their start and end apart: 15, of which 9 were waited for; matrix products, arithmetic and copies ran while one was open for 0% of the time, Pallas kernels for 28%

profile of v6, /device:TPU:0, one launch (start us, length us, event | category | flops | bytes accessed | tf_op | source)
XLA Modules:
  0.0 62.2 jit_solution(8444976402689915113)
XLA Ops:
  0.0 0.9 %shard_map.73.refs_0_ = bf16[8,6272]{1,0:T(8,128)(2,1)S(1)} custom-call(bf16[8,6144]{1,0:T(8,128)(2,1)} %tokens_ref.1, s32[4,8]{1,0:T(4,128)} %bitcast.6, f32[4,8]{1,0:T(4,128)} %bitcast.7), custom_call_target="tpu_custom_call" | custom-call | tf_op jit(solution)/shard_map/pallas_call | solution.py:373
  0.9 5.1 %collective-permute-start.2 = (bf16[8,6272]{1,0:T(8,128)(2,1)S(1)}, bf16[8,6272]{1,0:T(8,128)(2,1)S(1)}, u32[]{:S(2)}, u32[]{:S(2)}) collective-permute-start(bf16[8,6272]{1,0:T(8,128)(2,1)S(1)} %shard_map.73.refs_0_), channel_id=1, source_target_pairs={{0,12},{4,8},{8,4},{12,0},{1,13},{5,9},{9,5},{13,1},{2,14},{6,10},... | collective-permute-start | bytes 301064 | tf_op jit(solution)/shard_map/ppermute | solution.py:336
  6.0 0.6 %collective-permute-start = (bf16[8,6272]{1,0:T(8,128)(2,1)S(1)}, bf16[8,6272]{1,0:T(8,128)(2,1)S(1)}, u32[]{:S(2)}, u32[]{:S(2)}) collective-permute-start(bf16[8,6272]{1,0:T(8,128)(2,1)S(1)} %shard_map.73.refs_0_), channel_id=1, source_target_pairs={{0,4},{4,0},{8,12},{12,8},{1,5},{5,1},{9,13},{13,9},{2,6},{6,2},{1... | collective-permute-start | bytes 301064 | tf_op jit(solution)/shard_map/ppermute | solution.py:336
  6.6 8.8 %shard_map.74 = (bf16[2,6144,1024]{2,1,0:T(8,128)(2,1)S(1)}, f32[8,128]{1,0:T(8,128)}) custom-call(bf16[6144,3072]{1,0:T(8,128)(2,1)} %refs_0_.1), custom_call_target="tpu_custom_call" | custom-call | bytes 25165 | tf_op jit(solution)/shard_map/pallas_call | solution.py:389
  15.6 1.7 %collective-permute-done.3.refs_2_ = bf16[4,8,6272]{2,1,0:T(8,128)(2,1)S(1)} collective-permute-done((bf16[4,8,6272]{2,1,0:T(8,128)(2,1)S(1)}, bf16[4,8,6272]{2,1,0:T(8,128)(2,1)S(1)}, u32[]{:S(2)}, u32[]{:S(2)}) %collective-permute-start.3) | collective-permute-done | bytes 401440 | tf_op jit(solution)/shard_map/ppermute | solution.py:331
  17.5 10.1 %shard_map.77 = (bf16[64,3072]{1,0:T(8,128)(2,1)S(1)}, f32[64,128]{1,0:T(8,128)S(1)}, bf16[64,1536]{1,0:T(8,128)(2,1)S(1)}, bf16[3,3072,512]{2,1,0:T(8,128)(2,1)S(1)}) custom-call(bf16[2,6144,1024]{2,1,0:T(8,128)(2,1)S(1)} %get-tuple-element.32.refs_0_.blocks_ref, bf16[64,6272]{1,0:T(8,128)(2,1)S(1)} %get-tuple-element.38.x_ref, bf16[6144,3072]{1,0:T(8,128)(2,1)} %refs_0_.1, ...), custom_call_target="tpu_custom_call" | custom-call | flops 3019898 | bytes 25165 | tf_op jit(solution)/shard_map/pallas_call | solution.py:429
  27.9 3.8 %shard_map.78 = (f32[64,1536]{1,0:T(8,128)S(1)}, bf16[3,3072,512]{2,1,0:T(8,128)(2,1)S(1)}) custom-call(bf16[64,3072]{1,0:T(8,128)(2,1)S(1)} %get-tuple-element.39.hidden_ref, f32[64,128]{1,0:T(8,128)S(1)} %get-tuple-element.40.gate_ref, bf16[3,3072,512]{2,1,0:T(8,128)(2,1)S(1)} %get-tuple-element.41.slots, bf16[3072,6144]{1,0:T(8,128)(2,1)} %w_down_ref.1), custom_call_target="tpu_custom_call" | custom-call | flops 603979 | bytes 9437 | tf_op jit(solution)/shard_map/pallas_call | solution.py:456
  31.8 1.7 %collective-permute-start.5 = (bf16[64,1536]{1,0:T(8,128)(2,1)S(1)}, bf16[64,1536]{1,0:T(8,128)(2,1)S(1)}, u32[]{:S(2)}, u32[]{:S(2)}) collective-permute-start(bf16[64,1536]{1,0:T(8,128)(2,1)S(1)} %shard_map.79), channel_id=1, source_target_pairs={{0,2},{2,0},{1,3},{3,1},{4,6},{6,4},{5,7},{7,5},{8,10},{10,8},{9,1... | collective-permute-start | bytes 589832 | tf_op jit(solution)/shard_map/ppermute | solution.py:331
  33.5 4.4 %shard_map.80 = (bf16[64,1536]{1,0:T(8,128)(2,1)S(1)}, f32[64,1536]{1,0:T(8,128)S(1)}) custom-call(bf16[64,3072]{1,0:T(8,128)(2,1)S(1)} %get-tuple-element.39.hidden_ref, f32[64,128]{1,0:T(8,128)S(1)} %get-tuple-element.40.gate_ref, bf16[3,3072,512]{2,1,0:T(8,128)(2,1)S(1)} %get-tuple-element.44.first_ref, bf16[3072,6144]{1,0:T(8,128)(2,1)} %w_down_ref.1), custom_call_target="tpu_custom_call" | custom-call | flops 603979 | bytes 9437 | tf_op jit(solution)/shard_map/pallas_call | solution.py:481
  38.0 1.0 %collective-permute-done.5.refs_1_ = bf16[64,1536]{1,0:T(8,128)(2,1)S(1)} collective-permute-done((bf16[64,1536]{1,0:T(8,128)(2,1)S(1)}, bf16[64,1536]{1,0:T(8,128)(2,1)S(1)}, u32[]{:S(2)}, u32[]{:S(2)}) %collective-permute-start.5) | collective-permute-done | bytes 196640 | tf_op jit(solution)/shard_map/ppermute | solution.py:331
  39.4 2.2 %collective-permute-start.7 = (bf16[16,1536]{1,0:T(8,128)(2,1)S(1)}, bf16[16,1536]{1,0:T(8,128)(2,1)S(1)}, u32[]{:S(2)}, u32[]{:S(2)}) collective-permute-start(bf16[16,1536]{1,0:T(8,128)(2,1)S(1)} %get-tuple-element.51), channel_id=1, source_target_pairs={{0,8},{4,12},{8,0},{12,4},{1,9},{5,13},{9,1},{13,5},{2,10},{6,14},... | collective-permute-start | bytes 147464 | tf_op jit(solution)/shard_map/ppermute | solution.py:336
  41.6 1.5 %collective-permute-start.8 = (bf16[16,1536]{1,0:T(8,128)(2,1)S(1)}, bf16[16,1536]{1,0:T(8,128)(2,1)S(1)}, u32[]{:S(2)}, u32[]{:S(2)}) collective-permute-start(bf16[16,1536]{1,0:T(8,128)(2,1)S(1)} %get-tuple-element.52), channel_id=1, source_target_pairs={{0,12},{4,8},{8,4},{12,0},{1,13},{5,9},{9,5},{13,1},{2,14},{6,10},... | collective-permute-start | bytes 147464 | tf_op jit(solution)/shard_map/ppermute | solution.py:336
  43.2 0.5 collective-permute-start.9
  43.6 1.9 %collective-permute-done.7.refs_0_ = bf16[16,1536]{1,0:T(8,128)(2,1)S(1)} collective-permute-done((bf16[16,1536]{1,0:T(8,128)(2,1)S(1)}, bf16[16,1536]{1,0:T(8,128)(2,1)S(1)}, u32[]{:S(2)}, u32[]{:S(2)}) %collective-permute-start.7) | collective-permute-done | bytes 49184 | tf_op jit(solution)/shard_map/ppermute | solution.py:336
  45.5 2.3 %collective-permute-done.8.refs_1_ = bf16[16,1536]{1,0:T(8,128)(2,1)S(1)} collective-permute-done((bf16[16,1536]{1,0:T(8,128)(2,1)S(1)}, bf16[16,1536]{1,0:T(8,128)(2,1)S(1)}, u32[]{:S(2)}, u32[]{:S(2)}) %collective-permute-start.8) | collective-permute-done | bytes 49184 | tf_op jit(solution)/shard_map/ppermute | solution.py:336
  47.8 2.7 %collective-permute-start.12 = (bf16[16,1536]{1,0:T(8,128)(2,1)S(1)}, bf16[16,1536]{1,0:T(8,128)(2,1)S(1)}, u32[]{:S(2)}, u32[]{:S(2)}) collective-permute-start(bf16[16,1536]{1,0:T(8,128)(2,1)S(1)} %shard_map.83.refs_0_), channel_id=1, source_target_pairs={{0,12},{4,8},{8,4},{12,0},{1,13},{5,9},{9,5},{13,1},{2,14},{6,10},... | collective-permute-start | bytes 147464 | tf_op jit(solution)/shard_map/ppermute | solution.py:336
  50.5 1.8 %collective-permute-start.10 = (bf16[16,1536]{1,0:T(8,128)(2,1)S(1)}, bf16[16,1536]{1,0:T(8,128)(2,1)S(1)}, u32[]{:S(2)}, u32[]{:S(2)}) collective-permute-start(bf16[16,1536]{1,0:T(8,128)(2,1)S(1)} %shard_map.83.refs_0_), channel_id=1, source_target_pairs={{0,4},{4,0},{8,12},{12,8},{1,5},{5,1},{9,13},{13,9},{2,6},{6,2},{1... | collective-permute-start | bytes 147464 | tf_op jit(solution)/shard_map/ppermute | solution.py:336
  52.3 1.6 %collective-permute-done.12.refs_3_ = bf16[16,1536]{1,0:T(8,128)(2,1)S(1)} collective-permute-done((bf16[16,1536]{1,0:T(8,128)(2,1)S(1)}, bf16[16,1536]{1,0:T(8,128)(2,1)S(1)}, u32[]{:S(2)}, u32[]{:S(2)}) %collective-permute-start.12) | collective-permute-done | bytes 49184 | tf_op jit(solution)/shard_map/ppermute | solution.py:336
  53.9 1.6 %collective-permute-done.11.refs_2_ = bf16[16,1536]{1,0:T(8,128)(2,1)S(1)} collective-permute-done((bf16[16,1536]{1,0:T(8,128)(2,1)S(1)}, bf16[16,1536]{1,0:T(8,128)(2,1)S(1)}, u32[]{:S(2)}, u32[]{:S(2)}) %collective-permute-start.11) | collective-permute-done | bytes 49184 | tf_op jit(solution)/shard_map/ppermute | solution.py:336
  56.0 1.0 %collective-permute-done.13.refs_0_ = bf16[64,1536]{1,0:T(8,128)(2,1)S(1)} collective-permute-done((bf16[64,1536]{1,0:T(8,128)(2,1)S(1)}, bf16[64,1536]{1,0:T(8,128)(2,1)S(1)}, u32[]{:S(2)}, u32[]{:S(2)}) %collective-permute-start.13) | collective-permute-done | bytes 196640 | tf_op jit(solution)/shard_map/ppermute | solution.py:331
  57.0 0.4 shard_map.86
  57.5 0.8 %collective-permute-start.14 = (bf16[32,640]{1,0:T(8,128)(2,1)S(1)}, bf16[32,640]{1,0:T(8,128)(2,1)S(1)}, u32[]{:S(2)}, u32[]{:S(2)}) collective-permute-start(bf16[32,640]{1,0:T(8,128)(2,1)S(1)} %get-tuple-element.56), channel_id=1, source_target_pairs={{0,2},{2,0},{1,3},{3,1},{4,6},{6,4},{5,7},{7,5},{8,10},{10,8},{9,1... | collective-permute-start | bytes 122888 | tf_op jit(solution)/shard_map/ppermute | solution.py:331
  58.3 3.3 %collective-permute-done.14.refs_0_ = bf16[32,640]{1,0:T(8,128)(2,1)S(1)} collective-permute-done((bf16[32,640]{1,0:T(8,128)(2,1)S(1)}, bf16[32,640]{1,0:T(8,128)(2,1)S(1)}, u32[]{:S(2)}, u32[]{:S(2)}) %collective-permute-start.14) | collective-permute-done | bytes 40992 | tf_op jit(solution)/shard_map/ppermute | solution.py:331
  61.5 0.7 %shard_map.87 = bf16[32,512]{1,0:T(8,128)(2,1)} custom-call(f32[32,512]{1,0:T(8,128)S(1)} %get-tuple-element.54.keep_ref, f32[32,128]{1,0:T(8,128)S(1)} %get-tuple-element.55.square_ref, bf16[32,640]{1,0:T(8,128)(2,1)S(1)} %collective-permute-done.14.refs_0_), custom_call_target="tpu_custom_call" | custom-call | tf_op jit(solution)/shard_map/pallas_call | solution.py:562
  (25 shorter events, 1.6 us)
Async XLA Ops:
  0.9 14.5 %collective-permute-start.2 = (bf16[8,6272]{1,0:T(8,128)(2,1)S(1)}, bf16[8,6272]{1,0:T(8,128)(2,1)S(1)}, u32[]{:S(2)}, u32[]{:S(2)}) collective-permute-start(bf16[8,6272]{1,0:T(8,128)(2,1)S(1)} %shard_map.73.refs_0_), channel_id=1, source_target_pairs={{0,12},{4,8},{8,4},{12,0},{1,13},{5,9},{9,5},{13,1},{2,14},{6,10},... | collective-permute-start | bytes 301064 | tf_op jit(solution)/shard_map/ppermute | solution.py:336
  6.0 9.4 %collective-permute-start.1 = (bf16[8,6272]{1,0:T(8,128)(2,1)S(1)}, bf16[8,6272]{1,0:T(8,128)(2,1)S(1)}, u32[]{:S(2)}, u32[]{:S(2)}) collective-permute-start(bf16[8,6272]{1,0:T(8,128)(2,1)S(1)} %shard_map.73.refs_0_), channel_id=1, source_target_pairs={{0,8},{4,12},{8,0},{12,4},{1,9},{5,13},{9,1},{13,5},{2,10},{6,14},... | collective-permute-start | bytes 301064 | tf_op jit(solution)/shard_map/ppermute | solution.py:336
  6.0 9.5 %collective-permute-start = (bf16[8,6272]{1,0:T(8,128)(2,1)S(1)}, bf16[8,6272]{1,0:T(8,128)(2,1)S(1)}, u32[]{:S(2)}, u32[]{:S(2)}) collective-permute-start(bf16[8,6272]{1,0:T(8,128)(2,1)S(1)} %shard_map.73.refs_0_), channel_id=1, source_target_pairs={{0,4},{4,0},{8,12},{12,8},{1,5},{5,1},{9,13},{13,9},{2,6},{6,2},{1... | collective-permute-start | bytes 301064 | tf_op jit(solution)/shard_map/ppermute | solution.py:336
  15.5 1.8 %collective-permute-start.3 = (bf16[4,8,6272]{2,1,0:T(8,128)(2,1)S(1)}, bf16[4,8,6272]{2,1,0:T(8,128)(2,1)S(1)}, u32[]{:S(2)}, u32[]{:S(2)}) collective-permute-start(bf16[4,8,6272]{2,1,0:T(8,128)(2,1)S(1)} %shard_map.75.refs_1_), channel_id=1, source_target_pairs={{0,1},{1,0},{2,3},{3,2},{4,5},{5,4},{6,7},{7,6},{8,9},{9,8},{10,11... | collective-permute-start | bytes 1204232 | tf_op jit(solution)/shard_map/ppermute | solution.py:331
  27.7 4.0 %collective-permute-start.4 = (bf16[64,1536]{1,0:T(8,128)(2,1)S(1)}, bf16[64,1536]{1,0:T(8,128)(2,1)S(1)}, u32[]{:S(2)}, u32[]{:S(2)}) collective-permute-start(bf16[64,1536]{1,0:T(8,128)(2,1)S(1)} %get-tuple-element.42), channel_id=1, source_target_pairs={{0,1},{1,0},{2,3},{3,2},{4,5},{5,4},{6,7},{7,6},{8,9},{9,8},{10,11... | collective-permute-start | bytes 589832 | tf_op jit(solution)/shard_map/ppermute | solution.py:331
  31.7 16.1 %copy-start.1 = (f32[3072]{0:T(1024)S(1)}, f32[3072]{0:T(1024)}, u32[]{:S(2)}) copy-start(f32[3072]{0:T(1024)} %param.8) | copy-start | bytes 36868
  31.7 23.9 %copy-start = (bf16[3072,512]{1,0:T(8,128)(2,1)S(1)}, bf16[3072,512]{1,0:T(8,128)(2,1)}, u32[]{:S(2)}) copy-start(bf16[3072,512]{1,0:T(8,128)(2,1)} %refs_3_.1) | copy-start | bytes 9437188
  31.8 7.2 %collective-permute-start.5 = (bf16[64,1536]{1,0:T(8,128)(2,1)S(1)}, bf16[64,1536]{1,0:T(8,128)(2,1)S(1)}, u32[]{:S(2)}, u32[]{:S(2)}) collective-permute-start(bf16[64,1536]{1,0:T(8,128)(2,1)S(1)} %shard_map.79), channel_id=1, source_target_pairs={{0,2},{2,0},{1,3},{3,1},{4,6},{6,4},{5,7},{7,5},{8,10},{10,8},{9,1... | collective-permute-start | bytes 589832 | tf_op jit(solution)/shard_map/ppermute | solution.py:331
  37.9 1.5 %collective-permute-start.6 = (bf16[64,1536]{1,0:T(8,128)(2,1)S(1)}, bf16[64,1536]{1,0:T(8,128)(2,1)S(1)}, u32[]{:S(2)}, u32[]{:S(2)}) collective-permute-start(bf16[64,1536]{1,0:T(8,128)(2,1)S(1)} %get-tuple-element.48), channel_id=1, source_target_pairs={{0,1},{1,0},{2,3},{3,2},{4,5},{5,4},{6,7},{7,6},{8,9},{9,8},{10,11... | collective-permute-start | bytes 589832 | tf_op jit(solution)/shard_map/ppermute | solution.py:331
  39.4 6.1 %collective-permute-start.7 = (bf16[16,1536]{1,0:T(8,128)(2,1)S(1)}, bf16[16,1536]{1,0:T(8,128)(2,1)S(1)}, u32[]{:S(2)}, u32[]{:S(2)}) collective-permute-start(bf16[16,1536]{1,0:T(8,128)(2,1)S(1)} %get-tuple-element.51), channel_id=1, source_target_pairs={{0,8},{4,12},{8,0},{12,4},{1,9},{5,13},{9,1},{13,5},{2,10},{6,14},... | collective-permute-start | bytes 147464 | tf_op jit(solution)/shard_map/ppermute | solution.py:336
  41.6 6.2 %collective-permute-start.8 = (bf16[16,1536]{1,0:T(8,128)(2,1)S(1)}, bf16[16,1536]{1,0:T(8,128)(2,1)S(1)}, u32[]{:S(2)}, u32[]{:S(2)}) collective-permute-start(bf16[16,1536]{1,0:T(8,128)(2,1)S(1)} %get-tuple-element.52), channel_id=1, source_target_pairs={{0,12},{4,8},{8,4},{12,0},{1,13},{5,9},{9,5},{13,1},{2,14},{6,10},... | collective-permute-start | bytes 147464 | tf_op jit(solution)/shard_map/ppermute | solution.py:336
  43.2 4.6 %collective-permute-start.9 = (bf16[16,1536]{1,0:T(8,128)(2,1)S(1)}, bf16[16,1536]{1,0:T(8,128)(2,1)S(1)}, u32[]{:S(2)}, u32[]{:S(2)}) collective-permute-start(bf16[16,1536]{1,0:T(8,128)(2,1)S(1)} %get-tuple-element.53), channel_id=1, source_target_pairs={{0,4},{4,0},{8,12},{12,8},{1,5},{5,1},{9,13},{13,9},{2,6},{6,2},{1... | collective-permute-start | bytes 147464 | tf_op jit(solution)/shard_map/ppermute | solution.py:336
  47.8 6.0 %collective-permute-start.12 = (bf16[16,1536]{1,0:T(8,128)(2,1)S(1)}, bf16[16,1536]{1,0:T(8,128)(2,1)S(1)}, u32[]{:S(2)}, u32[]{:S(2)}) collective-permute-start(bf16[16,1536]{1,0:T(8,128)(2,1)S(1)} %shard_map.83.refs_0_), channel_id=1, source_target_pairs={{0,12},{4,8},{8,4},{12,0},{1,13},{5,9},{9,5},{13,1},{2,14},{6,10},... | collective-permute-start | bytes 147464 | tf_op jit(solution)/shard_map/ppermute | solution.py:336
  50.5 5.0 %collective-permute-start.11 = (bf16[16,1536]{1,0:T(8,128)(2,1)S(1)}, bf16[16,1536]{1,0:T(8,128)(2,1)S(1)}, u32[]{:S(2)}, u32[]{:S(2)}) collective-permute-start(bf16[16,1536]{1,0:T(8,128)(2,1)S(1)} %shard_map.83.refs_0_), channel_id=1, source_target_pairs={{0,8},{4,12},{8,0},{12,4},{1,9},{5,13},{9,1},{13,5},{2,10},{6,14},... | collective-permute-start | bytes 147464 | tf_op jit(solution)/shard_map/ppermute | solution.py:336
  50.5 5.0 %collective-permute-start.10 = (bf16[16,1536]{1,0:T(8,128)(2,1)S(1)}, bf16[16,1536]{1,0:T(8,128)(2,1)S(1)}, u32[]{:S(2)}, u32[]{:S(2)}) collective-permute-start(bf16[16,1536]{1,0:T(8,128)(2,1)S(1)} %shard_map.83.refs_0_), channel_id=1, source_target_pairs={{0,4},{4,0},{8,12},{12,8},{1,5},{5,1},{9,13},{13,9},{2,6},{6,2},{1... | collective-permute-start | bytes 147464 | tf_op jit(solution)/shard_map/ppermute | solution.py:336
  55.5 1.5 %collective-permute-start.13 = (bf16[64,1536]{1,0:T(8,128)(2,1)S(1)}, bf16[64,1536]{1,0:T(8,128)(2,1)S(1)}, u32[]{:S(2)}, u32[]{:S(2)}) collective-permute-start(bf16[64,1536]{1,0:T(8,128)(2,1)S(1)} %shard_map.84.x_ref), channel_id=1, source_target_pairs={{0,1},{1,0},{2,3},{3,2},{4,5},{5,4},{6,7},{7,6},{8,9},{9,8},{10,11... | collective-permute-start | bytes 589832 | tf_op jit(solution)/shard_map/ppermute | solution.py:331
  57.5 4.1 %collective-permute-start.14 = (bf16[32,640]{1,0:T(8,128)(2,1)S(1)}, bf16[32,640]{1,0:T(8,128)(2,1)S(1)}, u32[]{:S(2)}, u32[]{:S(2)}) collective-permute-start(bf16[32,640]{1,0:T(8,128)(2,1)S(1)} %get-tuple-element.56), channel_id=1, source_target_pairs={{0,2},{2,0},{1,3},{3,1},{4,6},{6,4},{5,7},{7,5},{8,10},{10,8},{9,1... | collective-permute-start | bytes 122888 | tf_op jit(solution)/shard_map/ppermute | solution.py:331
